TPU v7x, 32 devices: a whole 2x2x4 slice. The times are simulated.
32 devices in a mesh: parts: 2 (over y), blk: 16 (over z, x, core).
Axes of the slice: x: 2, y: 2, z: 4, core: 2. Of those that a mesh axis runs over, the one named last changes fastest.
Arguments:
- codes: bfloat16 [8192, 1024], P(('parts', 'blk')), parts along dimension 0, may hold values from -8 to 8
- exponents: int32 [8192, 32], P(('parts', 'blk')), parts along dimension 0, may hold values from -2 to 2
- clusters: int32 [8192], P(('parts', 'blk')), parts along dimension 0, may hold values from 0 to 63, as said below
Outputs:
- best: float32 [8192], P(('parts', 'blk')), parts along dimension 0
There are 2 independent parts, one for each index of `parts`. A program takes and returns all parts, laid end to end along the dimension named above; each array names one. Nothing has to cross between parts.
Inputs may be any that keep to these rules, and one draw needn't show every extreme that they name: The owner of a cluster is cluster // 4. Among the rows of one device, at most 48 have clusters of one owner, and every device has exactly 48 rows of some owner.
All inputs are finite; a program needn't handle non-finite values.
Results may differ from a plain program's by a relative error of at most 0.0003.
Values may be sent and summed in bfloat16 or wider, within the bound.
No kernel may reach another device: no remote copies, remote signals or barrier semaphores. Data moves between devices by JAX's collectives and lax.ppermute only.
A program may use at most 64 MiB of HBM per device.

v0:
```python
import jax
import jax.numpy as jnp
from jax import lax
from jax.sharding import PartitionSpec as P

GROUP = 32
CL_DEV = 4


def dequantize(codes, exponents):
    rows = codes.shape[0]
    grouped = (
        codes.astype(jnp.float32).reshape(rows, -1, GROUP)
        * jnp.exp2(exponents.astype(jnp.float32))[:, :, None]
    )
    return grouped.reshape(rows, -1).astype(jnp.bfloat16)


def inverse_norm(values):
    wide = values.astype(jnp.float32)
    return lax.rsqrt(jnp.sum(wide * wide, axis=1) + 1e-06)


def similarity(left, left_inverse, right, right_inverse):
    dots = lax.dot_general(
        left, right, (((1,), (1,)), ((), ())), preferred_element_type=jnp.float32
    )
    return dots * left_inverse[:, None] * right_inverse[None, :]


def shards(codes, exponents, clusters):
    values = dequantize(codes, exponents)
    rows = codes.shape[0]
    count = lax.axis_size("blk")
    capacity = max(2, (3 * rows + count - 1) // count)
    owner = clusters // CL_DEV
    member = (owner[:, None] == lax.iota(jnp.int32, count)[None, :]).astype(jnp.int32)
    rank = jnp.sum((jnp.cumsum(member, axis=0) - member) * member, axis=1)
    slot = owner * capacity + rank
    slots_total = count * capacity
    positions = jnp.zeros((slots_total,), jnp.int32).at[slot].set(lax.iota(jnp.int32, rows))
    filled = jnp.zeros((slots_total,), jnp.bool_).at[slot].set(True)
    send_values = values[positions]
    send_clusters = jnp.where(filled, clusters[positions], -1)
    owner_values, owner_clusters = (
        lax.all_to_all(send_values, "blk", split_axis=0, concat_axis=0, tiled=True),
        lax.all_to_all(send_clusters, "blk", split_axis=0, concat_axis=0, tiled=True),
    )
    owner_inverse = inverse_norm(owner_values)
    scores = similarity(owner_values, owner_inverse, owner_values, owner_inverse)
    index = lax.iota(jnp.int32, slots_total)
    same = (
        (owner_clusters[:, None] == owner_clusters[None, :])
        & (owner_clusters[:, None] >= 0)
        & (index[:, None] != index[None, :])
    )
    result = jnp.max(jnp.where(same, scores, -1.0), axis=1)
    back = lax.all_to_all(result, "blk", split_axis=0, concat_axis=0, tiled=True)
    best = back[slot]
    return best


def solution(mesh):
    placed = (P(("parts", "blk"), None), P(("parts", "blk"), None), P(("parts", "blk")))
    return jax.shard_map(
        shards, mesh=mesh, in_specs=placed, out_specs=P(("parts", "blk")), check_vma=False
    )
```

profile of v0, /device:TPU:0, one launch (start us, length us, event | category | flops | bytes accessed | tf_op | source)
XLA Modules:
  0.0 83.4 jit_solution(15587409037123014486)
XLA Ops:
  0.0 0.8 and_select_fusion
  0.8 0.7 fusion.11
  1.5 0.6 reduce-window.6
  2.0 0.2 slice_reduce_fusion
  2.3 0.1 fusion.3
  2.4 0.7 compare_select_fusion.1
  3.1 1.4 %scatter_custom_fusion.1 = s32[768]{0:T(1024)S(1)} fusion(s32[256]{0:T(256)S(1)} %compare_select_fusion.1, s32[256]{0:T(256)S(1)} %iota.18, s32[]{:T(128)} %constant.17.clone.1), kind=kCustom, calls=%fused_computation.27 | custom fusion | bytes 3076 | tf_op jit(solution)/shard_map/scatter | solution.py:41
  4.5 5.0 %gather_fusion = s32[768]{0:T(1024)S(1)} fusion(s32[256]{0:T(256)S(1)} %copy-done, s32[1024]{0:T(1024)S(1)} %pad_clamp_fusion.1), kind=kCustom, calls=%fused_computation | custom fusion | bytes 9216 | tf_op jit(solution)/shard_map/gather | solution.py:44
  9.5 1.5 %scatter_custom_fusion = pred[768]{0:T(1024)(128)(4,1)S(1)} fusion(s32[256]{0:T(256)S(1)} %compare_select_fusion.1, pred[256]{0:T(512)(128)(4,1)S(1)} %broadcast.55, pred[]{:T(512)} %constant.15.clone.1), kind=kCustom, calls=%fused_computation.30 | custom fusion | bytes 769 | tf_op jit(solution)/shard_map/scatter | solution.py:42
  11.0 0.7 all_to_all.22
  11.7 7.4 %all-to-all-start = ((s32[16,48,1]{1,2,0:T(1,128)}), s32[16,48,1]{1,2,0:T(1,128)S(1)}, u32[]{:S(2)}, u32[]{:S(2)}) async-start(s32[16,48,1]{1,2,0:T(1,128)} %bitcast.2), calls=%async_computation | async-start | bytes 16384 | tf_op jit(solution)/shard_map/all_to_all | solution.py:47
  19.1 0.1 mul.43
  19.2 0.3 copy.9
  19.5 0.6 copy-done.1
  20.1 0.1 multiply_convert_fusion
  20.3 3.6 %gather_fusion.1 = bf16[768,1024]{1,0:T(8,128)(2,1)} fusion(bf16[256,1024]{1,0:T(8,128)(2,1)S(1)} %multiply_convert_fusion, s32[1024]{0:T(1024)S(1)} %pad_clamp_fusion.1), kind=kCustom, calls=%fused_computation.1 | custom fusion | bytes 3148800 | tf_op jit(solution)/shard_map/gather | solution.py:43
  23.9 1.6 %all-to-all-done = s32[16,48,1]{1,2,0:T(1,128)S(1)} async-done(((s32[16,48,1]{1,2,0:T(1,128)}), s32[16,48,1]{1,2,0:T(1,128)S(1)}, u32[]{:S(2)}, u32[]{:S(2)}) %all-to-all-start) | async-done | bytes 3104 | tf_op jit(solution)/shard_map/all_to_all | solution.py:47
  25.5 4.4 %all-to-all-start.1 = ((bf16[16,48,1024]{2,1,0:T(8,128)(2,1)}), bf16[16,48,1024]{2,1,0:T(8,128)(2,1)S(1)}, u32[]{:S(2)}, u32[]{:S(2)}) async-start(bf16[16,48,1024]{2,1,0:T(8,128)(2,1)} %bitcast.4), calls=%async_computation.1 | async-start | bytes 3145728 | tf_op jit(solution)/shard_map/all_to_all | solution.py:46
  29.9 0.5 broadcast.83
  30.4 0.7 reduce.9
  31.1 0.1 eq.45
  31.2 30.7 %all-to-all-done.1 = bf16[16,48,1024]{2,1,0:T(8,128)(2,1)S(1)} async-done(((bf16[16,48,1024]{2,1,0:T(8,128)(2,1)}), bf16[16,48,1024]{2,1,0:T(8,128)(2,1)S(1)}, u32[]{:S(2)}, u32[]{:S(2)}) %all-to-all-start.1) | async-done | bytes 1572896 | tf_op jit(solution)/shard_map/all_to_all | solution.py:46
  61.9 0.4 multiply_reduce_fusion
  62.3 0.1 rsqrt.15
  62.3 1.7 %select_reduce_fusion = f32[768]{0:T(1024)S(1)} fusion(bf16[768,1024]{1,0:T(8,128)(2,1)S(1)} %bitcast.30, f32[768]{0:T(1024)S(1)} %rsqrt.15, s32[768]{0:T(1024)S(1)} %eq.45, pred[768]{0:T(1024)(128)(4,1)S(1)} %broadcast_compare_fusion), kind=kOutput, calls=%fused_computation.6 | convolution fusion | flops 1212677376 | bytes 1582848 | tf_op jit(solution)/shard_map/dot_general | solution.py:25
  64.0 0.7 all_to_all.27
  64.7 9.1 %all-to-all-start.2 = ((f32[16,48,1]{1,2,0:T(1,128)}), f32[16,48,1]{1,2,0:T(1,128)S(1)}, u32[]{:S(2)}, u32[]{:S(2)}) async-start(f32[16,48,1]{1,2,0:T(1,128)} %bitcast.6), calls=%async_computation.2 | async-start | bytes 16384 | tf_op jit(solution)/shard_map/all_to_all | solution.py:58
  73.8 6.4 %all-to-all-done.2 = f32[16,48,1]{1,2,0:T(1,128)S(1)} async-done(((f32[16,48,1]{1,2,0:T(1,128)}), f32[16,48,1]{1,2,0:T(1,128)S(1)}, u32[]{:S(2)}, u32[]{:S(2)}) %all-to-all-start.2) | async-done | bytes 3104 | tf_op jit(solution)/shard_map/all_to_all | solution.py:58
  80.2 0.5 broadcast.84
  80.8 0.7 reduce.10
  81.4 0.1 all_to_all.29
  81.5 1.9 %gather_fusion.2 = f32[256]{0:T(256)} fusion(f32[768]{0:T(1024)S(1)} %all_to_all.29, s32[1024]{0:T(1024)S(1)} %pad_clamp_fusion), kind=kCustom, calls=%fused_computation.2 | custom fusion | bytes 3072 | tf_op jit(solution)/shard_map/gather | solution.py:59
  (17 shorter events, 0.1 us)
Async XLA Ops:
  0.0 4.5 %copy-start = (s32[256]{0:T(256)S(1)}, s32[256]{0:T(256)}, u32[]{:S(2)}) copy-start(s32[256]{0:T(256)} %param.5) | copy-start | bytes 3076
  4.5 14.6 %copy-start.2 = (s32[256,32]{0,1:T(8,128)S(1)}, s32[256,32]{0,1:T(8,128)}, u32[]{:S(2)}) copy-start(s32[256,32]{0,1:T(8,128)} %param.4) | copy-start | bytes 98308
  11.7 13.8 %all-to-all-start = ((s32[16,48,1]{1,2,0:T(1,128)}), s32[16,48,1]{1,2,0:T(1,128)S(1)}, u32[]{:S(2)}, u32[]{:S(2)}) async-start(s32[16,48,1]{1,2,0:T(1,128)} %bitcast.2), calls=%async_computation | async-start | bytes 16384 | tf_op jit(solution)/shard_map/all_to_all | solution.py:47
  19.1 1.0 %copy-start.1 = (bf16[256,1024]{1,0:T(8,128)(2,1)S(1)}, bf16[256,1024]{1,0:T(8,128)(2,1)}, u32[]{:S(2)}) copy-start(bf16[256,1024]{1,0:T(8,128)(2,1)} %param.3) | copy-start | bytes 1572868
  25.5 36.4 %all-to-all-start.1 = ((bf16[16,48,1024]{2,1,0:T(8,128)(2,1)}), bf16[16,48,1024]{2,1,0:T(8,128)(2,1)S(1)}, u32[]{:S(2)}, u32[]{:S(2)}) async-start(bf16[16,48,1024]{2,1,0:T(8,128)(2,1)} %bitcast.4), calls=%async_computation.1 | async-start | bytes 3145728 | tf_op jit(solution)/shard_map/all_to_all | solution.py:46
  64.7 15.5 %all-to-all-start.2 = ((f32[16,48,1]{1,2,0:T(1,128)}), f32[16,48,1]{1,2,0:T(1,128)S(1)}, u32[]{:S(2)}, u32[]{:S(2)}) async-start(f32[16,48,1]{1,2,0:T(1,128)} %bitcast.6), calls=%async_computation.2 | async-start | bytes 16384 | tf_op jit(solution)/shard_map/all_to_all | solution.py:58
where the time goes:
time: 83.8 us; the launch traced here: 83.4 us
  waiting for transfers between devices  38.7 us (46%)
  starting transfers between devices  20.9 us (25%)
  local copies, waits for them, and re-layouts  17.2 us (21%)
  other arithmetic  4.77 us (6%)
  matrix products  1.71 us (2%)
    all_to_all x1, waiting for transfers between devices, shards(): lax.all_to_all(send_values, 'blk', split_axis=0, concat_axis=0, tiled=True)  30.7 us
    all_to_all x1, starting transfers between devices, shards(): lax.all_to_all(result, 'blk', split_axis=0, concat_axis=0, tiled=True)  9.11 us
    all_to_all x1, starting transfers between devices, shards(): lax.all_to_all(send_clusters, 'blk', split_axis=0, concat_axis=0, tiled=T...  7.36 us
    all_to_all x1, waiting for transfers between devices, shards(): lax.all_to_all(result, 'blk', split_axis=0, concat_axis=0, tiled=True)  6.39 us
    gather x1, local copies, waits for them, and re-layouts, shards(): send_clusters = jnp.where(filled, clusters[positions], -1)  4.98 us
    all_to_all x1, starting transfers between devices, shards(): lax.all_to_all(send_values, 'blk', split_axis=0, concat_axis=0, tiled=True)  4.41 us
    gather x1, local copies, waits for them, and re-layouts, shards(): send_values = values[positions]  3.58 us
    gather x1, local copies, waits for them, and re-layouts, shards(): best = back[slot]  1.93 us
  transfers between devices with their start and end apart: 3, of which 3 were waited for; matrix products, arithmetic and copies ran while one was open for 6% of the time, Pallas kernels for 0%

commit v1 on v0

v1 whole, which is shorter than its diff:
```python
import functools
import jax
import jax.numpy as jnp
from jax import lax
from jax.experimental import pallas as pl
from jax.experimental.pallas import tpu as pltpu
from jax.sharding import PartitionSpec as P

GROUP = 32
META_ROWS = 40
VMEM_LIMIT = 32 * 1024 * 1024


def expand(lane_row, rows):
    eye = lax.broadcasted_iota(jnp.int32, (rows, rows), 0) == lax.broadcasted_iota(jnp.int32, (rows, rows), 1)
    return jnp.sum(jnp.where(eye, lane_row, 0.0), axis=1, keepdims=True)


def flatten(column, rows):
    eye = lax.broadcasted_iota(jnp.int32, (rows, rows), 0) == lax.broadcasted_iota(jnp.int32, (rows, rows), 1)
    return jnp.sum(jnp.where(eye, column, 0.0), axis=0, keepdims=True)


def dequantize(codes, meta, groups):
    width = codes.shape[1]
    spread = (
        lax.broadcasted_iota(jnp.int32, (groups, width), 1) // GROUP
        == lax.broadcasted_iota(jnp.int32, (groups, width), 0)
    ).astype(jnp.bfloat16)
    scale = lax.dot_general(
        meta[:groups].astype(jnp.bfloat16), spread, (((0,), (0,)), ((), ())),
        preferred_element_type=jnp.float32,
    )
    values = (codes.astype(jnp.float32) * scale).astype(jnp.bfloat16)
    wide = values.astype(jnp.float32)
    inverse = lax.rsqrt(jnp.sum(wide * wide, axis=1, keepdims=True) + 1e-06)
    return values, inverse, meta[groups:groups + 1]


def plane_kernel(planes, groups, *refs):
    code_refs, meta_refs = refs[:planes], refs[planes:2 * planes]
    values_ref, side_ref, best_ref = refs[2 * planes:]
    rows = code_refs[0].shape[0]
    own = own_inverse = own_code = None
    best = jnp.full((1, rows), -1.0, jnp.float32)
    for r in range(planes):
        values, inverse, code = dequantize(code_refs[r][...], meta_refs[r][...], groups)
        values_ref[r * rows:(r + 1) * rows] = values
        inverse_row = flatten(inverse, rows)
        side_ref[0:1, r * rows:(r + 1) * rows] = code
        side_ref[1:2, r * rows:(r + 1) * rows] = inverse_row
        if r == 0:
            own, own_inverse, own_code = values, inverse_row, code
        dots = lax.dot_general(
            values, own, (((1,), (1,)), ((), ())), preferred_element_type=jnp.float32
        )
        same = expand(code, rows) == own_code
        if r == 0:
            same &= (
                lax.broadcasted_iota(jnp.int32, (rows, rows), 0)
                != lax.broadcasted_iota(jnp.int32, (rows, rows), 1)
            )
        scores = jnp.where(same, dots * inverse * own_inverse, -1.0)
        best = jnp.maximum(best, jnp.max(scores, axis=0, keepdims=True))
    best_ref[...] = jnp.full(best_ref.shape, -1.0, jnp.float32)
    best_ref[0:1, 0:rows] = best


def block_kernel(planes, groups, codes_ref, meta_ref, values_ref, side_ref, before_ref, best_ref, back_ref):
    rows = codes_ref.shape[0]
    values, inverse, code = dequantize(codes_ref[...], meta_ref[...], groups)
    code = expand(code, rows)
    back = jnp.full((rows, 1), -1.0, jnp.float32)
    for r in range(planes):
        at = slice(r * rows, (r + 1) * rows)
        dots = lax.dot_general(
            values, values_ref[at], (((1,), (1,)), ((), ())), preferred_element_type=jnp.float32
        )
        same = code == side_ref[0:1, at]
        scores = jnp.where(same, dots * inverse * side_ref[1:2, at], -1.0)
        back = jnp.maximum(back, jnp.max(scores, axis=1, keepdims=True))
        best_ref[0:1, at] = jnp.maximum(before_ref[0:1, at], jnp.max(scores, axis=0, keepdims=True))
    back_ref[...] = flatten(back, rows)


def call(kernel, shapes, flops, *operands):
    spec = pl.BlockSpec(memory_space=pltpu.VMEM)
    return pl.pallas_call(
        kernel,
        out_shape=[jax.ShapeDtypeStruct(shape, dtype) for shape, dtype in shapes],
        in_specs=[spec] * len(operands),
        out_specs=[spec] * len(shapes),
        compiler_params=pltpu.CompilerParams(vmem_limit_bytes=VMEM_LIMIT),
        cost_estimate=pl.CostEstimate(flops=flops, bytes_accessed=4 * 1024 * 1024, transcendentals=0),
    )(*operands)


def split_axis(count):
    planes = 1
    while planes * planes * 4 <= count:
        planes *= 2
    if count % planes or (count // planes) & (count // planes - 1):
        return 1, count
    return planes, count // planes


def far_rounds(height):
    rounds = []
    for step in range(2, height, 2):
        top = 1 << (step.bit_length() - 1)
        rounds.append([(a, a ^ (step + 1) if a & top else a ^ step) for a in range(height)])
    if height > 1:
        rounds.append([(a, a ^ 1) for a in range(height) if (a & 1) != (a >> 1 & 1)])
    return rounds


def shards(codes, exponents, clusters):
    count = lax.axis_size("blk")
    rows, width = codes.shape
    groups = exponents.shape[1]
    plane, height = split_axis(count)
    near = [
        [(z * plane + p, z * plane + (p ^ r)) for z in range(height) for p in range(plane)]
        for r in range(plane)
    ]
    far = [
        [(a * plane + p, b * plane + p) for a, b in pairs for p in range(plane)]
        for pairs in far_rounds(height)
    ]
    meta = jnp.concatenate(
        [
            jnp.exp2(exponents.astype(jnp.float32)).T,
            (clusters + 1).astype(jnp.float32)[None],
            jnp.zeros((META_ROWS - groups - 1, rows), jnp.float32),
        ]
    )
    far_codes = [lax.ppermute(codes, "blk", pairs) for pairs in far]
    far_meta = [lax.ppermute(meta, "blk", pairs) for pairs in far]
    near_codes = [codes] + [lax.ppermute(codes, "blk", pairs) for pairs in near[1:]]
    near_meta = [meta] + [lax.ppermute(meta, "blk", pairs) for pairs in near[1:]]

    block_flops = 2 * rows * rows * width * plane
    values, side, best = call(
        functools.partial(plane_kernel, plane, groups),
        [
            ((plane * rows, width), jnp.bfloat16),
            ((8, plane * rows), jnp.float32),
            ((1, plane * rows), jnp.float32),
        ],
        block_flops, *near_codes, *near_meta,
    )
    backs = []
    for far_code, far_side in reversed(list(zip(far_codes, far_meta))):
        best, back = call(
            functools.partial(block_kernel, plane, groups),
            [((1, plane * rows), jnp.float32), ((1, rows), jnp.float32)],
            block_flops, far_code, far_side, values, side, best,
        )
        backs.append(back)
    backs.reverse()

    result = best[:, :rows]
    for r in range(1, plane):
        result = jnp.maximum(
            result, lax.ppermute(best[:, r * rows:(r + 1) * rows], "blk", near[r])
        )
    me = lax.axis_index("blk")
    for pairs, back in zip(far, backs):
        home = lax.ppermute(back, "blk", [(b, a) for a, b in pairs])
        if len(pairs) < count:
            sent = functools.reduce(jnp.logical_or, [me == a for a, _ in pairs])
            home = jnp.where(sent, home, -1.0)
        result = jnp.maximum(result, home)
    return result.reshape(rows)


def solution(mesh):
    placed = (P(("parts", "blk"), None), P(("parts", "blk"), None), P(("parts", "blk")))
    return jax.shard_map(
        shards, mesh=mesh, in_specs=placed, out_specs=P(("parts", "blk")), check_vma=False
    )
```

time: 83.8 us -> 69.9 us (0.83)
  local copies, waits for them, and re-layouts: 17.2 us -> 1.12 us
  starting transfers between devices: 20.9 us -> 29.8 us
  waiting for transfers between devices: 38.7 us -> 32.8 us
  Pallas kernels: 0 us -> 3.69 us
  other arithmetic: 4.77 us -> 2.1 us
  matrix products: 1.71 us -> 0 us
    all_to_all x3 -> x0, waiting for transfers between devices: 38.7 us -> none  [the longest x1 30.7 us: shards(): lax.all_to_all(send_values, 'blk', split_axis=0, concat_axis=0, tiled=True)]
    ppermute x0 -> x15, waiting for transfers between devices: none -> 32.8 us  [the longest x3 22.4 us: shards(): lax.ppermute(meta, 'blk', pairs)]
    ppermute x0 -> x15, starting transfers between devices: none -> 29.8 us  [the longest x2 13.8 us: shards(): home = lax.ppermute(back, 'blk', [(b, a) for a, b in pairs])]
    all_to_all x3 -> x0, starting transfers between devices: 20.9 us -> none  [the longest x1 9.11 us: shards(): lax.all_to_all(result, 'blk', split_axis=0, concat_axis=0, tiled=True)]
    gather x3 -> x0, local copies, waits for them, and re-layouts: 10.5 us -> none  [the longest x1 4.98 us: shards(): send_clusters = jnp.where(filled, clusters[positions], -1)]
    pallas_call x0 -> x3, Pallas kernels: none -> 3.69 us  [call(): pl.pallas_call(kernel, out_shape=[jax.ShapeDtypeStruct(shape, dtype) for...]
    scatter x2 -> x0, local copies, waits for them, and re-layouts: 2.89 us -> none  [the longest x1 1.49 us: shards(): filled = jnp.zeros((slots_total,), jnp.bool_).at[slot].set(True)]
    all_to_all x5 -> x0, local copies, waits for them, and re-layouts: 2.44 us -> none  [the longest x3 1.26 us: shards(): lax.all_to_all(result, 'blk', split_axis=0, concat_axis=0, tiled=True)]
  transfers between devices with their start and end apart: 3 -> 15, of which waited for: 3 -> 4; matrix products, arithmetic and copies ran while one was open for 6% -> 2% of each run, Pallas kernels for 0% -> 4%
where the time goes in v1:
time: 69.9 us; the launch traced here: 69.6 us
  waiting for transfers between devices  32.8 us (47%)
  starting transfers between devices  29.8 us (43%)
  Pallas kernels  3.69 us (5%)
  other arithmetic  2.1 us (3%)
  local copies, waits for them, and re-layouts  1.12 us (2%)
    ppermute x3, waiting for transfers between devices, shards(): lax.ppermute(meta, 'blk', pairs)  22.4 us
    ppermute x2, starting transfers between devices, shards(): home = lax.ppermute(back, 'blk', [(b, a) for a, b in pairs])  13.8 us
    ppermute x2, waiting for transfers between devices, shards(): far_meta = [lax.ppermute(meta, 'blk', pairs) for pairs in far]  9.16 us
    ppermute x2, starting transfers between devices, shards(): far_codes = [lax.ppermute(codes, 'blk', pairs) for pairs in far]  4.37 us
    pallas_call x3, Pallas kernels, call(): pl.pallas_call(kernel, out_shape=[jax.ShapeDtypeStruct(shape, dtype) for...  3.69 us
    ppermute x2, starting transfers between devices, shards(): far_meta = [lax.ppermute(meta, 'blk', pairs) for pairs in far]  3.53 us
    ppermute x3, starting transfers between devices, shards(): lax.ppermute(codes, 'blk', pairs)  3.09 us
    ppermute x3, starting transfers between devices, shards(): lax.ppermute(meta, 'blk', pairs)  3.07 us
  transfers between devices with their start and end apart: 15, of which 4 were waited for; matrix products, arithmetic and copies ran while one was open for 2% of the time, Pallas kernels for 4%

profile of v1, /device:TPU:0, one launch (start us, length us, event | category | flops | bytes accessed | tf_op | source)
XLA Modules:
  0.0 69.6 jit_solution(10963225699109867839)
XLA Ops:
  0.0 0.5 collective-permute-start.2
  0.5 2.5 %collective-permute-start.3 = (bf16[256,1024]{1,0:T(8,128)(2,1)}, bf16[256,1024]{1,0:T(8,128)(2,1)S(1)}, u32[]{:S(2)}, u32[]{:S(2)}) collective-permute-start(bf16[256,1024]{1,0:T(8,128)(2,1)} %refs_0_.1), channel_id=1, source_target_pairs={{0,2},{1,3},{2,0},{3,1},{4,6},{5,7},{6,4},{7,5},{8,10},{9,11},{10,... | collective-permute-start | bytes 1572872 | tf_op jit(solution)/shard_map/ppermute | solution.py:139
  2.9 0.1 collective-permute-start.4
  3.1 0.8 %exponential_bitcast_fusion = f32[32,256]{1,0:T(8,128)S(1)} fusion(s32[256,32]{0,1:T(8,128)} %param.4), kind=kLoop, calls=%fused_computation.1 | loop fusion | flops 16384 | bytes 65536 | tf_op jit(solution)/shard_map/transpose | solution.py:132
  3.9 0.7 add_convert_fusion
  4.5 0.1 pad.2.clone
  4.6 0.1 maximum_maximum_fusion.refs_4_
  4.7 0.1 collective-permute-start.5
  4.8 1.9 %collective-permute-start.6 = (f32[40,256]{1,0:T(8,128)S(1)}, f32[40,256]{1,0:T(8,128)S(1)}, u32[]{:S(2)}, u32[]{:S(2)}) collective-permute-start(f32[40,256]{1,0:T(8,128)S(1)} %maximum_maximum_fusion.refs_4_), channel_id=1, source_target_pairs={{0,2},{1,3},{2,0},{3,1},{4,6},{5,7},{6,4},{7,5},{8,10},{9,11},{10,... | collective-permute-start | bytes 122888 | tf_op jit(solution)/shard_map/ppermute | solution.py:140
  6.7 1.3 %collective-permute-start.8 = (bf16[256,1024]{1,0:T(8,128)(2,1)}, bf16[256,1024]{1,0:T(8,128)(2,1)S(1)}, u32[]{:S(2)}, u32[]{:S(2)}) collective-permute-start(bf16[256,1024]{1,0:T(8,128)(2,1)} %refs_0_.1), channel_id=1, source_target_pairs={{4,0},{5,1},{6,2},{7,3},{8,12},{9,13},{10,14},{11,15},{20,16},{21,... | collective-permute-start | bytes 1572872 | tf_op jit(solution)/shard_map/ppermute | solution.py:137
  8.0 19.9 %collective-permute-done.6.refs_6_ = f32[40,256]{1,0:T(8,128)S(1)} collective-permute-done((f32[40,256]{1,0:T(8,128)S(1)}, f32[40,256]{1,0:T(8,128)S(1)}, u32[]{:S(2)}, u32[]{:S(2)}) %collective-permute-start.6) | collective-permute-done | bytes 40992 | tf_op jit(solution)/shard_map/ppermute | solution.py:140
  27.9 1.1 %collective-permute-start.7 = (f32[40,256]{1,0:T(8,128)S(1)}, f32[40,256]{1,0:T(8,128)S(1)}, u32[]{:S(2)}, u32[]{:S(2)}) collective-permute-start(f32[40,256]{1,0:T(8,128)S(1)} %maximum_maximum_fusion.refs_4_), channel_id=1, source_target_pairs={{0,3},{1,2},{2,1},{3,0},{4,7},{5,6},{6,5},{7,4},{8,11},{9,10},{10,... | collective-permute-start | bytes 122888 | tf_op jit(solution)/shard_map/ppermute | solution.py:140
  28.9 2.5 %collective-permute-done.7.refs_7_ = f32[40,256]{1,0:T(8,128)S(1)} collective-permute-done((f32[40,256]{1,0:T(8,128)S(1)}, f32[40,256]{1,0:T(8,128)S(1)}, u32[]{:S(2)}, u32[]{:S(2)}) %collective-permute-start.7) | collective-permute-done | bytes 40992 | tf_op jit(solution)/shard_map/ppermute | solution.py:140
  31.4 3.1 %collective-permute-start = (bf16[256,1024]{1,0:T(8,128)(2,1)}, bf16[256,1024]{1,0:T(8,128)(2,1)S(1)}, u32[]{:S(2)}, u32[]{:S(2)}) collective-permute-start(bf16[256,1024]{1,0:T(8,128)(2,1)} %refs_0_.1), channel_id=1, source_target_pairs={{0,8},{1,9},{2,10},{3,11},{4,12},{5,13},{6,14},{7,15},{8,4},{9,5},... | collective-permute-start | bytes 1572872 | tf_op jit(solution)/shard_map/ppermute | solution.py:137
  34.5 0.0 collective-permute-done.2.refs_1_
  34.5 1.3 %collective-permute-start.9 = (f32[40,256]{1,0:T(8,128)S(1)}, f32[40,256]{1,0:T(8,128)S(1)}, u32[]{:S(2)}, u32[]{:S(2)}) collective-permute-start(f32[40,256]{1,0:T(8,128)S(1)} %maximum_maximum_fusion.refs_4_), channel_id=1, source_target_pairs={{4,0},{5,1},{6,2},{7,3},{8,12},{9,13},{10,14},{11,15},{20,16},{21,... | collective-permute-start | bytes 122888 | tf_op jit(solution)/shard_map/ppermute | solution.py:138
  35.8 2.2 %collective-permute-start.1 = (f32[40,256]{1,0:T(8,128)S(1)}, f32[40,256]{1,0:T(8,128)S(1)}, u32[]{:S(2)}, u32[]{:S(2)}) collective-permute-start(f32[40,256]{1,0:T(8,128)S(1)} %maximum_maximum_fusion.refs_4_), channel_id=1, source_target_pairs={{0,8},{1,9},{2,10},{3,11},{4,12},{5,13},{6,14},{7,15},{8,4},{9,5},... | collective-permute-start | bytes 122888 | tf_op jit(solution)/shard_map/ppermute | solution.py:138
  38.1 0.0 collective-permute-done.4.refs_3_
  38.1 1.0 %copy-done = bf16[256,1024]{1,0:T(8,128)(2,1)S(1)} copy-done((bf16[256,1024]{1,0:T(8,128)(2,1)S(1)}, bf16[256,1024]{1,0:T(8,128)(2,1)}, u32[]{:S(2)}) %copy-start) | copy-done | bytes 524312
  39.1 1.5 %shard_map.37 = (bf16[1024,1024]{1,0:T(8,128)(2,1)S(1)}, f32[8,1024]{1,0:T(8,128)S(1)}, f32[1,1024]{1,0:T(1,128)S(1)}) custom-call(bf16[256,1024]{1,0:T(8,128)(2,1)S(1)} %copy-done, bf16[256,1024]{1,0:T(8,128)(2,1)S(1)} %collective-permute-done.2.refs_1_, bf16[256,1024]{1,0:T(8,128)(2,1)S(1)} %collective-permute-done.3.refs_2_, ...), custom_call_target="tpu_custom_call" | custom-call | flops 536870912 | bytes 4194304 | tf_op jit(solution)/shard_map/pallas_call | solution.py:88
  40.7 9.2 %collective-permute-done.9.meta_ref = f32[40,256]{1,0:T(8,128)S(1)} collective-permute-done((f32[40,256]{1,0:T(8,128)S(1)}, f32[40,256]{1,0:T(8,128)S(1)}, u32[]{:S(2)}, u32[]{:S(2)}) %collective-permute-start.9) | collective-permute-done | bytes 40992 | tf_op jit(solution)/shard_map/ppermute | solution.py:138
  49.8 0.0 collective-permute-done.8.codes_ref
  49.8 1.1 %shard_map.38 = (f32[1,1024]{1,0:T(1,128)S(1)}, f32[1,256]{1,0:T(1,128)S(1)}) custom-call(bf16[256,1024]{1,0:T(8,128)(2,1)S(1)} %collective-permute-done.8.codes_ref, f32[40,256]{1,0:T(8,128)S(1)} %collective-permute-done.9.meta_ref, bf16[1024,1024]{1,0:T(8,128)(2,1)S(1)} %get-tuple-element.12.values_ref, f32[8,1024]{1,0:T(8,128)S(1)} %get-tuple-element.13.side_ref, ...), custom_call_target="tpu_custom_call" | custom-call | flops 536870912 | bytes 4194304 | tf_op jit(solution)/shard_map/pallas_call | solution.py:88
  50.9 0.0 collective-permute-done.1.meta_ref
  50.9 1.1 %shard_map.39 = (f32[1,1024]{1,0:T(1,128)S(1)}, f32[1,256]{1,0:T(1,128)S(1)}) custom-call(bf16[256,1024]{1,0:T(8,128)(2,1)S(1)} %collective-permute-done.codes_ref, f32[40,256]{1,0:T(8,128)S(1)} %collective-permute-done.1.meta_ref, bf16[1024,1024]{1,0:T(8,128)(2,1)S(1)} %get-tuple-element.12.values_ref, f32[8,1024]{1,0:T(8,128)S(1)} %get-tuple-element.13.side_ref, ...), custom_call_target="tpu_custom_call" | custom-call | flops 536870912 | bytes 4194304 | tf_op jit(solution)/shard_map/pallas_call | solution.py:88
  52.0 0.1 collective-permute-start.10
  52.1 1.4 %collective-permute-start.11 = (f32[1,256]{1,0:T(1,128)S(1)}, f32[1,256]{1,0:T(1,128)S(1)}, u32[]{:S(2)}, u32[]{:S(2)}) collective-permute-start(f32[1,256]{1,0:T(1,128)S(1)} %get-tuple-element.21), channel_id=1, source_target_pairs={{0,2},{1,3},{2,0},{3,1},{4,6},{5,7},{6,4},{7,5},{8,10},{9,11},{10,... | collective-permute-start | bytes 3080 | tf_op jit(solution)/shard_map/ppermute | solution.py:165
  53.5 0.5 collective-permute-start.12
  53.9 12.6 %collective-permute-start.13 = (f32[1,256]{1,0:T(1,128)S(1)}, f32[1,256]{1,0:T(1,128)S(1)}, u32[]{:S(2)}, u32[]{:S(2)}) collective-permute-start(f32[1,256]{1,0:T(1,128)S(1)} %get-tuple-element.17), channel_id=1, source_target_pairs={{8,0},{9,1},{10,2},{11,3},{12,4},{13,5},{14,6},{15,7},{4,8},{5,9},... | collective-permute-start | bytes 3080 | tf_op jit(solution)/shard_map/ppermute | solution.py:169
  66.5 1.3 %collective-permute-start.14 = (f32[1,256]{1,0:T(1,128)S(1)}, f32[1,256]{1,0:T(1,128)S(1)}, u32[]{:S(2)}, u32[]{:S(2)}) collective-permute-start(f32[1,256]{1,0:T(1,128)S(1)} %get-tuple-element.18), channel_id=1, source_target_pairs={{0,4},{1,5},{2,6},{3,7},{12,8},{13,9},{14,10},{15,11},{16,20},{17,... | collective-permute-start | bytes 3080 | tf_op jit(solution)/shard_map/ppermute | solution.py:169
  67.9 1.2 %collective-permute-done.14 = f32[1,256]{1,0:T(1,128)S(1)} collective-permute-done((f32[1,256]{1,0:T(1,128)S(1)}, f32[1,256]{1,0:T(1,128)S(1)}, u32[]{:S(2)}, u32[]{:S(2)}) %collective-permute-start.14) | collective-permute-done | bytes 1056 | tf_op jit(solution)/shard_map/ppermute | solution.py:169
  69.1 0.6 fusion
  (10 shorter events, 0.0 us)
Async XLA Ops:
  0.0 34.5 %collective-permute-start.2 = (bf16[256,1024]{1,0:T(8,128)(2,1)}, bf16[256,1024]{1,0:T(8,128)(2,1)S(1)}, u32[]{:S(2)}, u32[]{:S(2)}) collective-permute-start(bf16[256,1024]{1,0:T(8,128)(2,1)} %refs_0_.1), channel_id=1, source_target_pairs={{0,1},{1,0},{2,3},{3,2},{4,5},{5,4},{6,7},{7,6},{8,9},{9,8},{10,11... | collective-permute-start | bytes 1572872 | tf_op jit(solution)/shard_map/ppermute | solution.py:139
  0.5 35.4 %collective-permute-start.3 = (bf16[256,1024]{1,0:T(8,128)(2,1)}, bf16[256,1024]{1,0:T(8,128)(2,1)S(1)}, u32[]{:S(2)}, u32[]{:S(2)}) collective-permute-start(bf16[256,1024]{1,0:T(8,128)(2,1)} %refs_0_.1), channel_id=1, source_target_pairs={{0,2},{1,3},{2,0},{3,1},{4,6},{5,7},{6,4},{7,5},{8,10},{9,11},{10,... | collective-permute-start | bytes 1572872 | tf_op jit(solution)/shard_map/ppermute | solution.py:139
  2.9 35.1 %collective-permute-start.4 = (bf16[256,1024]{1,0:T(8,128)(2,1)}, bf16[256,1024]{1,0:T(8,128)(2,1)S(1)}, u32[]{:S(2)}, u32[]{:S(2)}) collective-permute-start(bf16[256,1024]{1,0:T(8,128)(2,1)} %refs_0_.1), channel_id=1, source_target_pairs={{0,3},{1,2},{2,1},{3,0},{4,7},{5,6},{6,5},{7,4},{8,11},{9,10},{10,... | collective-permute-start | bytes 1572872 | tf_op jit(solution)/shard_map/ppermute | solution.py:139
  4.7 2.0 %collective-permute-start.5 = (f32[40,256]{1,0:T(8,128)S(1)}, f32[40,256]{1,0:T(8,128)S(1)}, u32[]{:S(2)}, u32[]{:S(2)}) collective-permute-start(f32[40,256]{1,0:T(8,128)S(1)} %maximum_maximum_fusion.refs_4_), channel_id=1, source_target_pairs={{0,1},{1,0},{2,3},{3,2},{4,5},{5,4},{6,7},{7,6},{8,9},{9,8},{10,11... | collective-permute-start | bytes 122888 | tf_op jit(solution)/shard_map/ppermute | solution.py:140
  4.8 23.1 %collective-permute-start.6 = (f32[40,256]{1,0:T(8,128)S(1)}, f32[40,256]{1,0:T(8,128)S(1)}, u32[]{:S(2)}, u32[]{:S(2)}) collective-permute-start(f32[40,256]{1,0:T(8,128)S(1)} %maximum_maximum_fusion.refs_4_), channel_id=1, source_target_pairs={{0,2},{1,3},{2,0},{3,1},{4,6},{5,7},{6,4},{7,5},{8,10},{9,11},{10,... | collective-permute-start | bytes 122888 | tf_op jit(solution)/shard_map/ppermute | solution.py:140
  6.7 43.1 %collective-permute-start.8 = (bf16[256,1024]{1,0:T(8,128)(2,1)}, bf16[256,1024]{1,0:T(8,128)(2,1)S(1)}, u32[]{:S(2)}, u32[]{:S(2)}) collective-permute-start(bf16[256,1024]{1,0:T(8,128)(2,1)} %refs_0_.1), channel_id=1, source_target_pairs={{4,0},{5,1},{6,2},{7,3},{8,12},{9,13},{10,14},{11,15},{20,16},{21,... | collective-permute-start | bytes 1572872 | tf_op jit(solution)/shard_map/ppermute | solution.py:137
  27.9 3.6 %collective-permute-start.7 = (f32[40,256]{1,0:T(8,128)S(1)}, f32[40,256]{1,0:T(8,128)S(1)}, u32[]{:S(2)}, u32[]{:S(2)}) collective-permute-start(f32[40,256]{1,0:T(8,128)S(1)} %maximum_maximum_fusion.refs_4_), channel_id=1, source_target_pairs={{0,3},{1,2},{2,1},{3,0},{4,7},{5,6},{6,5},{7,4},{8,11},{9,10},{10,... | collective-permute-start | bytes 122888 | tf_op jit(solution)/shard_map/ppermute | solution.py:140
  31.4 19.5 %collective-permute-start = (bf16[256,1024]{1,0:T(8,128)(2,1)}, bf16[256,1024]{1,0:T(8,128)(2,1)S(1)}, u32[]{:S(2)}, u32[]{:S(2)}) collective-permute-start(bf16[256,1024]{1,0:T(8,128)(2,1)} %refs_0_.1), channel_id=1, source_target_pairs={{0,8},{1,9},{2,10},{3,11},{4,12},{5,13},{6,14},{7,15},{8,4},{9,5},... | collective-permute-start | bytes 1572872 | tf_op jit(solution)/shard_map/ppermute | solution.py:137
  34.5 15.3 %collective-permute-start.9 = (f32[40,256]{1,0:T(8,128)S(1)}, f32[40,256]{1,0:T(8,128)S(1)}, u32[]{:S(2)}, u32[]{:S(2)}) collective-permute-start(f32[40,256]{1,0:T(8,128)S(1)} %maximum_maximum_fusion.refs_4_), channel_id=1, source_target_pairs={{4,0},{5,1},{6,2},{7,3},{8,12},{9,13},{10,14},{11,15},{20,16},{21,... | collective-permute-start | bytes 122888 | tf_op jit(solution)/shard_map/ppermute | solution.py:138
  35.8 15.1 %collective-permute-start.1 = (f32[40,256]{1,0:T(8,128)S(1)}, f32[40,256]{1,0:T(8,128)S(1)}, u32[]{:S(2)}, u32[]{:S(2)}) collective-permute-start(f32[40,256]{1,0:T(8,128)S(1)} %maximum_maximum_fusion.refs_4_), channel_id=1, source_target_pairs={{0,8},{1,9},{2,10},{3,11},{4,12},{5,13},{6,14},{7,15},{8,4},{9,5},... | collective-permute-start | bytes 122888 | tf_op jit(solution)/shard_map/ppermute | solution.py:138
  38.1 1.0 %copy-start = (bf16[256,1024]{1,0:T(8,128)(2,1)S(1)}, bf16[256,1024]{1,0:T(8,128)(2,1)}, u32[]{:S(2)}) copy-start(bf16[256,1024]{1,0:T(8,128)(2,1)} %refs_0_.1) | copy-start | bytes 1572868
  52.0 15.8 %collective-permute-start.10 = (f32[1,256]{1,0:T(1,128)S(1)}, f32[1,256]{1,0:T(1,128)S(1)}, u32[]{:S(2)}, u32[]{:S(2)}) collective-permute-start(f32[1,256]{1,0:T(1,128)S(1)} %get-tuple-element.19), channel_id=1, source_target_pairs={{0,1},{1,0},{2,3},{3,2},{4,5},{5,4},{6,7},{7,6},{8,9},{9,8},{10,11... | collective-permute-start | bytes 3080 | tf_op jit(solution)/shard_map/ppermute | solution.py:165
  52.1 15.7 %collective-permute-start.11 = (f32[1,256]{1,0:T(1,128)S(1)}, f32[1,256]{1,0:T(1,128)S(1)}, u32[]{:S(2)}, u32[]{:S(2)}) collective-permute-start(f32[1,256]{1,0:T(1,128)S(1)} %get-tuple-element.21), channel_id=1, source_target_pairs={{0,2},{1,3},{2,0},{3,1},{4,6},{5,7},{6,4},{7,5},{8,10},{9,11},{10,... | collective-permute-start | bytes 3080 | tf_op jit(solution)/shard_map/ppermute | solution.py:165
  53.5 14.3 %collective-permute-start.12 = (f32[1,256]{1,0:T(1,128)S(1)}, f32[1,256]{1,0:T(1,128)S(1)}, u32[]{:S(2)}, u32[]{:S(2)}) collective-permute-start(f32[1,256]{1,0:T(1,128)S(1)} %get-tuple-element.20), channel_id=1, source_target_pairs={{0,3},{1,2},{2,1},{3,0},{4,7},{5,6},{6,5},{7,4},{8,11},{9,10},{10,... | collective-permute-start | bytes 3080 | tf_op jit(solution)/shard_map/ppermute | solution.py:165
  53.9 13.9 %collective-permute-start.13 = (f32[1,256]{1,0:T(1,128)S(1)}, f32[1,256]{1,0:T(1,128)S(1)}, u32[]{:S(2)}, u32[]{:S(2)}) collective-permute-start(f32[1,256]{1,0:T(1,128)S(1)} %get-tuple-element.17), channel_id=1, source_target_pairs={{8,0},{9,1},{10,2},{11,3},{12,4},{13,5},{14,6},{15,7},{4,8},{5,9},... | collective-permute-start | bytes 3080 | tf_op jit(solution)/shard_map/ppermute | solution.py:169
  66.5 2.6 %collective-permute-start.14 = (f32[1,256]{1,0:T(1,128)S(1)}, f32[1,256]{1,0:T(1,128)S(1)}, u32[]{:S(2)}, u32[]{:S(2)}) collective-permute-start(f32[1,256]{1,0:T(1,128)S(1)} %get-tuple-element.18), channel_id=1, source_target_pairs={{0,4},{1,5},{2,6},{3,7},{12,8},{13,9},{14,10},{15,11},{16,20},{17,... | collective-permute-start | bytes 3080 | tf_op jit(solution)/shard_map/ppermute | solution.py:169

commit v2 on v1

--- a/solution.py
+++ b/solution.py
@@ -7,7 +7,8 @@
 from jax.sharding import PartitionSpec as P
 
 GROUP = 32
-META_ROWS = 40
+SIDE_ROWS = 16
+COST = 1
 VMEM_LIMIT = 32 * 1024 * 1024
 
 
@@ -21,31 +22,50 @@
     return jnp.sum(jnp.where(eye, column, 0.0), axis=0, keepdims=True)
 
 
-def dequantize(codes, meta, groups):
-    width = codes.shape[1]
+def pack_kernel(groups, codes_hbm, exponents_hbm, clusters_hbm, message_ref, codes_ref, exponents_ref, clusters_ref, sems):
+    copies = [
+        pltpu.make_async_copy(source, target, sems.at[i])
+        for i, (source, target) in enumerate(
+            [(exponents_hbm, exponents_ref), (clusters_hbm, clusters_ref), (codes_hbm, codes_ref)]
+        )
+    ]
+    for copy in copies:
+        copy.start()
+    rows, width = codes_ref.shape
+    copies[1].wait()
+    code = clusters_ref[...] + 1
+    row = lax.broadcasted_iota(jnp.int32, (SIDE_ROWS, rows), 0)
+    side = jnp.where(row == 0, code >> 8, jnp.where(row == 1, code & 255, 0))
+    message_ref[rows:, 0:rows] = side.astype(jnp.float32).astype(jnp.bfloat16)
+    message_ref[rows:, rows:] = jnp.zeros((SIDE_ROWS, width - rows), jnp.bfloat16)
     spread = (
         lax.broadcasted_iota(jnp.int32, (groups, width), 1) // GROUP
         == lax.broadcasted_iota(jnp.int32, (groups, width), 0)
     ).astype(jnp.bfloat16)
+    copies[0].wait()
     scale = lax.dot_general(
-        meta[:groups].astype(jnp.bfloat16), spread, (((0,), (0,)), ((), ())),
-        preferred_element_type=jnp.float32,
+        jnp.exp2(exponents_ref[...].astype(jnp.float32)).astype(jnp.bfloat16), spread,
+        (((0,), (0,)), ((), ())), preferred_element_type=jnp.float32,
     )
-    values = (codes.astype(jnp.float32) * scale).astype(jnp.bfloat16)
+    copies[2].wait()
+    message_ref[0:rows] = (codes_ref[...].astype(jnp.float32) * scale).astype(jnp.bfloat16)
+
+
+def unpack(message_ref):
+    rows = message_ref.shape[0] - SIDE_ROWS
+    values = message_ref[0:rows]
     wide = values.astype(jnp.float32)
     inverse = lax.rsqrt(jnp.sum(wide * wide, axis=1, keepdims=True) + 1e-06)
-    return values, inverse, meta[groups:groups + 1]
-
-
-def plane_kernel(planes, groups, *refs):
-    code_refs, meta_refs = refs[:planes], refs[planes:2 * planes]
-    values_ref, side_ref, best_ref = refs[2 * planes:]
-    rows = code_refs[0].shape[0]
-    own = own_inverse = own_code = None
+    side = message_ref[rows:, 0:rows].astype(jnp.float32)
+    return values, inverse, side[0:1] * 256.0 + side[1:2]
+
+
+def plane_kernel(planes, *refs):
+    side_ref, best_ref = refs[planes:]
+    rows = refs[0].shape[0] - SIDE_ROWS
     best = jnp.full((1, rows), -1.0, jnp.float32)
     for r in range(planes):
-        values, inverse, code = dequantize(code_refs[r][...], meta_refs[r][...], groups)
-        values_ref[r * rows:(r + 1) * rows] = values
+        values, inverse, code = unpack(refs[r])
         inverse_row = flatten(inverse, rows)
         side_ref[0:1, r * rows:(r + 1) * rows] = code
         side_ref[1:2, r * rows:(r + 1) * rows] = inverse_row
@@ -66,15 +86,18 @@
     best_ref[0:1, 0:rows] = best
 
 
-def block_kernel(planes, groups, codes_ref, meta_ref, values_ref, side_ref, before_ref, best_ref, back_ref):
-    rows = codes_ref.shape[0]
-    values, inverse, code = dequantize(codes_ref[...], meta_ref[...], groups)
+def block_kernel(planes, *refs):
+    block_ref, near_refs = refs[0], refs[1:1 + planes]
+    side_ref, before_ref, best_ref, back_ref = refs[1 + planes:]
+    values, inverse, code = unpack(block_ref)
+    rows = values.shape[0]
     code = expand(code, rows)
     back = jnp.full((rows, 1), -1.0, jnp.float32)
     for r in range(planes):
         at = slice(r * rows, (r + 1) * rows)
         dots = lax.dot_general(
-            values, values_ref[at], (((1,), (1,)), ((), ())), preferred_element_type=jnp.float32
+            values, near_refs[r][0:rows], (((1,), (1,)), ((), ())),
+            preferred_element_type=jnp.float32,
         )
         same = code == side_ref[0:1, at]
         scores = jnp.where(same, dots * inverse * side_ref[1:2, at], -1.0)
@@ -83,7 +106,7 @@
     back_ref[...] = flatten(back, rows)
 
 
-def call(kernel, shapes, flops, *operands):
+def call(kernel, shapes, *operands):
     spec = pl.BlockSpec(memory_space=pltpu.VMEM)
     return pl.pallas_call(
         kernel,
@@ -91,7 +114,7 @@
         in_specs=[spec] * len(operands),
         out_specs=[spec] * len(shapes),
         compiler_params=pltpu.CompilerParams(vmem_limit_bytes=VMEM_LIMIT),
-        cost_estimate=pl.CostEstimate(flops=flops, bytes_accessed=4 * 1024 * 1024, transcendentals=0),
+        cost_estimate=pl.CostEstimate(flops=COST, bytes_accessed=1, transcendentals=0),
     )(*operands)
 
 
@@ -127,34 +150,32 @@
         [(a * plane + p, b * plane + p) for a, b in pairs for p in range(plane)]
         for pairs in far_rounds(height)
     ]
-    meta = jnp.concatenate(
-        [
-            jnp.exp2(exponents.astype(jnp.float32)).T,
-            (clusters + 1).astype(jnp.float32)[None],
-            jnp.zeros((META_ROWS - groups - 1, rows), jnp.float32),
-        ]
-    )
-    far_codes = [lax.ppermute(codes, "blk", pairs) for pairs in far]
-    far_meta = [lax.ppermute(meta, "blk", pairs) for pairs in far]
-    near_codes = [codes] + [lax.ppermute(codes, "blk", pairs) for pairs in near[1:]]
-    near_meta = [meta] + [lax.ppermute(meta, "blk", pairs) for pairs in near[1:]]
-
-    block_flops = 2 * rows * rows * width * plane
-    values, side, best = call(
-        functools.partial(plane_kernel, plane, groups),
-        [
-            ((plane * rows, width), jnp.bfloat16),
-            ((8, plane * rows), jnp.float32),
-            ((1, plane * rows), jnp.float32),
+    message = pl.pallas_call(
+        functools.partial(pack_kernel, groups),
+        out_shape=jax.ShapeDtypeStruct((rows + SIDE_ROWS, width), jnp.bfloat16),
+        in_specs=[pl.BlockSpec(memory_space=pl.ANY)] * 3,
+        out_specs=pl.BlockSpec(memory_space=pltpu.VMEM),
+        scratch_shapes=[
+            pltpu.VMEM((rows, width), jnp.bfloat16),
+            pltpu.VMEM((groups, rows), jnp.int32),
+            pltpu.VMEM((1, rows), jnp.int32),
+            pltpu.SemaphoreType.DMA((3,)),
         ],
-        block_flops, *near_codes, *near_meta,
+        compiler_params=pltpu.CompilerParams(vmem_limit_bytes=VMEM_LIMIT),
+    )(codes, exponents.T, clusters[None])
+    far_blocks = [lax.ppermute(message, "blk", pairs) for pairs in far]
+    near_blocks = [message] + [lax.ppermute(message, "blk", pairs) for pairs in near[1:]]
+    side, best = call(
+        functools.partial(plane_kernel, plane),
+        [((8, plane * rows), jnp.float32), ((1, plane * rows), jnp.float32)],
+        *near_blocks,
     )
     backs = []
-    for far_code, far_side in reversed(list(zip(far_codes, far_meta))):
+    for block in reversed(far_blocks):
         best, back = call(
-            functools.partial(block_kernel, plane, groups),
+            functools.partial(block_kernel, plane),
             [((1, plane * rows), jnp.float32), ((1, rows), jnp.float32)],
-            block_flops, far_code, far_side, values, side, best,
+            block, *near_blocks, side, best,
         )
         backs.append(back)
     backs.reverse()

time: 69.9 us -> 45.4 us (0.65)
  starting transfers between devices: 29.8 us -> 16.2 us
  waiting for transfers between devices: 32.8 us -> 22.3 us
  other arithmetic: 2.1 us -> 0.57 us
  local copies, waits for them, and re-layouts: 1.12 us -> 2.48 us
    ppermute x10 -> x5, waiting for transfers between devices: 31.5 us -> 21.1 us  [the longest x3 18.4 us: shards(): lax.ppermute(message, 'blk', pairs)]
    ppermute x2, starting transfers between devices: 13.8 us -> 4.54 us  [shards(): home = lax.ppermute(back, 'blk', [(b, a) for a, b in pairs])]
    ppermute x10 -> x5, starting transfers between devices: 14.1 us -> 9.53 us  [the longest x2 6.38 us: shards(): far_blocks = [lax.ppermute(message, 'blk', pairs) for pairs in far]]
    unnamed x2 -> x6, local copies, waits for them, and re-layouts: 1.04 us -> 2.48 us
    pallas_call x3, Pallas kernels: 3.69 us -> 2.91 us  [call(): pl.pallas_call(kernel, out_shape=[jax.ShapeDtypeStruct(shape, dtype) for...]
    transpose x1 -> x0, other arithmetic: 0.77 us -> none  [shards(): jnp.exp2(exponents.astype(jnp.float32))]
  transfers between devices with their start and end apart: 15 -> 10, of which waited for: 4 -> 4; matrix products, arithmetic and copies ran while one was open for 2% -> 0% of each run, Pallas kernels for 4% -> 4%
where the time goes in v2:
time: 45.4 us; the launch traced here: 45.1 us
  waiting for transfers between devices  22.3 us (49%)
  starting transfers between devices  16.2 us (36%)
  Pallas kernels  3.4 us (7%)
  local copies, waits for them, and re-layouts  2.48 us (5%)
  other arithmetic  0.57 us (1%)
    ppermute x3, waiting for transfers between devices, shards(): lax.ppermute(message, 'blk', pairs)  18.4 us
    ppermute x2, starting transfers between devices, shards(): far_blocks = [lax.ppermute(message, 'blk', pairs) for pairs in far]  6.38 us
    ppermute x2, starting transfers between devices, shards(): home = lax.ppermute(back, 'blk', [(b, a) for a, b in pairs])  4.54 us
    ppermute x3, starting transfers between devices, shards(): lax.ppermute(message, 'blk', pairs)  3.16 us
    pallas_call x3, Pallas kernels, call(): pl.pallas_call(kernel, out_shape=[jax.ShapeDtypeStruct(shape, dtype) for...  2.91 us
    ppermute x2, waiting for transfers between devices, shards(): far_blocks = [lax.ppermute(message, 'blk', pairs) for pairs in far]  2.69 us
    unnamed x6, local copies, waits for them, and re-layouts  2.48 us
    ppermute x3, starting transfers between devices, shards(): lax.ppermute(best[:, r * rows:(r + 1) * rows], 'blk', near[r])  2.14 us
  transfers between devices with their start and end apart: 10, of which 4 were waited for; matrix products, arithmetic and copies ran while one was open for 0% of the time, Pallas kernels for 4%

profile of v2, /device:TPU:0, one launch (start us, length us, event | category | flops | bytes accessed | tf_op | source)
XLA Modules:
  0.0 45.1 jit_solution(16139762457970543470)
XLA Ops:
  0.0 0.0 copy-start.2
  0.0 0.7 %copy-done.2 = s32[256]{0:T(256)S(1)} copy-done((s32[256]{0:T(256)S(1)}, s32[256]{0:T(256)}, u32[]{:S(2)}) %copy-start.2) | copy-done | bytes 1048
  0.7 0.0 copy-start
  0.7 1.0 %copy-done = bf16[256,1024]{1,0:T(8,128)(2,1)S(1)} copy-done((bf16[256,1024]{1,0:T(8,128)(2,1)S(1)}, bf16[256,1024]{1,0:T(8,128)(2,1)}, u32[]{:S(2)}) %copy-start) | copy-done | bytes 524312
  1.7 0.0 copy-start.1
  1.7 0.8 %copy-done.1 = s32[256,32]{0,1:T(8,128)S(1)} copy-done((s32[256,32]{0,1:T(8,128)S(1)}, s32[256,32]{0,1:T(8,128)}, u32[]{:S(2)}) %copy-start.1) | copy-done | bytes 32792
  2.5 0.5 %shard_map.37.refs_0_.refs_1_ = bf16[272,1024]{1,0:T(8,128)(2,1)S(1)} custom-call(bf16[256,1024]{1,0:T(8,128)(2,1)S(1)} %copy-done, s32[32,256]{1,0:T(8,128)S(1)} %bitcast.3, s32[1,256]{1,0:T(1,128)S(1)} %bitcast.4), custom_call_target="tpu_custom_call" | custom-call | tf_op jit(solution)/shard_map/pallas_call | solution.py:153
  3.0 0.5 %collective-permute-start.1 = (bf16[272,1024]{1,0:T(8,128)(2,1)S(1)}, bf16[272,1024]{1,0:T(8,128)(2,1)S(1)}, u32[]{:S(2)}, u32[]{:S(2)}) collective-permute-start(bf16[272,1024]{1,0:T(8,128)(2,1)S(1)} %shard_map.37.refs_0_.refs_1_), channel_id=1, source_target_pairs={{0,1},{1,0},{2,3},{3,2},{4,5},{5,4},{6,7},{7,6},{8,9},{9,8},{10,11... | collective-permute-start | bytes 1671176 | tf_op jit(solution)/shard_map/ppermute | solution.py:167
  3.5 2.6 %collective-permute-start.2 = (bf16[272,1024]{1,0:T(8,128)(2,1)S(1)}, bf16[272,1024]{1,0:T(8,128)(2,1)S(1)}, u32[]{:S(2)}, u32[]{:S(2)}) collective-permute-start(bf16[272,1024]{1,0:T(8,128)(2,1)S(1)} %shard_map.37.refs_0_.refs_1_), channel_id=1, source_target_pairs={{0,2},{1,3},{2,0},{3,1},{4,6},{5,7},{6,4},{7,5},{8,10},{9,11},{10,... | collective-permute-start | bytes 1671176 | tf_op jit(solution)/shard_map/ppermute | solution.py:167
  6.1 0.1 collective-permute-start.3
  6.1 1.3 %collective-permute-start.4 = (bf16[272,1024]{1,0:T(8,128)(2,1)S(1)}, bf16[272,1024]{1,0:T(8,128)(2,1)S(1)}, u32[]{:S(2)}, u32[]{:S(2)}) collective-permute-start(bf16[272,1024]{1,0:T(8,128)(2,1)S(1)} %shard_map.37.refs_0_.refs_1_), channel_id=1, source_target_pairs={{4,0},{5,1},{6,2},{7,3},{8,12},{9,13},{10,14},{11,15},{20,16},{21,... | collective-permute-start | bytes 1671176 | tf_op jit(solution)/shard_map/ppermute | solution.py:166
  7.4 5.1 %collective-permute-start = (bf16[272,1024]{1,0:T(8,128)(2,1)S(1)}, bf16[272,1024]{1,0:T(8,128)(2,1)S(1)}, u32[]{:S(2)}, u32[]{:S(2)}) collective-permute-start(bf16[272,1024]{1,0:T(8,128)(2,1)S(1)} %shard_map.37.refs_0_.refs_1_), channel_id=1, source_target_pairs={{0,8},{1,9},{2,10},{3,11},{4,12},{5,13},{6,14},{7,15},{8,4},{9,5},... | collective-permute-start | bytes 1671176 | tf_op jit(solution)/shard_map/ppermute | solution.py:166
  12.5 0.0 collective-permute-done.1.refs_1_.refs_2_
  12.5 7.0 %collective-permute-done.2.refs_2_.refs_3_ = bf16[272,1024]{1,0:T(8,128)(2,1)S(1)} collective-permute-done((bf16[272,1024]{1,0:T(8,128)(2,1)S(1)}, bf16[272,1024]{1,0:T(8,128)(2,1)S(1)}, u32[]{:S(2)}, u32[]{:S(2)}) %collective-permute-start.2) | collective-permute-done | bytes 557088 | tf_op jit(solution)/shard_map/ppermute | solution.py:167
  19.6 11.4 %collective-permute-done.3.refs_3_.refs_4_ = bf16[272,1024]{1,0:T(8,128)(2,1)S(1)} collective-permute-done((bf16[272,1024]{1,0:T(8,128)(2,1)S(1)}, bf16[272,1024]{1,0:T(8,128)(2,1)S(1)}, u32[]{:S(2)}, u32[]{:S(2)}) %collective-permute-start.3) | collective-permute-done | bytes 557088 | tf_op jit(solution)/shard_map/ppermute | solution.py:167
  31.0 1.0 %shard_map.38 = (f32[8,1024]{1,0:T(8,128)S(1)}, f32[1,1024]{1,0:T(1,128)S(1)}) custom-call(bf16[272,1024]{1,0:T(8,128)(2,1)S(1)} %shard_map.37.refs_0_.refs_1_, bf16[272,1024]{1,0:T(8,128)(2,1)S(1)} %collective-permute-done.1.refs_1_.refs_2_, bf16[272,1024]{1,0:T(8,128)(2,1)S(1)} %collective-permute-done.2.refs_2_.refs_3_, ...), custom_call_target="tpu_custom_call" | custom-call | flops 1 | bytes 1 | tf_op jit(solution)/shard_map/pallas_call | solution.py:111
  31.9 2.7 %collective-permute-done.4.refs_0_ = bf16[272,1024]{1,0:T(8,128)(2,1)S(1)} collective-permute-done((bf16[272,1024]{1,0:T(8,128)(2,1)S(1)}, bf16[272,1024]{1,0:T(8,128)(2,1)S(1)}, u32[]{:S(2)}, u32[]{:S(2)}) %collective-permute-start.4) | collective-permute-done | bytes 557088 | tf_op jit(solution)/shard_map/ppermute | solution.py:166
  34.6 1.0 %shard_map.39 = (f32[1,1024]{1,0:T(1,128)S(1)}, f32[1,256]{1,0:T(1,128)S(1)}) custom-call(bf16[272,1024]{1,0:T(8,128)(2,1)S(1)} %collective-permute-done.4.refs_0_, bf16[272,1024]{1,0:T(8,128)(2,1)S(1)} %shard_map.37.refs_0_.refs_1_, bf16[272,1024]{1,0:T(8,128)(2,1)S(1)} %collective-permute-done.1.refs_1_.refs_2_, ...), custom_call_target="tpu_custom_call" | custom-call | flops 1 | bytes 1 | tf_op jit(solution)/shard_map/pallas_call | solution.py:111
  35.6 0.0 collective-permute-done.refs_0_
  35.6 1.0 %shard_map.40 = (f32[1,1024]{1,0:T(1,128)S(1)}, f32[1,256]{1,0:T(1,128)S(1)}) custom-call(bf16[272,1024]{1,0:T(8,128)(2,1)S(1)} %collective-permute-done.refs_0_, bf16[272,1024]{1,0:T(8,128)(2,1)S(1)} %shard_map.37.refs_0_.refs_1_, bf16[272,1024]{1,0:T(8,128)(2,1)S(1)} %collective-permute-done.1.refs_1_.refs_2_, ...), custom_call_target="tpu_custom_call" | custom-call | flops 1 | bytes 1 | tf_op jit(solution)/shard_map/pallas_call | solution.py:111
  36.6 0.1 collective-permute-start.5
  36.7 2.0 %collective-permute-start.6 = (f32[1,256]{1,0:T(1,128)S(1)}, f32[1,256]{1,0:T(1,128)S(1)}, u32[]{:S(2)}, u32[]{:S(2)}) collective-permute-start(f32[1,256]{1,0:T(1,128)S(1)} %get-tuple-element.19), channel_id=1, source_target_pairs={{0,2},{1,3},{2,0},{3,1},{4,6},{5,7},{6,4},{7,5},{8,10},{9,11},{10,... | collective-permute-start | bytes 3080 | tf_op jit(solution)/shard_map/ppermute | solution.py:186
  38.7 0.1 collective-permute-start.7
  38.7 3.3 %collective-permute-start.8 = (f32[1,256]{1,0:T(1,128)S(1)}, f32[1,256]{1,0:T(1,128)S(1)}, u32[]{:S(2)}, u32[]{:S(2)}) collective-permute-start(f32[1,256]{1,0:T(1,128)S(1)} %get-tuple-element.15), channel_id=1, source_target_pairs={{8,0},{9,1},{10,2},{11,3},{12,4},{13,5},{14,6},{15,7},{4,8},{5,9},... | collective-permute-start | bytes 3080 | tf_op jit(solution)/shard_map/ppermute | solution.py:190
  42.0 1.3 %collective-permute-start.9 = (f32[1,256]{1,0:T(1,128)S(1)}, f32[1,256]{1,0:T(1,128)S(1)}, u32[]{:S(2)}, u32[]{:S(2)}) collective-permute-start(f32[1,256]{1,0:T(1,128)S(1)} %get-tuple-element.16), channel_id=1, source_target_pairs={{0,4},{1,5},{2,6},{3,7},{12,8},{13,9},{14,10},{15,11},{16,20},{17,... | collective-permute-start | bytes 3080 | tf_op jit(solution)/shard_map/ppermute | solution.py:190
  43.3 0.0 collective-permute-done.5
  43.3 0.0 collective-permute-done.6
  43.3 0.0 collective-permute-done.7
  43.3 0.0 collective-permute-done.8
  43.4 1.2 %collective-permute-done.9 = f32[1,256]{1,0:T(1,128)S(1)} collective-permute-done((f32[1,256]{1,0:T(1,128)S(1)}, f32[1,256]{1,0:T(1,128)S(1)}, u32[]{:S(2)}, u32[]{:S(2)}) %collective-permute-start.9) | collective-permute-done | bytes 1056 | tf_op jit(solution)/shard_map/ppermute | solution.py:190
  44.6 0.6 %fusion = f32[1,256]{1,0:T(1,128)} fusion(f32[1,256]{1,0:T(1,128)S(1)} %collective-permute-done.9, pred[]{:T(512)S(6)} %or.27, f32[1,256]{1,0:T(1,128)S(1)} %collective-permute-done.8, f32[1,256]{1,0:T(1,128)S(1)} %collective-permute-done.7, f32[1,256]{1,0:T(1,128)S(1)} %collective-permute-done.6, f32[1,256]{1,0:T(1,128)S(1)} %collective-permute-done.5, ...), kind=kLoop, calls=%fused_computation.1 | loop fusion | flops 1536 | bytes 7169 | tf_op jit(solution)/shard_map/max | solution.py:194
  (1 shorter events, 0.0 us)
Async XLA Ops:
  0.0 0.7 %copy-start.2 = (s32[256]{0:T(256)S(1)}, s32[256]{0:T(256)}, u32[]{:S(2)}) copy-start(s32[256]{0:T(256)} %param.5) | copy-start | bytes 3076
  0.7 1.0 %copy-start = (bf16[256,1024]{1,0:T(8,128)(2,1)S(1)}, bf16[256,1024]{1,0:T(8,128)(2,1)}, u32[]{:S(2)}) copy-start(bf16[256,1024]{1,0:T(8,128)(2,1)} %codes_hbm.1) | copy-start | bytes 1572868
  1.7 0.8 %copy-start.1 = (s32[256,32]{0,1:T(8,128)S(1)}, s32[256,32]{0,1:T(8,128)}, u32[]{:S(2)}) copy-start(s32[256,32]{0,1:T(8,128)} %param.4) | copy-start | bytes 98308
  3.0 9.5 %collective-permute-start.1 = (bf16[272,1024]{1,0:T(8,128)(2,1)S(1)}, bf16[272,1024]{1,0:T(8,128)(2,1)S(1)}, u32[]{:S(2)}, u32[]{:S(2)}) collective-permute-start(bf16[272,1024]{1,0:T(8,128)(2,1)S(1)} %shard_map.37.refs_0_.refs_1_), channel_id=1, source_target_pairs={{0,1},{1,0},{2,3},{3,2},{4,5},{5,4},{6,7},{7,6},{8,9},{9,8},{10,11... | collective-permute-start | bytes 1671176 | tf_op jit(solution)/shard_map/ppermute | solution.py:167
  3.5 16.0 %collective-permute-start.2 = (bf16[272,1024]{1,0:T(8,128)(2,1)S(1)}, bf16[272,1024]{1,0:T(8,128)(2,1)S(1)}, u32[]{:S(2)}, u32[]{:S(2)}) collective-permute-start(bf16[272,1024]{1,0:T(8,128)(2,1)S(1)} %shard_map.37.refs_0_.refs_1_), channel_id=1, source_target_pairs={{0,2},{1,3},{2,0},{3,1},{4,6},{5,7},{6,4},{7,5},{8,10},{9,11},{10,... | collective-permute-start | bytes 1671176 | tf_op jit(solution)/shard_map/ppermute | solution.py:167
  6.1 24.9 %collective-permute-start.3 = (bf16[272,1024]{1,0:T(8,128)(2,1)S(1)}, bf16[272,1024]{1,0:T(8,128)(2,1)S(1)}, u32[]{:S(2)}, u32[]{:S(2)}) collective-permute-start(bf16[272,1024]{1,0:T(8,128)(2,1)S(1)} %shard_map.37.refs_0_.refs_1_), channel_id=1, source_target_pairs={{0,3},{1,2},{2,1},{3,0},{4,7},{5,6},{6,5},{7,4},{8,11},{9,10},{10,... | collective-permute-start | bytes 1671176 | tf_op jit(solution)/shard_map/ppermute | solution.py:167
  6.1 28.5 %collective-permute-start.4 = (bf16[272,1024]{1,0:T(8,128)(2,1)S(1)}, bf16[272,1024]{1,0:T(8,128)(2,1)S(1)}, u32[]{:S(2)}, u32[]{:S(2)}) collective-permute-start(bf16[272,1024]{1,0:T(8,128)(2,1)S(1)} %shard_map.37.refs_0_.refs_1_), channel_id=1, source_target_pairs={{4,0},{5,1},{6,2},{7,3},{8,12},{9,13},{10,14},{11,15},{20,16},{21,... | collective-permute-start | bytes 1671176 | tf_op jit(solution)/shard_map/ppermute | solution.py:166
  7.4 28.2 %collective-permute-start = (bf16[272,1024]{1,0:T(8,128)(2,1)S(1)}, bf16[272,1024]{1,0:T(8,128)(2,1)S(1)}, u32[]{:S(2)}, u32[]{:S(2)}) collective-permute-start(bf16[272,1024]{1,0:T(8,128)(2,1)S(1)} %shard_map.37.refs_0_.refs_1_), channel_id=1, source_target_pairs={{0,8},{1,9},{2,10},{3,11},{4,12},{5,13},{6,14},{7,15},{8,4},{9,5},... | collective-permute-start | bytes 1671176 | tf_op jit(solution)/shard_map/ppermute | solution.py:166
  36.6 6.7 %collective-permute-start.5 = (f32[1,256]{1,0:T(1,128)S(1)}, f32[1,256]{1,0:T(1,128)S(1)}, u32[]{:S(2)}, u32[]{:S(2)}) collective-permute-start(f32[1,256]{1,0:T(1,128)S(1)} %get-tuple-element.17), channel_id=1, source_target_pairs={{0,1},{1,0},{2,3},{3,2},{4,5},{5,4},{6,7},{7,6},{8,9},{9,8},{10,11... | collective-permute-start | bytes 3080 | tf_op jit(solution)/shard_map/ppermute | solution.py:186
  36.7 6.7 %collective-permute-start.6 = (f32[1,256]{1,0:T(1,128)S(1)}, f32[1,256]{1,0:T(1,128)S(1)}, u32[]{:S(2)}, u32[]{:S(2)}) collective-permute-start(f32[1,256]{1,0:T(1,128)S(1)} %get-tuple-element.19), channel_id=1, source_target_pairs={{0,2},{1,3},{2,0},{3,1},{4,6},{5,7},{6,4},{7,5},{8,10},{9,11},{10,... | collective-permute-start | bytes 3080 | tf_op jit(solution)/shard_map/ppermute | solution.py:186
  38.7 4.7 %collective-permute-start.7 = (f32[1,256]{1,0:T(1,128)S(1)}, f32[1,256]{1,0:T(1,128)S(1)}, u32[]{:S(2)}, u32[]{:S(2)}) collective-permute-start(f32[1,256]{1,0:T(1,128)S(1)} %get-tuple-element.18), channel_id=1, source_target_pairs={{0,3},{1,2},{2,1},{3,0},{4,7},{5,6},{6,5},{7,4},{8,11},{9,10},{10,... | collective-permute-start | bytes 3080 | tf_op jit(solution)/shard_map/ppermute | solution.py:186
  38.7 4.6 %collective-permute-start.8 = (f32[1,256]{1,0:T(1,128)S(1)}, f32[1,256]{1,0:T(1,128)S(1)}, u32[]{:S(2)}, u32[]{:S(2)}) collective-permute-start(f32[1,256]{1,0:T(1,128)S(1)} %get-tuple-element.15), channel_id=1, source_target_pairs={{8,0},{9,1},{10,2},{11,3},{12,4},{13,5},{14,6},{15,7},{4,8},{5,9},... | collective-permute-start | bytes 3080 | tf_op jit(solution)/shard_map/ppermute | solution.py:190
  42.0 2.6 %collective-permute-start.9 = (f32[1,256]{1,0:T(1,128)S(1)}, f32[1,256]{1,0:T(1,128)S(1)}, u32[]{:S(2)}, u32[]{:S(2)}) collective-permute-start(f32[1,256]{1,0:T(1,128)S(1)} %get-tuple-element.16), channel_id=1, source_target_pairs={{0,4},{1,5},{2,6},{3,7},{12,8},{13,9},{14,10},{15,11},{16,20},{17,... | collective-permute-start | bytes 3080 | tf_op jit(solution)/shard_map/ppermute | solution.py:190

commit v3 on v2

v3 whole, which is shorter than its diff:
```python
import functools
import jax
import jax.numpy as jnp
from jax import lax
from jax.experimental import pallas as pl
from jax.experimental.pallas import tpu as pltpu
from jax.sharding import PartitionSpec as P

GROUP = 32
SIDE_ROWS = 16
COST = 1
CHUNKS = 4
PACK_LIMIT = 32 * 1024 * 1024
VMEM_LIMIT = 32 * 1024 * 1024


def expand(lane_row, rows):
    eye = lax.broadcasted_iota(jnp.int32, (rows, rows), 0) == lax.broadcasted_iota(jnp.int32, (rows, rows), 1)
    return jnp.sum(jnp.where(eye, lane_row, 0.0), axis=1, keepdims=True)


def flatten(column, rows):
    eye = lax.broadcasted_iota(jnp.int32, (rows, rows), 0) == lax.broadcasted_iota(jnp.int32, (rows, rows), 1)
    return jnp.sum(jnp.where(eye, column, 0.0), axis=0, keepdims=True)


def spread_scale(scale, width):
    groups = scale.shape[0]
    spread = (
        lax.broadcasted_iota(jnp.int32, (groups, width), 1) // GROUP
        == lax.broadcasted_iota(jnp.int32, (groups, width), 0)
    ).astype(jnp.bfloat16)
    return lax.dot_general(
        scale, spread, (((0,), (0,)), ((), ())), preferred_element_type=jnp.float32
    )


def pack_kernel(groups, codes_hbm, exponents_hbm, clusters_hbm, message_ref, side_ref, codes_ref, exponents_ref, clusters_ref, sems):
    copies = [
        pltpu.make_async_copy(source, target, sems.at[i])
        for i, (source, target) in enumerate(
            [(exponents_hbm, exponents_ref), (clusters_hbm, clusters_ref), (codes_hbm, codes_ref)]
        )
    ]
    for copy in copies:
        copy.start()
    rows, width = codes_ref.shape
    copies[1].wait()
    code = clusters_ref[...] + 1
    row = lax.broadcasted_iota(jnp.int32, (SIDE_ROWS, rows), 0)
    side = jnp.where(row == 0, code >> 8, jnp.where(row == 1, code & 255, 0))
    side = side.astype(jnp.float32).astype(jnp.bfloat16)
    message_ref[rows:, 0:rows] = side
    message_ref[rows:, rows:] = jnp.zeros((SIDE_ROWS, width - rows), jnp.bfloat16)
    side_ref[groups:] = side
    copies[0].wait()
    scale = jnp.exp2(exponents_ref[...].astype(jnp.float32)).astype(jnp.bfloat16)
    side_ref[0:groups] = scale
    scale = spread_scale(scale, width)
    copies[2].wait()
    message_ref[0:rows] = (codes_ref[...].astype(jnp.float32) * scale).astype(jnp.bfloat16)


def cluster_code(parts):
    parts = parts.astype(jnp.float32)
    return parts[0:1] * 256.0 + parts[1:2]


def inverse_norm(values):
    wide = values.astype(jnp.float32)
    return lax.rsqrt(jnp.sum(wide * wide, axis=1, keepdims=True) + 1e-06)


def unpack_near(message_ref):
    rows = message_ref.shape[0] - SIDE_ROWS
    values = message_ref[0:rows]
    return values, inverse_norm(values), cluster_code(message_ref[rows:, 0:rows])


def unpack_far(codes_ref, side_ref):
    groups = side_ref.shape[0] - SIDE_ROWS
    scale = spread_scale(side_ref[0:groups], codes_ref.shape[1])
    values = (codes_ref[...].astype(jnp.float32) * scale).astype(jnp.bfloat16)
    return values, inverse_norm(values), cluster_code(side_ref[groups:])


def plane_kernel(planes, *refs):
    values_ref, lanes_ref, best_ref = refs[planes:]
    rows = refs[0].shape[0] - SIDE_ROWS
    best = jnp.full((1, rows), -1.0, jnp.float32)
    for r in range(planes):
        values, inverse, code = unpack_near(refs[r])
        values_ref[r * rows:(r + 1) * rows] = values
        inverse_row = flatten(inverse, rows)
        lanes_ref[0:1, r * rows:(r + 1) * rows] = code
        lanes_ref[1:2, r * rows:(r + 1) * rows] = inverse_row
        if r == 0:
            own, own_inverse, own_code = values, inverse_row, code
        dots = lax.dot_general(
            values, own, (((1,), (1,)), ((), ())), preferred_element_type=jnp.float32
        )
        same = expand(code, rows) == own_code
        if r == 0:
            same &= (
                lax.broadcasted_iota(jnp.int32, (rows, rows), 0)
                != lax.broadcasted_iota(jnp.int32, (rows, rows), 1)
            )
        scores = jnp.where(same, dots * inverse * own_inverse, -1.0)
        best = jnp.maximum(best, jnp.max(scores, axis=0, keepdims=True))
    best_ref[...] = jnp.full(best_ref.shape, -1.0, jnp.float32)
    best_ref[0:1, 0:rows] = best


def far_kernel(planes, fars, *refs):
    code_refs, side_refs = refs[:fars], refs[fars:2 * fars]
    values_ref, lanes_ref, before_ref = refs[2 * fars:2 * fars + 3]
    outs = refs[2 * fars + 3:]
    back_refs, best_refs = outs[:fars], outs[fars:]
    rows = code_refs[0].shape[0]
    bests = [before_ref[0:1, r * rows:(r + 1) * rows] for r in range(planes)]
    for code_ref, side_ref, back_ref in zip(code_refs, side_refs, back_refs):
        values, inverse, code = unpack_far(code_ref, side_ref)
        code = expand(code, rows)
        back = jnp.full((rows, 1), -1.0, jnp.float32)
        for r in range(planes):
            at = slice(r * rows, (r + 1) * rows)
            dots = lax.dot_general(
                values, values_ref[at], (((1,), (1,)), ((), ())),
                preferred_element_type=jnp.float32,
            )
            same = code == lanes_ref[0:1, at]
            scores = jnp.where(same, dots * inverse * lanes_ref[1:2, at], -1.0)
            back = jnp.maximum(back, jnp.max(scores, axis=1, keepdims=True))
            bests[r] = jnp.maximum(bests[r], jnp.max(scores, axis=0, keepdims=True))
        back_ref[...] = flatten(back, rows)
    for r in range(planes):
        best_refs[r][...] = bests[r]


def call(kernel, shapes, *operands):
    spec = pl.BlockSpec(memory_space=pltpu.VMEM)
    return pl.pallas_call(
        kernel,
        out_shape=[jax.ShapeDtypeStruct(shape, dtype) for shape, dtype in shapes],
        in_specs=[spec] * len(operands),
        out_specs=[spec] * len(shapes),
        compiler_params=pltpu.CompilerParams(vmem_limit_bytes=VMEM_LIMIT),
        cost_estimate=pl.CostEstimate(flops=COST, bytes_accessed=1, transcendentals=0),
    )(*operands)


def split_axis(count):
    planes = 1
    while planes * planes * 4 <= count:
        planes *= 2
    if count % planes or (count // planes) & (count // planes - 1):
        return 1, count
    return planes, count // planes


def far_rounds(height):
    rounds = []
    for step in range(2, height, 2):
        top = 1 << (step.bit_length() - 1)
        rounds.append([(a, a ^ (step + 1) if a & top else a ^ step) for a in range(height)])
    if height > 1:
        rounds.append([(a, a ^ 1) for a in range(height) if (a & 1) != (a >> 1 & 1)])
    return rounds


def shards(codes, exponents, clusters):
    count = lax.axis_size("blk")
    rows, width = codes.shape
    groups = exponents.shape[1]
    plane, height = split_axis(count)
    near = [
        [(z * plane + p, z * plane + (p ^ r)) for z in range(height) for p in range(plane)]
        for r in range(plane)
    ]
    far = [
        [(a * plane + p, b * plane + p) for a, b in pairs for p in range(plane)]
        for pairs in far_rounds(height)
    ]
    far_codes = [lax.ppermute(codes, "blk", pairs) for pairs in far]

    def near_phase(codes, exponents, clusters):
        message, side = pl.pallas_call(
            functools.partial(pack_kernel, groups),
            out_shape=[
                jax.ShapeDtypeStruct((rows + SIDE_ROWS, width), jnp.bfloat16),
                jax.ShapeDtypeStruct((groups + SIDE_ROWS, rows), jnp.bfloat16),
            ],
            in_specs=[pl.BlockSpec(memory_space=pl.ANY)] * 3,
            out_specs=[pl.BlockSpec(memory_space=pltpu.VMEM)] * 2,
            scratch_shapes=[
                pltpu.VMEM((rows, width), jnp.bfloat16),
                pltpu.VMEM((groups, rows), jnp.int32),
                pltpu.VMEM((1, rows), jnp.int32),
                pltpu.SemaphoreType.DMA((3,)),
            ],
            compiler_params=pltpu.CompilerParams(vmem_limit_bytes=PACK_LIMIT),
        )(codes, exponents, clusters)
        blocks = [message]
        for r in range(1, plane):
            relayed = r > 1 and r & 1
            blocks.append(
                lax.ppermute(blocks[r - 1], "blk", near[1]) if relayed
                else lax.ppermute(message, "blk", near[r])
            )
        if plane > 1:
            side, blocks[1] = lax.optimization_barrier((side, blocks[1]))
        sides = tuple(lax.ppermute(side, "blk", pairs) for pairs in far)
        values, lanes, best = call(
            functools.partial(plane_kernel, plane),
            [
                ((plane * rows, width), jnp.bfloat16),
                ((8, plane * rows), jnp.float32),
                ((1, plane * rows), jnp.float32),
            ],
            *blocks,
        )
        return values, sides, lanes, best

    values, far_sides, lanes, best = lax.cond(
        lax.axis_index("blk") >= 0,
        near_phase,
        lambda *operands: jax.tree.map(lambda t: jnp.zeros(t.shape, t.dtype), jax.eval_shape(near_phase, *operands)),
        codes, exponents.T, clusters[None],
    )
    outs = call(
        functools.partial(far_kernel, plane, len(far)),
        [((1, rows), jnp.float32)] * (plane + len(far)),
        *far_codes, *far_sides, values, lanes, best,
    )
    backs, bests = outs[:len(far)], outs[len(far):]

    homes = []
    me = lax.axis_index("blk")
    for pairs, back in reversed(list(zip(far, backs))):
        home = lax.ppermute(back, "blk", [(b, a) for a, b in pairs])
        if len(pairs) < count:
            sent = functools.reduce(jnp.logical_or, [me == a for a, _ in pairs])
            home = jnp.where(sent, home, -1.0)
        homes.append(home)
    for r in range(1, plane):
        homes.append(lax.ppermute(bests[r], "blk", near[r]))
    result = functools.reduce(jnp.maximum, homes, bests[0])
    return result.reshape(rows)


def solution(mesh):
    placed = (P(("parts", "blk"), None), P(("parts", "blk"), None), P(("parts", "blk")))
    return jax.shard_map(
        shards, mesh=mesh, in_specs=placed, out_specs=P(("parts", "blk")), check_vma=False
    )
```

time: 45.4 us -> 40.8 us (0.90)
  waiting for transfers between devices: 22.3 us -> 18 us
  local copies, waits for them, and re-layouts: 2.48 us -> 0 us
  Pallas kernels: 3.4 us -> 4.84 us
  starting transfers between devices: 16.2 us -> 17.1 us
    ppermute x8 -> x10, waiting for transfers between devices: 21.1 us -> 17 us  [the longest x2 12.6 us: near_phase(): lax.ppermute(message, 'blk', near[r])]
    unnamed x6 -> x0, local copies, waits for them, and re-layouts: 2.48 us -> none
    pallas_call x3 -> x2, Pallas kernels: 2.91 us -> 3.64 us  [call(): pl.pallas_call(kernel, out_shape=[jax.ShapeDtypeStruct(shape, dtype) for...]
    pallas_call x1, Pallas kernels: 0.5 us -> 1.2 us  [near_phase(): pl.pallas_call(functools.partial(pack_kernel, groups), out_shape=[jax.Sha...]
    ppermute x8 -> x10, starting transfers between devices: 11.7 us -> 12.3 us  [the longest x2 5.32 us: shards(): far_codes = [lax.ppermute(codes, 'blk', pairs) for pairs in far]]
  transfers between devices with their start and end apart: 10 -> 12, of which waited for: 4 -> 4; matrix products, arithmetic and copies ran while one was open for 0% -> 0% of each run, Pallas kernels for 4% -> 6%
where the time goes in v3:
time: 40.8 us; the launch traced here: 40.5 us
  waiting for transfers between devices  18 us (44%)
  starting transfers between devices  17.1 us (42%)
  Pallas kernels  4.84 us (12%)
  other arithmetic  0.57 us (1%)
    ppermute x2, waiting for transfers between devices, near_phase(): lax.ppermute(message, 'blk', near[r])  12.6 us
    ppermute x2, starting transfers between devices, shards(): far_codes = [lax.ppermute(codes, 'blk', pairs) for pairs in far]  5.32 us
    ppermute x2, starting transfers between devices, shards(): home = lax.ppermute(back, 'blk', [(b, a) for a, b in pairs])  4.82 us
    ppermute x2, waiting for transfers between devices, near_phase(): sides = tuple((lax.ppermute(side, 'blk', pairs) for pairs in far))  4.38 us
    pallas_call x2, Pallas kernels, call(): pl.pallas_call(kernel, out_shape=[jax.ShapeDtypeStruct(shape, dtype) for...  3.64 us
    ppermute x2, starting transfers between devices, near_phase(): sides = tuple((lax.ppermute(side, 'blk', pairs) for pairs in far))  3.51 us
    ppermute x3, starting transfers between devices, shards(): homes.append(lax.ppermute(bests[r], 'blk', near[r]))  1.86 us
    ppermute x2, starting transfers between devices, near_phase(): lax.ppermute(message, 'blk', near[r])  1.56 us
  transfers between devices with their start and end apart: 12, of which 4 were waited for; matrix products, arithmetic and copies ran while one was open for 0% of the time, Pallas kernels for 6%

profile of v3, /device:TPU:0, one launch (start us, length us, event | category | flops | bytes accessed | tf_op | source)
XLA Modules:
  0.0 40.5 jit_solution(15813575624890099754)
XLA Ops:
  0.0 4.0 %collective-permute-start.5 = (bf16[256,1024]{1,0:T(8,128)(2,1)}, bf16[256,1024]{1,0:T(8,128)(2,1)S(1)}, u32[]{:S(2)}, u32[]{:S(2)}) collective-permute-start(bf16[256,1024]{1,0:T(8,128)(2,1)} %param.5), channel_id=1, source_target_pairs={{0,8},{1,9},{2,10},{3,11},{4,12},{5,13},{6,14},{7,15},{8,4},{9,5},... | collective-permute-start | bytes 1572872 | tf_op jit(solution)/shard_map/ppermute | solution.py:184
  4.0 1.3 %collective-permute-start.6 = (bf16[256,1024]{1,0:T(8,128)(2,1)}, bf16[256,1024]{1,0:T(8,128)(2,1)S(1)}, u32[]{:S(2)}, u32[]{:S(2)}) collective-permute-start(bf16[256,1024]{1,0:T(8,128)(2,1)} %param.5), channel_id=1, source_target_pairs={{4,0},{5,1},{6,2},{7,3},{8,12},{9,13},{10,14},{11,15},{20,16},{21,... | collective-permute-start | bytes 1572872 | tf_op jit(solution)/shard_map/ppermute | solution.py:184
  5.3 24.3 %conditional.1 = (bf16[1024,1024]{1,0:T(8,128)(2,1)S(1)}, bf16[48,256]{1,0:T(8,128)(2,1)}, bf16[48,256]{1,0:T(8,128)(2,1)}, f32[8,1024]{1,0:T(8,128)S(1)}, f32[1,1024]{1,0:T(1,128)S(1)}) conditional(s32[]{:T(128)} %convert_element_type.3, () %tuple.14, (bf16[256,1024]{1,0:T(8,128)(2,1)}, s32[32,256]{1,0:T(8,128)}, s32[256]{0:T(256)}) %tuple.18), branch_computations={%region_0.0_spmd, %region_1.0_spmd} | conditional | flops 1 | bytes 6881521 | solution.py:224
  5.3 1.2 %branch_1_fun.2 = (bf16[272,1024]{1,0:T(8,128)(2,1)S(1)}, bf16[48,256]{1,0:T(8,128)(2,1)S(1)}) custom-call(bf16[256,1024]{1,0:T(8,128)(2,1)} %get-tuple-element.11.codes_hbm, s32[32,256]{1,0:T(8,128)} %get-tuple-element.12.exponents_hbm, s32[1,256]{1,0:T(1,128)} %bitcast.4), custom_call_target="tpu_custom_call" | custom-call | tf_op jit(solution)/shard_map/cond/branch_1_fun/pallas_call | solution.py:187
  6.6 1.6 %collective-permute-start.1 = (bf16[272,1024]{1,0:T(8,128)(2,1)S(1)}, bf16[272,1024]{1,0:T(8,128)(2,1)S(1)}, u32[]{:S(2)}, u32[]{:S(2)}) collective-permute-start(bf16[272,1024]{1,0:T(8,128)(2,1)S(1)} %get-tuple-element.14.refs_0_), channel_id=1, source_target_pairs={{0,2},{1,3},{2,0},{3,1},{4,6},{5,7},{6,4},{7,5},{8,10},{9,11},{10,... | collective-permute-start | bytes 1671176 | tf_op jit(solution)/shard_map/cond/branch_1_fun/ppermute | solution.py:208
  8.1 0.0 collective-permute-start
  8.1 12.6 %collective-permute-done.1.refs_2_ = bf16[272,1024]{1,0:T(8,128)(2,1)S(1)} collective-permute-done((bf16[272,1024]{1,0:T(8,128)(2,1)S(1)}, bf16[272,1024]{1,0:T(8,128)(2,1)S(1)}, u32[]{:S(2)}, u32[]{:S(2)}) %collective-permute-start.1) | collective-permute-done | bytes 557088 | tf_op jit(solution)/shard_map/cond/branch_1_fun/ppermute | solution.py:208
  20.7 0.0 collective-permute-start.2
  20.7 0.0 collective-permute-done.refs_1_
  20.7 2.2 %collective-permute-start.3 = (bf16[48,256]{1,0:T(8,128)(2,1)S(1)}, bf16[48,256]{1,0:T(8,128)(2,1)}, u32[]{:S(2)}, u32[]{:S(2)}) collective-permute-start(bf16[48,256]{1,0:T(8,128)(2,1)S(1)} %get-tuple-element.18), channel_id=1, source_target_pairs={{0,8},{1,9},{2,10},{3,11},{4,12},{5,13},{6,14},{7,15},{8,4},{9,5},... | collective-permute-start | bytes 73736 | tf_op jit(solution)/shard_map/cond/branch_1_fun/ppermute | solution.py:212
  22.9 1.3 %collective-permute-start.4 = (bf16[48,256]{1,0:T(8,128)(2,1)S(1)}, bf16[48,256]{1,0:T(8,128)(2,1)}, u32[]{:S(2)}, u32[]{:S(2)}) collective-permute-start(bf16[48,256]{1,0:T(8,128)(2,1)S(1)} %get-tuple-element.18), channel_id=1, source_target_pairs={{4,0},{5,1},{6,2},{7,3},{8,12},{9,13},{10,14},{11,15},{20,16},{21,... | collective-permute-start | bytes 73736 | tf_op jit(solution)/shard_map/cond/branch_1_fun/ppermute | solution.py:212
  24.2 0.0 collective-permute-done.2.refs_3_
  24.2 1.1 %branch_1_fun.3 = (bf16[1024,1024]{1,0:T(8,128)(2,1)S(1)}, f32[8,1024]{1,0:T(8,128)S(1)}, f32[1,1024]{1,0:T(1,128)S(1)}) custom-call(bf16[272,1024]{1,0:T(8,128)(2,1)S(1)} %get-tuple-element.14.refs_0_, bf16[272,1024]{1,0:T(8,128)(2,1)S(1)} %collective-permute-done.refs_1_, bf16[272,1024]{1,0:T(8,128)(2,1)S(1)} %collective-permute-done.1.refs_2_, ...), custom_call_target="tpu_custom_call" | custom-call | flops 1 | bytes 1 | tf_op jit(solution)/shard_map/cond/branch_1_fun/pallas_call | solution.py:142
  25.3 1.2 %collective-permute-done.3 = bf16[48,256]{1,0:T(8,128)(2,1)} collective-permute-done((bf16[48,256]{1,0:T(8,128)(2,1)S(1)}, bf16[48,256]{1,0:T(8,128)(2,1)}, u32[]{:S(2)}, u32[]{:S(2)}) %collective-permute-start.3) | collective-permute-done | bytes 24608 | tf_op jit(solution)/shard_map/cond/branch_1_fun/ppermute | solution.py:212
  26.5 3.2 %collective-permute-done.4 = bf16[48,256]{1,0:T(8,128)(2,1)} collective-permute-done((bf16[48,256]{1,0:T(8,128)(2,1)S(1)}, bf16[48,256]{1,0:T(8,128)(2,1)}, u32[]{:S(2)}, u32[]{:S(2)}) %collective-permute-start.4) | collective-permute-done | bytes 24608 | tf_op jit(solution)/shard_map/cond/branch_1_fun/ppermute | solution.py:212
  29.7 0.0 collective-permute-done.5.refs_0_
  29.7 0.0 collective-permute-done.6.refs_1_
  29.7 2.6 %shard_map.38 = (f32[1,256]{1,0:T(1,128)S(1)}, f32[1,256]{1,0:T(1,128)S(1)}, f32[1,256]{1,0:T(1,128)S(1)}, f32[1,256]{1,0:T(1,128)S(1)}, f32[1,256]{1,0:T(1,128)S(1)}, /*index=5*/f32[1,256]{1,0:T(1,128)S(1)}) custom-call(bf16[256,1024]{1,0:T(8,128)(2,1)S(1)} %collective-permute-done.5.refs_0_, bf16[256,1024]{1,0:T(8,128)(2,1)S(1)} %collective-permute-done.6.refs_1_, ...), custom_call_target="tpu_custom_call" | custom-call | flops 1 | bytes 1 | tf_op jit(solution)/shard_map/pallas_call | solution.py:142
  32.3 1.6 %collective-permute-start.10 = (f32[1,256]{1,0:T(1,128)S(1)}, f32[1,256]{1,0:T(1,128)S(1)}, u32[]{:S(2)}, u32[]{:S(2)}) collective-permute-start(f32[1,256]{1,0:T(1,128)S(1)} %get-tuple-element.41), channel_id=1, source_target_pairs={{0,2},{1,3},{2,0},{3,1},{4,6},{5,7},{6,4},{7,5},{8,10},{9,11},{10,... | collective-permute-start | bytes 3080 | tf_op jit(solution)/shard_map/ppermute | solution.py:246
  33.8 0.0 collective-permute-start.11
  33.8 1.5 %collective-permute-start.7 = (f32[1,256]{1,0:T(1,128)S(1)}, f32[1,256]{1,0:T(1,128)S(1)}, u32[]{:S(2)}, u32[]{:S(2)}) collective-permute-start(f32[1,256]{1,0:T(1,128)S(1)} %get-tuple-element.38), channel_id=1, source_target_pairs={{0,4},{1,5},{2,6},{3,7},{12,8},{13,9},{14,10},{15,11},{16,20},{17,... | collective-permute-start | bytes 3080 | tf_op jit(solution)/shard_map/ppermute | solution.py:240
  35.4 3.3 %collective-permute-start.8 = (f32[1,256]{1,0:T(1,128)S(1)}, f32[1,256]{1,0:T(1,128)S(1)}, u32[]{:S(2)}, u32[]{:S(2)}) collective-permute-start(f32[1,256]{1,0:T(1,128)S(1)} %get-tuple-element.39), channel_id=1, source_target_pairs={{8,0},{9,1},{10,2},{11,3},{12,4},{13,5},{14,6},{15,7},{4,8},{5,9},... | collective-permute-start | bytes 3080 | tf_op jit(solution)/shard_map/ppermute | solution.py:240
  38.7 0.3 collective-permute-start.9
  39.0 0.0 collective-permute-done.10
  39.0 0.0 collective-permute-done.11
  39.0 0.0 collective-permute-done.7
  39.0 1.0 %collective-permute-done.8 = f32[1,256]{1,0:T(1,128)S(1)} collective-permute-done((f32[1,256]{1,0:T(1,128)S(1)}, f32[1,256]{1,0:T(1,128)S(1)}, u32[]{:S(2)}, u32[]{:S(2)}) %collective-permute-start.8) | collective-permute-done | bytes 1056 | tf_op jit(solution)/shard_map/ppermute | solution.py:240
  40.0 0.0 collective-permute-done.9
  40.0 0.6 %maximum_maximum_fusion = f32[1,256]{1,0:T(1,128)} fusion(f32[1,256]{1,0:T(1,128)S(1)} %collective-permute-done.11, f32[1,256]{1,0:T(1,128)S(1)} %collective-permute-done.10, f32[1,256]{1,0:T(1,128)S(1)} %collective-permute-done.9, f32[1,256]{1,0:T(1,128)S(1)} %collective-permute-done.8, f32[1,256]{1,0:T(1,128)S(1)} %get-tuple-element.37, ...), kind=kLoop, calls=%fused_computation.4 | loop fusion | flops 1536 | bytes 7169 | tf_op jit(solution)/shard_map/max | solution.py:247
Async XLA Ops:
  0.0 29.7 %collective-permute-start.5 = (bf16[256,1024]{1,0:T(8,128)(2,1)}, bf16[256,1024]{1,0:T(8,128)(2,1)S(1)}, u32[]{:S(2)}, u32[]{:S(2)}) collective-permute-start(bf16[256,1024]{1,0:T(8,128)(2,1)} %param.5), channel_id=1, source_target_pairs={{0,8},{1,9},{2,10},{3,11},{4,12},{5,13},{6,14},{7,15},{8,4},{9,5},... | collective-permute-start | bytes 1572872 | tf_op jit(solution)/shard_map/ppermute | solution.py:184
  4.0 25.6 %collective-permute-start.6 = (bf16[256,1024]{1,0:T(8,128)(2,1)}, bf16[256,1024]{1,0:T(8,128)(2,1)S(1)}, u32[]{:S(2)}, u32[]{:S(2)}) collective-permute-start(bf16[256,1024]{1,0:T(8,128)(2,1)} %param.5), channel_id=1, source_target_pairs={{4,0},{5,1},{6,2},{7,3},{8,12},{9,13},{10,14},{11,15},{20,16},{21,... | collective-permute-start | bytes 1572872 | tf_op jit(solution)/shard_map/ppermute | solution.py:184
  6.6 14.1 %collective-permute-start.1 = (bf16[272,1024]{1,0:T(8,128)(2,1)S(1)}, bf16[272,1024]{1,0:T(8,128)(2,1)S(1)}, u32[]{:S(2)}, u32[]{:S(2)}) collective-permute-start(bf16[272,1024]{1,0:T(8,128)(2,1)S(1)} %get-tuple-element.14.refs_0_), channel_id=1, source_target_pairs={{0,2},{1,3},{2,0},{3,1},{4,6},{5,7},{6,4},{7,5},{8,10},{9,11},{10,... | collective-permute-start | bytes 1671176 | tf_op jit(solution)/shard_map/cond/branch_1_fun/ppermute | solution.py:208
  8.1 12.6 %collective-permute-start = (bf16[272,1024]{1,0:T(8,128)(2,1)S(1)}, bf16[272,1024]{1,0:T(8,128)(2,1)S(1)}, u32[]{:S(2)}, u32[]{:S(2)}) collective-permute-start(bf16[272,1024]{1,0:T(8,128)(2,1)S(1)} %get-tuple-element.14.refs_0_), channel_id=1, source_target_pairs={{0,1},{1,0},{2,3},{3,2},{4,5},{5,4},{6,7},{7,6},{8,9},{9,8},{10,11... | collective-permute-start | bytes 1671176 | tf_op jit(solution)/shard_map/cond/branch_1_fun/ppermute | solution.py:208
  20.7 3.5 %collective-permute-start.2 = (bf16[272,1024]{1,0:T(8,128)(2,1)S(1)}, bf16[272,1024]{1,0:T(8,128)(2,1)S(1)}, u32[]{:S(2)}, u32[]{:S(2)}) collective-permute-start(bf16[272,1024]{1,0:T(8,128)(2,1)S(1)} %collective-permute-done.1.refs_2_), channel_id=1, source_target_pairs={{0,1},{1,0},{2,3},{3,2},{4,5},{5,4},{6,7},{7,6},{8,9},{9,8},{10,11... | collective-permute-start | bytes 1671176 | tf_op jit(solution)/shard_map/cond/branch_1_fun/ppermute | solution.py:207
  20.7 5.8 %collective-permute-start.3 = (bf16[48,256]{1,0:T(8,128)(2,1)S(1)}, bf16[48,256]{1,0:T(8,128)(2,1)}, u32[]{:S(2)}, u32[]{:S(2)}) collective-permute-start(bf16[48,256]{1,0:T(8,128)(2,1)S(1)} %get-tuple-element.18), channel_id=1, source_target_pairs={{0,8},{1,9},{2,10},{3,11},{4,12},{5,13},{6,14},{7,15},{8,4},{9,5},... | collective-permute-start | bytes 73736 | tf_op jit(solution)/shard_map/cond/branch_1_fun/ppermute | solution.py:212
  22.9 6.7 %collective-permute-start.4 = (bf16[48,256]{1,0:T(8,128)(2,1)S(1)}, bf16[48,256]{1,0:T(8,128)(2,1)}, u32[]{:S(2)}, u32[]{:S(2)}) collective-permute-start(bf16[48,256]{1,0:T(8,128)(2,1)S(1)} %get-tuple-element.18), channel_id=1, source_target_pairs={{4,0},{5,1},{6,2},{7,3},{8,12},{9,13},{10,14},{11,15},{20,16},{21,... | collective-permute-start | bytes 73736 | tf_op jit(solution)/shard_map/cond/branch_1_fun/ppermute | solution.py:212
  32.3 6.7 %collective-permute-start.10 = (f32[1,256]{1,0:T(1,128)S(1)}, f32[1,256]{1,0:T(1,128)S(1)}, u32[]{:S(2)}, u32[]{:S(2)}) collective-permute-start(f32[1,256]{1,0:T(1,128)S(1)} %get-tuple-element.41), channel_id=1, source_target_pairs={{0,2},{1,3},{2,0},{3,1},{4,6},{5,7},{6,4},{7,5},{8,10},{9,11},{10,... | collective-permute-start | bytes 3080 | tf_op jit(solution)/shard_map/ppermute | solution.py:246
  33.8 5.1 %collective-permute-start.11 = (f32[1,256]{1,0:T(1,128)S(1)}, f32[1,256]{1,0:T(1,128)S(1)}, u32[]{:S(2)}, u32[]{:S(2)}) collective-permute-start(f32[1,256]{1,0:T(1,128)S(1)} %get-tuple-element.42), channel_id=1, source_target_pairs={{0,3},{1,2},{2,1},{3,0},{4,7},{5,6},{6,5},{7,4},{8,11},{9,10},{10,... | collective-permute-start | bytes 3080 | tf_op jit(solution)/shard_map/ppermute | solution.py:246
  33.8 5.1 %collective-permute-start.7 = (f32[1,256]{1,0:T(1,128)S(1)}, f32[1,256]{1,0:T(1,128)S(1)}, u32[]{:S(2)}, u32[]{:S(2)}) collective-permute-start(f32[1,256]{1,0:T(1,128)S(1)} %get-tuple-element.38), channel_id=1, source_target_pairs={{0,4},{1,5},{2,6},{3,7},{12,8},{13,9},{14,10},{15,11},{16,20},{17,... | collective-permute-start | bytes 3080 | tf_op jit(solution)/shard_map/ppermute | solution.py:240
  35.4 4.6 %collective-permute-start.8 = (f32[1,256]{1,0:T(1,128)S(1)}, f32[1,256]{1,0:T(1,128)S(1)}, u32[]{:S(2)}, u32[]{:S(2)}) collective-permute-start(f32[1,256]{1,0:T(1,128)S(1)} %get-tuple-element.39), channel_id=1, source_target_pairs={{8,0},{9,1},{10,2},{11,3},{12,4},{13,5},{14,6},{15,7},{4,8},{5,9},... | collective-permute-start | bytes 3080 | tf_op jit(solution)/shard_map/ppermute | solution.py:240
  38.7 1.3 %collective-permute-start.9 = (f32[1,256]{1,0:T(1,128)S(1)}, f32[1,256]{1,0:T(1,128)S(1)}, u32[]{:S(2)}, u32[]{:S(2)}) collective-permute-start(f32[1,256]{1,0:T(1,128)S(1)} %get-tuple-element.40), channel_id=1, source_target_pairs={{0,1},{1,0},{2,3},{3,2},{4,5},{5,4},{6,7},{7,6},{8,9},{9,8},{10,11... | collective-permute-start | bytes 3080 | tf_op jit(solution)/shard_map/ppermute | solution.py:246

commit v4 on v3

--- a/solution.py
+++ b/solution.py
@@ -115,10 +115,11 @@
     code_refs, side_refs = refs[:fars], refs[fars:2 * fars]
     values_ref, lanes_ref, before_ref = refs[2 * fars:2 * fars + 3]
     outs = refs[2 * fars + 3:]
-    back_refs, best_refs = outs[:fars], outs[fars:]
+    returned = max(fars - 1, 0)
+    back_refs, best_refs = outs[:returned], outs[returned:]
     rows = code_refs[0].shape[0]
     bests = [before_ref[0:1, r * rows:(r + 1) * rows] for r in range(planes)]
-    for code_ref, side_ref, back_ref in zip(code_refs, side_refs, back_refs):
+    for i, (code_ref, side_ref) in enumerate(zip(code_refs, side_refs)):
         values, inverse, code = unpack_far(code_ref, side_ref)
         code = expand(code, rows)
         back = jnp.full((rows, 1), -1.0, jnp.float32)
@@ -130,9 +131,11 @@
             )
             same = code == lanes_ref[0:1, at]
             scores = jnp.where(same, dots * inverse * lanes_ref[1:2, at], -1.0)
-            back = jnp.maximum(back, jnp.max(scores, axis=1, keepdims=True))
+            if i < returned:
+                back = jnp.maximum(back, jnp.max(scores, axis=1, keepdims=True))
             bests[r] = jnp.maximum(bests[r], jnp.max(scores, axis=0, keepdims=True))
-        back_ref[...] = flatten(back, rows)
+        if i < returned:
+            back_refs[i][...] = flatten(back, rows)
     for r in range(planes):
         best_refs[r][...] = bests[r]
 
@@ -162,9 +165,9 @@
     rounds = []
     for step in range(2, height, 2):
         top = 1 << (step.bit_length() - 1)
-        rounds.append([(a, a ^ (step + 1) if a & top else a ^ step) for a in range(height)])
+        rounds.append([(a, a ^ step if a & top else a ^ (step + 1)) for a in range(height)])
     if height > 1:
-        rounds.append([(a, a ^ 1) for a in range(height) if (a & 1) != (a >> 1 & 1)])
+        rounds.append([(a, a ^ 1) for a in range(height)])
     return rounds
 
 
@@ -181,6 +184,7 @@
         [(a * plane + p, b * plane + p) for a, b in pairs for p in range(plane)]
         for pairs in far_rounds(height)
     ]
+    backward = [[(b, a) for a, b in pairs] for pairs in far[:-1]]
     far_codes = [lax.ppermute(codes, "blk", pairs) for pairs in far]
 
     def near_phase(codes, exponents, clusters):
@@ -229,21 +233,13 @@
     )
     outs = call(
         functools.partial(far_kernel, plane, len(far)),
-        [((1, rows), jnp.float32)] * (plane + len(far)),
+        [((1, rows), jnp.float32)] * (plane + len(backward)),
         *far_codes, *far_sides, values, lanes, best,
     )
-    backs, bests = outs[:len(far)], outs[len(far):]
-
-    homes = []
-    me = lax.axis_index("blk")
-    for pairs, back in reversed(list(zip(far, backs))):
-        home = lax.ppermute(back, "blk", [(b, a) for a, b in pairs])
-        if len(pairs) < count:
-            sent = functools.reduce(jnp.logical_or, [me == a for a, _ in pairs])
-            home = jnp.where(sent, home, -1.0)
-        homes.append(home)
-    for r in range(1, plane):
-        homes.append(lax.ppermute(bests[r], "blk", near[r]))
+    backs, bests = outs[:len(backward)], outs[len(backward):]
+
+    homes = [lax.ppermute(back, "blk", pairs) for pairs, back in zip(backward, backs)]
+    homes += [lax.ppermute(bests[r], "blk", near[r]) for r in range(1, plane)]
     result = functools.reduce(jnp.maximum, homes, bests[0])
     return result.reshape(rows)
 

time: 40.8 us -> 38.6 us (0.946)
  starting transfers between devices: 17.1 us -> 10.7 us
  waiting for transfers between devices: 18 us -> 22.4 us
    ppermute x5 -> x4, starting transfers between devices: 6.68 us -> 2.29 us  [the longest x3 1.87 us: shards(): homes += [lax.ppermute(bests[r], 'blk', near[r]) for r in range(1, plane)]]
    ppermute x5 -> x4, waiting for transfers between devices: 0.99 us -> 3.21 us  [the longest x1 2.44 us: shards(): lax.ppermute(back, 'blk', pairs)]
    ppermute x2, waiting for transfers between devices: 4.38 us -> 6.42 us  [near_phase(): sides = tuple((lax.ppermute(side, 'blk', pairs) for pairs in far))]
    ppermute x2, starting transfers between devices: 3.51 us -> 1.79 us  [near_phase(): sides = tuple((lax.ppermute(side, 'blk', pairs) for pairs in far))]
  transfers between devices with their start and end apart: 12 -> 11, of which waited for: 4 -> 6; matrix products, arithmetic and copies ran while one was open for 0% -> 0% of each run, Pallas kernels for 6% -> 6%
where the time goes in v4:
time: 38.6 us; the launch traced here: 38.4 us
  waiting for transfers between devices  22.4 us (58%)
  starting transfers between devices  10.7 us (28%)
  Pallas kernels  4.74 us (12%)
  other arithmetic  0.57 us (1%)
    ppermute x2, waiting for transfers between devices, near_phase(): lax.ppermute(message, 'blk', near[r])  12.6 us
    ppermute x2, waiting for transfers between devices, near_phase(): sides = tuple((lax.ppermute(side, 'blk', pairs) for pairs in far))  6.42 us
    ppermute x2, starting transfers between devices, shards(): far_codes = [lax.ppermute(codes, 'blk', pairs) for pairs in far]  5.05 us
    pallas_call x2, Pallas kernels, call(): pl.pallas_call(kernel, out_shape=[jax.ShapeDtypeStruct(shape, dtype) for...  3.51 us
    ppermute x1, waiting for transfers between devices, shards(): lax.ppermute(back, 'blk', pairs)  2.44 us
    ppermute x3, starting transfers between devices, shards(): homes += [lax.ppermute(bests[r], 'blk', near[r]) for r in range(1, plane)]  1.87 us
    ppermute x2, starting transfers between devices, near_phase(): sides = tuple((lax.ppermute(side, 'blk', pairs) for pairs in far))  1.79 us
    ppermute x2, starting transfers between devices, near_phase(): lax.ppermute(message, 'blk', near[r])  1.56 us
  transfers between devices with their start and end apart: 11, of which 6 were waited for; matrix products, arithmetic and copies ran while one was open for 0% of the time, Pallas kernels for 6%

profile of v4, /device:TPU:0, one launch (start us, length us, event | category | flops | bytes accessed | tf_op | source)
XLA Modules:
  0.0 38.4 jit_solution(9640528185667389808)
XLA Ops:
  0.0 5.0 %collective-permute-start.5 = (bf16[256,1024]{1,0:T(8,128)(2,1)}, bf16[256,1024]{1,0:T(8,128)(2,1)S(1)}, u32[]{:S(2)}, u32[]{:S(2)}) collective-permute-start(bf16[256,1024]{1,0:T(8,128)(2,1)} %param.5), channel_id=1, source_target_pairs={{0,12},{1,13},{2,14},{3,15},{4,8},{5,9},{6,10},{7,11},{8,0},{9,1},... | collective-permute-start | bytes 1572872 | tf_op jit(solution)/shard_map/ppermute | solution.py:188
  5.0 0.0 collective-permute-start.6
  5.1 24.8 %conditional.1 = (bf16[1024,1024]{1,0:T(8,128)(2,1)S(1)}, bf16[48,256]{1,0:T(8,128)(2,1)}, bf16[48,256]{1,0:T(8,128)(2,1)}, f32[8,1024]{1,0:T(8,128)S(1)}, f32[1,1024]{1,0:T(1,128)S(1)}) conditional(s32[]{:T(128)} %convert_element_type.3, () %tuple.14, (bf16[256,1024]{1,0:T(8,128)(2,1)}, s32[32,256]{1,0:T(8,128)}, s32[256]{0:T(256)}) %tuple.18), branch_computations={%region_0.0_spmd, %region_1.0_spmd} | conditional | flops 1 | bytes 6881521 | solution.py:228
  5.1 1.2 %branch_1_fun.2 = (bf16[272,1024]{1,0:T(8,128)(2,1)S(1)}, bf16[48,256]{1,0:T(8,128)(2,1)S(1)}) custom-call(bf16[256,1024]{1,0:T(8,128)(2,1)} %get-tuple-element.11.codes_hbm, s32[32,256]{1,0:T(8,128)} %get-tuple-element.12.exponents_hbm, s32[1,256]{1,0:T(1,128)} %bitcast.4), custom_call_target="tpu_custom_call" | custom-call | tf_op jit(solution)/shard_map/cond/branch_1_fun/pallas_call | solution.py:191
  6.3 1.6 %collective-permute-start.1 = (bf16[272,1024]{1,0:T(8,128)(2,1)S(1)}, bf16[272,1024]{1,0:T(8,128)(2,1)S(1)}, u32[]{:S(2)}, u32[]{:S(2)}) collective-permute-start(bf16[272,1024]{1,0:T(8,128)(2,1)S(1)} %get-tuple-element.14.refs_0_), channel_id=1, source_target_pairs={{0,2},{1,3},{2,0},{3,1},{4,6},{5,7},{6,4},{7,5},{8,10},{9,11},{10,... | collective-permute-start | bytes 1671176 | tf_op jit(solution)/shard_map/cond/branch_1_fun/ppermute | solution.py:212
  7.8 0.0 collective-permute-start
  7.8 12.6 %collective-permute-done.1.refs_2_ = bf16[272,1024]{1,0:T(8,128)(2,1)S(1)} collective-permute-done((bf16[272,1024]{1,0:T(8,128)(2,1)S(1)}, bf16[272,1024]{1,0:T(8,128)(2,1)S(1)}, u32[]{:S(2)}, u32[]{:S(2)}) %collective-permute-start.1) | collective-permute-done | bytes 557088 | tf_op jit(solution)/shard_map/cond/branch_1_fun/ppermute | solution.py:212
  20.4 0.0 collective-permute-start.2
  20.4 0.0 collective-permute-done.refs_1_
  20.4 0.4 %collective-permute-start.3 = (bf16[48,256]{1,0:T(8,128)(2,1)S(1)}, bf16[48,256]{1,0:T(8,128)(2,1)}, u32[]{:S(2)}, u32[]{:S(2)}) collective-permute-start(bf16[48,256]{1,0:T(8,128)(2,1)S(1)} %get-tuple-element.18), channel_id=1, source_target_pairs={{0,12},{1,13},{2,14},{3,15},{4,8},{5,9},{6,10},{7,11},{8,0},{9,1},... | collective-permute-start | bytes 73736 | tf_op jit(solution)/shard_map/cond/branch_1_fun/ppermute | solution.py:216
  20.9 1.4 %collective-permute-start.4 = (bf16[48,256]{1,0:T(8,128)(2,1)S(1)}, bf16[48,256]{1,0:T(8,128)(2,1)}, u32[]{:S(2)}, u32[]{:S(2)}) collective-permute-start(bf16[48,256]{1,0:T(8,128)(2,1)S(1)} %get-tuple-element.18), channel_id=1, source_target_pairs={{0,4},{1,5},{2,6},{3,7},{4,0},{5,1},{6,2},{7,3},{8,12},{9,13},{10,... | collective-permute-start | bytes 73736 | tf_op jit(solution)/shard_map/cond/branch_1_fun/ppermute | solution.py:216
  22.2 0.2 collective-permute-done.2.refs_3_
  22.4 1.1 %branch_1_fun.3 = (bf16[1024,1024]{1,0:T(8,128)(2,1)S(1)}, f32[8,1024]{1,0:T(8,128)S(1)}, f32[1,1024]{1,0:T(1,128)S(1)}) custom-call(bf16[272,1024]{1,0:T(8,128)(2,1)S(1)} %get-tuple-element.14.refs_0_, bf16[272,1024]{1,0:T(8,128)(2,1)S(1)} %collective-permute-done.refs_1_, bf16[272,1024]{1,0:T(8,128)(2,1)S(1)} %collective-permute-done.1.refs_2_, ...), custom_call_target="tpu_custom_call" | custom-call | flops 1 | bytes 1 | tf_op jit(solution)/shard_map/cond/branch_1_fun/pallas_call | solution.py:145
  23.4 5.1 %collective-permute-done.3 = bf16[48,256]{1,0:T(8,128)(2,1)} collective-permute-done((bf16[48,256]{1,0:T(8,128)(2,1)S(1)}, bf16[48,256]{1,0:T(8,128)(2,1)}, u32[]{:S(2)}, u32[]{:S(2)}) %collective-permute-start.3) | collective-permute-done | bytes 24608 | tf_op jit(solution)/shard_map/cond/branch_1_fun/ppermute | solution.py:216
  28.5 1.4 %collective-permute-done.4 = bf16[48,256]{1,0:T(8,128)(2,1)} collective-permute-done((bf16[48,256]{1,0:T(8,128)(2,1)S(1)}, bf16[48,256]{1,0:T(8,128)(2,1)}, u32[]{:S(2)}, u32[]{:S(2)}) %collective-permute-start.4) | collective-permute-done | bytes 24608 | tf_op jit(solution)/shard_map/cond/branch_1_fun/ppermute | solution.py:216
  29.9 0.0 collective-permute-done.5.refs_0_
  29.9 0.0 collective-permute-done.6.refs_1_
  29.9 2.5 %shard_map.38 = (f32[1,256]{1,0:T(1,128)S(1)}, f32[1,256]{1,0:T(1,128)S(1)}, f32[1,256]{1,0:T(1,128)S(1)}, f32[1,256]{1,0:T(1,128)S(1)}, f32[1,256]{1,0:T(1,128)S(1)}) custom-call(bf16[256,1024]{1,0:T(8,128)(2,1)S(1)} %collective-permute-done.5.refs_0_, bf16[256,1024]{1,0:T(8,128)(2,1)S(1)} %collective-permute-done.6.refs_1_, ...), custom_call_target="tpu_custom_call" | custom-call | flops 1 | bytes 1 | tf_op jit(solution)/shard_map/pallas_call | solution.py:145
  32.3 0.1 collective-permute-start.10
  32.4 0.4 %collective-permute-start.7 = (f32[1,256]{1,0:T(1,128)S(1)}, f32[1,256]{1,0:T(1,128)S(1)}, u32[]{:S(2)}, u32[]{:S(2)}) collective-permute-start(f32[1,256]{1,0:T(1,128)S(1)} %get-tuple-element.37), channel_id=1, source_target_pairs={{12,0},{13,1},{14,2},{15,3},{8,4},{9,5},{10,6},{11,7},{0,8},{1,9},... | collective-permute-start | bytes 3080 | tf_op jit(solution)/shard_map/ppermute | solution.py:241
  32.8 1.3 %collective-permute-start.8 = (f32[1,256]{1,0:T(1,128)S(1)}, f32[1,256]{1,0:T(1,128)S(1)}, u32[]{:S(2)}, u32[]{:S(2)}) collective-permute-start(f32[1,256]{1,0:T(1,128)S(1)} %get-tuple-element.38), channel_id=1, source_target_pairs={{0,1},{1,0},{2,3},{3,2},{4,5},{5,4},{6,7},{7,6},{8,9},{9,8},{10,11... | collective-permute-start | bytes 3080 | tf_op jit(solution)/shard_map/ppermute | solution.py:242
  34.1 0.5 %collective-permute-start.9 = (f32[1,256]{1,0:T(1,128)S(1)}, f32[1,256]{1,0:T(1,128)S(1)}, u32[]{:S(2)}, u32[]{:S(2)}) collective-permute-start(f32[1,256]{1,0:T(1,128)S(1)} %get-tuple-element.39), channel_id=1, source_target_pairs={{0,2},{1,3},{2,0},{3,1},{4,6},{5,7},{6,4},{7,5},{8,10},{9,11},{10,... | collective-permute-start | bytes 3080 | tf_op jit(solution)/shard_map/ppermute | solution.py:242
  34.6 0.8 %collective-permute-done.10 = f32[1,256]{1,0:T(1,128)S(1)} collective-permute-done((f32[1,256]{1,0:T(1,128)S(1)}, f32[1,256]{1,0:T(1,128)S(1)}, u32[]{:S(2)}, u32[]{:S(2)}) %collective-permute-start.10) | collective-permute-done | bytes 1056 | tf_op jit(solution)/shard_map/ppermute | solution.py:242
  35.4 2.4 %collective-permute-done.7 = f32[1,256]{1,0:T(1,128)S(1)} collective-permute-done((f32[1,256]{1,0:T(1,128)S(1)}, f32[1,256]{1,0:T(1,128)S(1)}, u32[]{:S(2)}, u32[]{:S(2)}) %collective-permute-start.7) | collective-permute-done | bytes 1056 | tf_op jit(solution)/shard_map/ppermute | solution.py:241
  37.8 0.0 collective-permute-done.8
  37.8 0.0 collective-permute-done.9
  37.9 0.6 %maximum_maximum_fusion = f32[1,256]{1,0:T(1,128)} fusion(f32[1,256]{1,0:T(1,128)S(1)} %collective-permute-done.10, f32[1,256]{1,0:T(1,128)S(1)} %collective-permute-done.9, f32[1,256]{1,0:T(1,128)S(1)} %collective-permute-done.8, f32[1,256]{1,0:T(1,128)S(1)} %get-tuple-element.36, f32[1,256]{1,0:T(1,128)S(1)} %collective-permute-done.7), kind=kLoop, calls=%fused_computation | loop fusion | flops 1024 | bytes 6144 | tf_op jit(solution)/shard_map/max | solution.py:243
Async XLA Ops:
  0.0 29.9 %collective-permute-start.5 = (bf16[256,1024]{1,0:T(8,128)(2,1)}, bf16[256,1024]{1,0:T(8,128)(2,1)S(1)}, u32[]{:S(2)}, u32[]{:S(2)}) collective-permute-start(bf16[256,1024]{1,0:T(8,128)(2,1)} %param.5), channel_id=1, source_target_pairs={{0,12},{1,13},{2,14},{3,15},{4,8},{5,9},{6,10},{7,11},{8,0},{9,1},... | collective-permute-start | bytes 1572872 | tf_op jit(solution)/shard_map/ppermute | solution.py:188
  5.0 24.8 %collective-permute-start.6 = (bf16[256,1024]{1,0:T(8,128)(2,1)}, bf16[256,1024]{1,0:T(8,128)(2,1)S(1)}, u32[]{:S(2)}, u32[]{:S(2)}) collective-permute-start(bf16[256,1024]{1,0:T(8,128)(2,1)} %param.5), channel_id=1, source_target_pairs={{0,4},{1,5},{2,6},{3,7},{4,0},{5,1},{6,2},{7,3},{8,12},{9,13},{10,... | collective-permute-start | bytes 1572872 | tf_op jit(solution)/shard_map/ppermute | solution.py:188
  6.3 14.2 %collective-permute-start.1 = (bf16[272,1024]{1,0:T(8,128)(2,1)S(1)}, bf16[272,1024]{1,0:T(8,128)(2,1)S(1)}, u32[]{:S(2)}, u32[]{:S(2)}) collective-permute-start(bf16[272,1024]{1,0:T(8,128)(2,1)S(1)} %get-tuple-element.14.refs_0_), channel_id=1, source_target_pairs={{0,2},{1,3},{2,0},{3,1},{4,6},{5,7},{6,4},{7,5},{8,10},{9,11},{10,... | collective-permute-start | bytes 1671176 | tf_op jit(solution)/shard_map/cond/branch_1_fun/ppermute | solution.py:212
  7.8 12.6 %collective-permute-start = (bf16[272,1024]{1,0:T(8,128)(2,1)S(1)}, bf16[272,1024]{1,0:T(8,128)(2,1)S(1)}, u32[]{:S(2)}, u32[]{:S(2)}) collective-permute-start(bf16[272,1024]{1,0:T(8,128)(2,1)S(1)} %get-tuple-element.14.refs_0_), channel_id=1, source_target_pairs={{0,1},{1,0},{2,3},{3,2},{4,5},{5,4},{6,7},{7,6},{8,9},{9,8},{10,11... | collective-permute-start | bytes 1671176 | tf_op jit(solution)/shard_map/cond/branch_1_fun/ppermute | solution.py:212
  20.4 2.0 %collective-permute-start.2 = (bf16[272,1024]{1,0:T(8,128)(2,1)S(1)}, bf16[272,1024]{1,0:T(8,128)(2,1)S(1)}, u32[]{:S(2)}, u32[]{:S(2)}) collective-permute-start(bf16[272,1024]{1,0:T(8,128)(2,1)S(1)} %collective-permute-done.1.refs_2_), channel_id=1, source_target_pairs={{0,1},{1,0},{2,3},{3,2},{4,5},{5,4},{6,7},{7,6},{8,9},{9,8},{10,11... | collective-permute-start | bytes 1671176 | tf_op jit(solution)/shard_map/cond/branch_1_fun/ppermute | solution.py:211
  20.4 8.1 %collective-permute-start.3 = (bf16[48,256]{1,0:T(8,128)(2,1)S(1)}, bf16[48,256]{1,0:T(8,128)(2,1)}, u32[]{:S(2)}, u32[]{:S(2)}) collective-permute-start(bf16[48,256]{1,0:T(8,128)(2,1)S(1)} %get-tuple-element.18), channel_id=1, source_target_pairs={{0,12},{1,13},{2,14},{3,15},{4,8},{5,9},{6,10},{7,11},{8,0},{9,1},... | collective-permute-start | bytes 73736 | tf_op jit(solution)/shard_map/cond/branch_1_fun/ppermute | solution.py:216
  20.9 9.0 %collective-permute-start.4 = (bf16[48,256]{1,0:T(8,128)(2,1)S(1)}, bf16[48,256]{1,0:T(8,128)(2,1)}, u32[]{:S(2)}, u32[]{:S(2)}) collective-permute-start(bf16[48,256]{1,0:T(8,128)(2,1)S(1)} %get-tuple-element.18), channel_id=1, source_target_pairs={{0,4},{1,5},{2,6},{3,7},{4,0},{5,1},{6,2},{7,3},{8,12},{9,13},{10,... | collective-permute-start | bytes 73736 | tf_op jit(solution)/shard_map/cond/branch_1_fun/ppermute | solution.py:216
  32.3 3.1 %collective-permute-start.10 = (f32[1,256]{1,0:T(1,128)S(1)}, f32[1,256]{1,0:T(1,128)S(1)}, u32[]{:S(2)}, u32[]{:S(2)}) collective-permute-start(f32[1,256]{1,0:T(1,128)S(1)} %get-tuple-element.40), channel_id=1, source_target_pairs={{0,3},{1,2},{2,1},{3,0},{4,7},{5,6},{6,5},{7,4},{8,11},{9,10},{10,... | collective-permute-start | bytes 3080 | tf_op jit(solution)/shard_map/ppermute | solution.py:242
  32.4 5.4 %collective-permute-start.7 = (f32[1,256]{1,0:T(1,128)S(1)}, f32[1,256]{1,0:T(1,128)S(1)}, u32[]{:S(2)}, u32[]{:S(2)}) collective-permute-start(f32[1,256]{1,0:T(1,128)S(1)} %get-tuple-element.37), channel_id=1, source_target_pairs={{12,0},{13,1},{14,2},{15,3},{8,4},{9,5},{10,6},{11,7},{0,8},{1,9},... | collective-permute-start | bytes 3080 | tf_op jit(solution)/shard_map/ppermute | solution.py:241
  32.8 5.0 %collective-permute-start.8 = (f32[1,256]{1,0:T(1,128)S(1)}, f32[1,256]{1,0:T(1,128)S(1)}, u32[]{:S(2)}, u32[]{:S(2)}) collective-permute-start(f32[1,256]{1,0:T(1,128)S(1)} %get-tuple-element.38), channel_id=1, source_target_pairs={{0,1},{1,0},{2,3},{3,2},{4,5},{5,4},{6,7},{7,6},{8,9},{9,8},{10,11... | collective-permute-start | bytes 3080 | tf_op jit(solution)/shard_map/ppermute | solution.py:242
  34.1 3.7 %collective-permute-start.9 = (f32[1,256]{1,0:T(1,128)S(1)}, f32[1,256]{1,0:T(1,128)S(1)}, u32[]{:S(2)}, u32[]{:S(2)}) collective-permute-start(f32[1,256]{1,0:T(1,128)S(1)} %get-tuple-element.39), channel_id=1, source_target_pairs={{0,2},{1,3},{2,0},{3,1},{4,6},{5,7},{6,4},{7,5},{8,10},{9,11},{10,... | collective-permute-start | bytes 3080 | tf_op jit(solution)/shard_map/ppermute | solution.py:242

commit v5 on v4

--- a/solution.py
+++ b/solution.py
@@ -49,16 +49,23 @@
     code = clusters_ref[...] + 1
     row = lax.broadcasted_iota(jnp.int32, (SIDE_ROWS, rows), 0)
     side = jnp.where(row == 0, code >> 8, jnp.where(row == 1, code & 255, 0))
-    side = side.astype(jnp.float32).astype(jnp.bfloat16)
-    message_ref[rows:, 0:rows] = side
+    side = side.astype(jnp.float32)
+    message_ref[rows:, 0:rows] = side.astype(jnp.bfloat16)
     message_ref[rows:, rows:] = jnp.zeros((SIDE_ROWS, width - rows), jnp.bfloat16)
-    side_ref[groups:] = side
     copies[0].wait()
     scale = jnp.exp2(exponents_ref[...].astype(jnp.float32)).astype(jnp.bfloat16)
     side_ref[0:groups] = scale
     scale = spread_scale(scale, width)
     copies[2].wait()
-    message_ref[0:rows] = (codes_ref[...].astype(jnp.float32) * scale).astype(jnp.bfloat16)
+    values = (codes_ref[...].astype(jnp.float32) * scale).astype(jnp.bfloat16)
+    message_ref[0:rows] = values
+    left = flatten(inverse_norm(values), rows)
+    row = lax.broadcasted_iota(jnp.int32, (SIDE_ROWS, rows), 0)
+    for i in range(2, 5):
+        part = left.astype(jnp.bfloat16)
+        left = left - part.astype(jnp.float32)
+        side = jnp.where(row == i, part.astype(jnp.float32), side)
+    side_ref[groups:] = side.astype(jnp.bfloat16)
 
 
 def cluster_code(parts):
@@ -77,11 +84,12 @@
     return values, inverse_norm(values), cluster_code(message_ref[rows:, 0:rows])
 
 
-def unpack_far(codes_ref, side_ref):
-    groups = side_ref.shape[0] - SIDE_ROWS
-    scale = spread_scale(side_ref[0:groups], codes_ref.shape[1])
-    values = (codes_ref[...].astype(jnp.float32) * scale).astype(jnp.bfloat16)
-    return values, inverse_norm(values), cluster_code(side_ref[groups:])
+def spread_kernel(groups, width, side_ref, scale_ref, column_ref):
+    rows = side_ref.shape[1]
+    scale_ref[...] = spread_scale(side_ref[0:groups], width).astype(jnp.bfloat16)
+    parts = side_ref[groups:].astype(jnp.float32)
+    column_ref[:, 0:1] = expand(cluster_code(parts), rows)
+    column_ref[:, 1:2] = expand(parts[2:3] + parts[3:4] + parts[4:5], rows)
 
 
 def plane_kernel(planes, *refs):
@@ -112,17 +120,17 @@
 
 
 def far_kernel(planes, fars, *refs):
-    code_refs, side_refs = refs[:fars], refs[fars:2 * fars]
-    values_ref, lanes_ref, before_ref = refs[2 * fars:2 * fars + 3]
-    outs = refs[2 * fars + 3:]
+    code_refs, scale_refs, column_refs = refs[:fars], refs[fars:2 * fars], refs[2 * fars:3 * fars]
+    values_ref, lanes_ref, before_ref = refs[3 * fars:3 * fars + 3]
+    outs = refs[3 * fars + 3:]
     returned = max(fars - 1, 0)
     back_refs, best_refs = outs[:returned], outs[returned:]
     rows = code_refs[0].shape[0]
     bests = [before_ref[0:1, r * rows:(r + 1) * rows] for r in range(planes)]
-    for i, (code_ref, side_ref) in enumerate(zip(code_refs, side_refs)):
-        values, inverse, code = unpack_far(code_ref, side_ref)
-        code = expand(code, rows)
-        back = jnp.full((rows, 1), -1.0, jnp.float32)
+    for i in range(fars):
+        values = code_refs[i][...] * scale_refs[i][...]
+        code, inverse = column_refs[i][:, 0:1], column_refs[i][:, 1:2]
+        back = jnp.full((rows, rows), -1.0, jnp.float32)
         for r in range(planes):
             at = slice(r * rows, (r + 1) * rows)
             dots = lax.dot_general(
@@ -132,10 +140,10 @@
             same = code == lanes_ref[0:1, at]
             scores = jnp.where(same, dots * inverse * lanes_ref[1:2, at], -1.0)
             if i < returned:
-                back = jnp.maximum(back, jnp.max(scores, axis=1, keepdims=True))
+                back = jnp.maximum(back, scores)
             bests[r] = jnp.maximum(bests[r], jnp.max(scores, axis=0, keepdims=True))
         if i < returned:
-            back_refs[i][...] = flatten(back, rows)
+            back_refs[i][...] = flatten(jnp.max(back, axis=1, keepdims=True), rows)
     for r in range(planes):
         best_refs[r][...] = bests[r]
 
@@ -223,9 +231,22 @@
             ],
             *blocks,
         )
-        return values, sides, lanes, best
-
-    values, far_sides, lanes, best = lax.cond(
+        spreads = []
+        for far_side in sides:
+            if spreads:
+                far_side, spreads[-1] = lax.optimization_barrier((far_side, spreads[-1]))
+            else:
+                far_side, best = lax.optimization_barrier((far_side, best))
+            spreads.append(
+                call(
+                    functools.partial(spread_kernel, groups, width),
+                    [((rows, width), jnp.bfloat16), ((rows, 128), jnp.float32)],
+                    far_side,
+                )
+            )
+        return values, [spread[0] for spread in spreads], [spread[1] for spread in spreads], lanes, best
+
+    values, scales, columns, lanes, best = lax.cond(
         lax.axis_index("blk") >= 0,
         near_phase,
         lambda *operands: jax.tree.map(lambda t: jnp.zeros(t.shape, t.dtype), jax.eval_shape(near_phase, *operands)),
@@ -234,13 +255,16 @@
     outs = call(
         functools.partial(far_kernel, plane, len(far)),
         [((1, rows), jnp.float32)] * (plane + len(backward)),
-        *far_codes, *far_sides, values, lanes, best,
+        *far_codes, *scales, *columns, values, lanes, best,
     )
     backs, bests = outs[:len(backward)], outs[len(backward):]
 
-    homes = [lax.ppermute(back, "blk", pairs) for pairs, back in zip(backward, backs)]
-    homes += [lax.ppermute(bests[r], "blk", near[r]) for r in range(1, plane)]
-    result = functools.reduce(jnp.maximum, homes, bests[0])
+    homes = [
+        lax.ppermute(bests[r], "blk", near[r]) for r in [*range(2, plane), *range(1, min(plane, 2))]
+    ]
+    homes.append(bests[0])
+    homes += [lax.ppermute(back, "blk", pairs) for pairs, back in zip(backward, backs)]
+    result = functools.reduce(jnp.maximum, homes)
     return result.reshape(rows)
 
 

time: 38.6 us -> 37.8 us (0.979)
  waiting for transfers between devices: 22.4 us -> 21.5 us
    ppermute x3, waiting for transfers between devices: 0.77 us -> 0.01 us  [shards(): lax.ppermute(bests[r], 'blk', near[r])]
    ppermute x2, waiting for transfers between devices: 6.42 us -> 5.87 us  [near_phase(): sides = tuple((lax.ppermute(side, 'blk', pairs) for pairs in far))]
    ppermute x1, waiting for transfers between devices: 2.44 us -> 2.86 us  [shards(): lax.ppermute(back, 'blk', pairs)]
    pallas_call x2 -> x4, Pallas kernels: 3.51 us -> 3.14 us  [call(): pl.pallas_call(kernel, out_shape=[jax.ShapeDtypeStruct(shape, dtype) for...]
  transfers between devices with their start and end apart: 11 -> 11, of which waited for: 6 -> 5; matrix products, arithmetic and copies ran while one was open for 0% -> 0% of each run, Pallas kernels for 6% -> 8%
where the time goes in v5:
time: 37.8 us; the launch traced here: 37.6 us
  waiting for transfers between devices  21.5 us (57%)
  starting transfers between devices  11 us (29%)
  Pallas kernels  4.52 us (12%)
  other arithmetic  0.57 us (2%)
    ppermute x2, waiting for transfers between devices, near_phase(): lax.ppermute(message, 'blk', near[r])  12.6 us
    ppermute x2, waiting for transfers between devices, near_phase(): sides = tuple((lax.ppermute(side, 'blk', pairs) for pairs in far))  5.87 us
    ppermute x2, starting transfers between devices, shards(): far_codes = [lax.ppermute(codes, 'blk', pairs) for pairs in far]  5.05 us
    pallas_call x4, Pallas kernels, call(): pl.pallas_call(kernel, out_shape=[jax.ShapeDtypeStruct(shape, dtype) for...  3.14 us
    ppermute x1, waiting for transfers between devices, shards(): lax.ppermute(back, 'blk', pairs)  2.86 us
    ppermute x3, starting transfers between devices, shards(): lax.ppermute(bests[r], 'blk', near[r])  2.14 us
    ppermute x2, starting transfers between devices, near_phase(): sides = tuple((lax.ppermute(side, 'blk', pairs) for pairs in far))  1.79 us
    ppermute x2, starting transfers between devices, near_phase(): lax.ppermute(message, 'blk', near[r])  1.56 us
  transfers between devices with their start and end apart: 11, of which 5 were waited for; matrix products, arithmetic and copies ran while one was open for 0% of the time, Pallas kernels for 8%

profile of v5, /device:TPU:0, one launch (start us, length us, event | category | flops | bytes accessed | tf_op | source)
XLA Modules:
  0.0 37.6 jit_solution(16012983725270416083)
XLA Ops:
  0.0 5.0 %collective-permute-start.5 = (bf16[256,1024]{1,0:T(8,128)(2,1)}, bf16[256,1024]{1,0:T(8,128)(2,1)S(1)}, u32[]{:S(2)}, u32[]{:S(2)}) collective-permute-start(bf16[256,1024]{1,0:T(8,128)(2,1)} %param.5), channel_id=1, source_target_pairs={{0,12},{1,13},{2,14},{3,15},{4,8},{5,9},{6,10},{7,11},{8,0},{9,1},... | collective-permute-start | bytes 1572872 | tf_op jit(solution)/shard_map/ppermute | solution.py:196
  5.0 0.0 collective-permute-start.6
  5.1 25.0 %conditional.1 = (bf16[1024,1024]{1,0:T(8,128)(2,1)S(1)}, bf16[256,1024]{1,0:T(8,128)(2,1)S(1)}, bf16[256,1024]{1,0:T(8,128)(2,1)S(1)}, f32[256,128]{1,0:T(8,128...) conditional(s32[]{:T(128)} %convert_element_type.3, () %tuple.16, ...), branch_computations={%region_0.0_spmd, %region_1.0_spmd} | conditional | flops 3 | bytes 6881539 | solution.py:249
  5.1 1.4 %branch_1_fun.4 = (bf16[272,1024]{1,0:T(8,128)(2,1)S(1)}, bf16[48,256]{1,0:T(8,128)(2,1)S(1)}) custom-call(bf16[256,1024]{1,0:T(8,128)(2,1)} %get-tuple-element.11.codes_hbm, s32[32,256]{1,0:T(8,128)} %get-tuple-element.12.exponents_hbm, s32[1,256]{1,0:T(1,128)} %bitcast.4), custom_call_target="tpu_custom_call" | custom-call | tf_op jit(solution)/shard_map/cond/branch_1_fun/pallas_call | solution.py:199
  6.4 1.6 %collective-permute-start.1 = (bf16[272,1024]{1,0:T(8,128)(2,1)S(1)}, bf16[272,1024]{1,0:T(8,128)(2,1)S(1)}, u32[]{:S(2)}, u32[]{:S(2)}) collective-permute-start(bf16[272,1024]{1,0:T(8,128)(2,1)S(1)} %get-tuple-element.14.refs_0_), channel_id=1, source_target_pairs={{0,2},{1,3},{2,0},{3,1},{4,6},{5,7},{6,4},{7,5},{8,10},{9,11},{10,... | collective-permute-start | bytes 1671176 | tf_op jit(solution)/shard_map/cond/branch_1_fun/ppermute | solution.py:220
  8.0 0.0 collective-permute-start
  8.0 12.6 %collective-permute-done.1.refs_2_ = bf16[272,1024]{1,0:T(8,128)(2,1)S(1)} collective-permute-done((bf16[272,1024]{1,0:T(8,128)(2,1)S(1)}, bf16[272,1024]{1,0:T(8,128)(2,1)S(1)}, u32[]{:S(2)}, u32[]{:S(2)}) %collective-permute-start.1) | collective-permute-done | bytes 557088 | tf_op jit(solution)/shard_map/cond/branch_1_fun/ppermute | solution.py:220
  20.6 0.0 collective-permute-start.2
  20.6 0.0 collective-permute-done.refs_1_
  20.6 0.4 %collective-permute-start.4 = (bf16[48,256]{1,0:T(8,128)(2,1)S(1)}, bf16[48,256]{1,0:T(8,128)(2,1)S(1)}, u32[]{:S(2)}, u32[]{:S(2)}) collective-permute-start(bf16[48,256]{1,0:T(8,128)(2,1)S(1)} %get-tuple-element.18), channel_id=1, source_target_pairs={{0,12},{1,13},{2,14},{3,15},{4,8},{5,9},{6,10},{7,11},{8,0},{9,1},... | collective-permute-start | bytes 73736 | tf_op jit(solution)/shard_map/cond/branch_1_fun/ppermute | solution.py:224
  21.0 1.4 %collective-permute-start.3 = (bf16[48,256]{1,0:T(8,128)(2,1)S(1)}, bf16[48,256]{1,0:T(8,128)(2,1)S(1)}, u32[]{:S(2)}, u32[]{:S(2)}) collective-permute-start(bf16[48,256]{1,0:T(8,128)(2,1)S(1)} %get-tuple-element.18), channel_id=1, source_target_pairs={{0,4},{1,5},{2,6},{3,7},{4,0},{5,1},{6,2},{7,3},{8,12},{9,13},{10,... | collective-permute-start | bytes 73736 | tf_op jit(solution)/shard_map/cond/branch_1_fun/ppermute | solution.py:224
  22.4 0.2 collective-permute-done.2.refs_3_
  22.6 1.0 %branch_1_fun.5 = (bf16[1024,1024]{1,0:T(8,128)(2,1)S(1)}, f32[8,1024]{1,0:T(8,128)S(1)}, f32[1,1024]{1,0:T(1,128)S(1)}) custom-call(bf16[272,1024]{1,0:T(8,128)(2,1)S(1)} %get-tuple-element.14.refs_0_, bf16[272,1024]{1,0:T(8,128)(2,1)S(1)} %collective-permute-done.refs_1_, bf16[272,1024]{1,0:T(8,128)(2,1)S(1)} %collective-permute-done.1.refs_2_, ...), custom_call_target="tpu_custom_call" | custom-call | flops 1 | bytes 1 | tf_op jit(solution)/shard_map/cond/branch_1_fun/pallas_call | solution.py:153
  23.6 4.9 %collective-permute-done.4.side_ref = bf16[48,256]{1,0:T(8,128)(2,1)S(1)} collective-permute-done((bf16[48,256]{1,0:T(8,128)(2,1)S(1)}, bf16[48,256]{1,0:T(8,128)(2,1)S(1)}, u32[]{:S(2)}, u32[]{:S(2)}) %collective-permute-start.4) | collective-permute-done | bytes 24608 | tf_op jit(solution)/shard_map/cond/branch_1_fun/ppermute | solution.py:224
  28.5 0.3 branch_1_fun.6
  28.8 0.9 %collective-permute-done.3.side_ref = bf16[48,256]{1,0:T(8,128)(2,1)S(1)} collective-permute-done((bf16[48,256]{1,0:T(8,128)(2,1)S(1)}, bf16[48,256]{1,0:T(8,128)(2,1)S(1)}, u32[]{:S(2)}, u32[]{:S(2)}) %collective-permute-start.3) | collective-permute-done | bytes 24608 | tf_op jit(solution)/shard_map/cond/branch_1_fun/ppermute | solution.py:224
  29.8 0.3 branch_1_fun.7
  30.1 0.0 collective-permute-done.5.refs_0_
  30.1 0.0 collective-permute-done.6.refs_1_
  30.1 1.5 %shard_map.38 = (f32[1,256]{1,0:T(1,128)S(1)}, f32[1,256]{1,0:T(1,128)S(1)}, f32[1,256]{1,0:T(1,128)S(1)}, f32[1,256]{1,0:T(1,128)S(1)}, f32[1,256]{1,0:T(1,128)S(1)}) custom-call(bf16[256,1024]{1,0:T(8,128)(2,1)S(1)} %collective-permute-done.5.refs_0_, bf16[256,1024]{1,0:T(8,128)(2,1)S(1)} %collective-permute-done.6.refs_1_, ...), custom_call_target="tpu_custom_call" | custom-call | flops 1 | bytes 1 | tf_op jit(solution)/shard_map/pallas_call | solution.py:153
  31.6 0.4 %collective-permute-start.10 = (f32[1,256]{1,0:T(1,128)S(1)}, f32[1,256]{1,0:T(1,128)S(1)}, u32[]{:S(2)}, u32[]{:S(2)}) collective-permute-start(f32[1,256]{1,0:T(1,128)S(1)} %get-tuple-element.53), channel_id=1, source_target_pairs={{12,0},{13,1},{14,2},{15,3},{8,4},{9,5},{10,6},{11,7},{0,8},{1,9},... | collective-permute-start | bytes 3080 | tf_op jit(solution)/shard_map/ppermute | solution.py:266
  32.0 1.5 %collective-permute-start.7 = (f32[1,256]{1,0:T(1,128)S(1)}, f32[1,256]{1,0:T(1,128)S(1)}, u32[]{:S(2)}, u32[]{:S(2)}) collective-permute-start(f32[1,256]{1,0:T(1,128)S(1)} %get-tuple-element.49), channel_id=1, source_target_pairs={{0,2},{1,3},{2,0},{3,1},{4,6},{5,7},{6,4},{7,5},{8,10},{9,11},{10,... | collective-permute-start | bytes 3080 | tf_op jit(solution)/shard_map/ppermute | solution.py:263
  33.5 0.0 collective-permute-start.8
  33.5 0.6 %collective-permute-start.9 = (f32[1,256]{1,0:T(1,128)S(1)}, f32[1,256]{1,0:T(1,128)S(1)}, u32[]{:S(2)}, u32[]{:S(2)}) collective-permute-start(f32[1,256]{1,0:T(1,128)S(1)} %get-tuple-element.51), channel_id=1, source_target_pairs={{0,1},{1,0},{2,3},{3,2},{4,5},{5,4},{6,7},{7,6},{8,9},{9,8},{10,11... | collective-permute-start | bytes 3080 | tf_op jit(solution)/shard_map/ppermute | solution.py:263
  34.2 2.9 %collective-permute-done.10 = f32[1,256]{1,0:T(1,128)S(1)} collective-permute-done((f32[1,256]{1,0:T(1,128)S(1)}, f32[1,256]{1,0:T(1,128)S(1)}, u32[]{:S(2)}, u32[]{:S(2)}) %collective-permute-start.10) | collective-permute-done | bytes 1056 | tf_op jit(solution)/shard_map/ppermute | solution.py:266
  37.0 0.0 collective-permute-done.7
  37.0 0.0 collective-permute-done.8
  37.0 0.0 collective-permute-done.9
  37.0 0.6 %maximum_maximum_fusion = f32[1,256]{1,0:T(1,128)} fusion(f32[1,256]{1,0:T(1,128)S(1)} %collective-permute-done.10, f32[1,256]{1,0:T(1,128)S(1)} %get-tuple-element.52, f32[1,256]{1,0:T(1,128)S(1)} %collective-permute-done.9, f32[1,256]{1,0:T(1,128)S(1)} %collective-permute-done.7, f32[1,256]{1,0:T(1,128)S(1)} %collective-permute-done.8), kind=kLoop, calls=%fused_computation | loop fusion | flops 1024 | bytes 6144 | tf_op jit(solution)/shard_map/max | solution.py:267
Async XLA Ops:
  0.0 30.1 %collective-permute-start.5 = (bf16[256,1024]{1,0:T(8,128)(2,1)}, bf16[256,1024]{1,0:T(8,128)(2,1)S(1)}, u32[]{:S(2)}, u32[]{:S(2)}) collective-permute-start(bf16[256,1024]{1,0:T(8,128)(2,1)} %param.5), channel_id=1, source_target_pairs={{0,12},{1,13},{2,14},{3,15},{4,8},{5,9},{6,10},{7,11},{8,0},{9,1},... | collective-permute-start | bytes 1572872 | tf_op jit(solution)/shard_map/ppermute | solution.py:196
  5.0 25.1 %collective-permute-start.6 = (bf16[256,1024]{1,0:T(8,128)(2,1)}, bf16[256,1024]{1,0:T(8,128)(2,1)S(1)}, u32[]{:S(2)}, u32[]{:S(2)}) collective-permute-start(bf16[256,1024]{1,0:T(8,128)(2,1)} %param.5), channel_id=1, source_target_pairs={{0,4},{1,5},{2,6},{3,7},{4,0},{5,1},{6,2},{7,3},{8,12},{9,13},{10,... | collective-permute-start | bytes 1572872 | tf_op jit(solution)/shard_map/ppermute | solution.py:196
  6.4 14.2 %collective-permute-start.1 = (bf16[272,1024]{1,0:T(8,128)(2,1)S(1)}, bf16[272,1024]{1,0:T(8,128)(2,1)S(1)}, u32[]{:S(2)}, u32[]{:S(2)}) collective-permute-start(bf16[272,1024]{1,0:T(8,128)(2,1)S(1)} %get-tuple-element.14.refs_0_), channel_id=1, source_target_pairs={{0,2},{1,3},{2,0},{3,1},{4,6},{5,7},{6,4},{7,5},{8,10},{9,11},{10,... | collective-permute-start | bytes 1671176 | tf_op jit(solution)/shard_map/cond/branch_1_fun/ppermute | solution.py:220
  8.0 12.6 %collective-permute-start = (bf16[272,1024]{1,0:T(8,128)(2,1)S(1)}, bf16[272,1024]{1,0:T(8,128)(2,1)S(1)}, u32[]{:S(2)}, u32[]{:S(2)}) collective-permute-start(bf16[272,1024]{1,0:T(8,128)(2,1)S(1)} %get-tuple-element.14.refs_0_), channel_id=1, source_target_pairs={{0,1},{1,0},{2,3},{3,2},{4,5},{5,4},{6,7},{7,6},{8,9},{9,8},{10,11... | collective-permute-start | bytes 1671176 | tf_op jit(solution)/shard_map/cond/branch_1_fun/ppermute | solution.py:220
  20.6 2.0 %collective-permute-start.2 = (bf16[272,1024]{1,0:T(8,128)(2,1)S(1)}, bf16[272,1024]{1,0:T(8,128)(2,1)S(1)}, u32[]{:S(2)}, u32[]{:S(2)}) collective-permute-start(bf16[272,1024]{1,0:T(8,128)(2,1)S(1)} %collective-permute-done.1.refs_2_), channel_id=1, source_target_pairs={{0,1},{1,0},{2,3},{3,2},{4,5},{5,4},{6,7},{7,6},{8,9},{9,8},{10,11... | collective-permute-start | bytes 1671176 | tf_op jit(solution)/shard_map/cond/branch_1_fun/ppermute | solution.py:219
  20.6 7.9 %collective-permute-start.4 = (bf16[48,256]{1,0:T(8,128)(2,1)S(1)}, bf16[48,256]{1,0:T(8,128)(2,1)S(1)}, u32[]{:S(2)}, u32[]{:S(2)}) collective-permute-start(bf16[48,256]{1,0:T(8,128)(2,1)S(1)} %get-tuple-element.18), channel_id=1, source_target_pairs={{0,12},{1,13},{2,14},{3,15},{4,8},{5,9},{6,10},{7,11},{8,0},{9,1},... | collective-permute-start | bytes 73736 | tf_op jit(solution)/shard_map/cond/branch_1_fun/ppermute | solution.py:224
  21.0 8.7 %collective-permute-start.3 = (bf16[48,256]{1,0:T(8,128)(2,1)S(1)}, bf16[48,256]{1,0:T(8,128)(2,1)S(1)}, u32[]{:S(2)}, u32[]{:S(2)}) collective-permute-start(bf16[48,256]{1,0:T(8,128)(2,1)S(1)} %get-tuple-element.18), channel_id=1, source_target_pairs={{0,4},{1,5},{2,6},{3,7},{4,0},{5,1},{6,2},{7,3},{8,12},{9,13},{10,... | collective-permute-start | bytes 73736 | tf_op jit(solution)/shard_map/cond/branch_1_fun/ppermute | solution.py:224
  31.6 5.4 %collective-permute-start.10 = (f32[1,256]{1,0:T(1,128)S(1)}, f32[1,256]{1,0:T(1,128)S(1)}, u32[]{:S(2)}, u32[]{:S(2)}) collective-permute-start(f32[1,256]{1,0:T(1,128)S(1)} %get-tuple-element.53), channel_id=1, source_target_pairs={{12,0},{13,1},{14,2},{15,3},{8,4},{9,5},{10,6},{11,7},{0,8},{1,9},... | collective-permute-start | bytes 3080 | tf_op jit(solution)/shard_map/ppermute | solution.py:266
  32.0 5.0 %collective-permute-start.7 = (f32[1,256]{1,0:T(1,128)S(1)}, f32[1,256]{1,0:T(1,128)S(1)}, u32[]{:S(2)}, u32[]{:S(2)}) collective-permute-start(f32[1,256]{1,0:T(1,128)S(1)} %get-tuple-element.49), channel_id=1, source_target_pairs={{0,2},{1,3},{2,0},{3,1},{4,6},{5,7},{6,4},{7,5},{8,10},{9,11},{10,... | collective-permute-start | bytes 3080 | tf_op jit(solution)/shard_map/ppermute | solution.py:263
  33.5 3.5 %collective-permute-start.8 = (f32[1,256]{1,0:T(1,128)S(1)}, f32[1,256]{1,0:T(1,128)S(1)}, u32[]{:S(2)}, u32[]{:S(2)}) collective-permute-start(f32[1,256]{1,0:T(1,128)S(1)} %get-tuple-element.50), channel_id=1, source_target_pairs={{0,3},{1,2},{2,1},{3,0},{4,7},{5,6},{6,5},{7,4},{8,11},{9,10},{10,... | collective-permute-start | bytes 3080 | tf_op jit(solution)/shard_map/ppermute | solution.py:263
  33.5 3.5 %collective-permute-start.9 = (f32[1,256]{1,0:T(1,128)S(1)}, f32[1,256]{1,0:T(1,128)S(1)}, u32[]{:S(2)}, u32[]{:S(2)}) collective-permute-start(f32[1,256]{1,0:T(1,128)S(1)} %get-tuple-element.51), channel_id=1, source_target_pairs={{0,1},{1,0},{2,3},{3,2},{4,5},{5,4},{6,7},{7,6},{8,9},{9,8},{10,11... | collective-permute-start | bytes 3080 | tf_op jit(solution)/shard_map/ppermute | solution.py:263

commit v6 on v5

--- a/solution.py
+++ b/solution.py
@@ -119,11 +119,26 @@
     best_ref[0:1, 0:rows] = best
 
 
+def swap_kernel(planes, code_ref, scale_ref, column_ref, values_ref, lanes_ref, before_ref, best_ref):
+    rows = code_ref.shape[0]
+    values = code_ref[...] * scale_ref[...]
+    code, inverse = column_ref[:, 0:1], column_ref[:, 1:2]
+    for r in range(planes):
+        at = slice(r * rows, (r + 1) * rows)
+        dots = lax.dot_general(
+            values, values_ref[at], (((1,), (1,)), ((), ())),
+            preferred_element_type=jnp.float32,
+        )
+        same = code == lanes_ref[0:1, at]
+        scores = jnp.where(same, dots * inverse * lanes_ref[1:2, at], -1.0)
+        best_ref[0:1, at] = jnp.maximum(before_ref[0:1, at], jnp.max(scores, axis=0, keepdims=True))
+
+
 def far_kernel(planes, fars, *refs):
     code_refs, scale_refs, column_refs = refs[:fars], refs[fars:2 * fars], refs[2 * fars:3 * fars]
     values_ref, lanes_ref, before_ref = refs[3 * fars:3 * fars + 3]
     outs = refs[3 * fars + 3:]
-    returned = max(fars - 1, 0)
+    returned = fars
     back_refs, best_refs = outs[:returned], outs[returned:]
     rows = code_refs[0].shape[0]
     bests = [before_ref[0:1, r * rows:(r + 1) * rows] for r in range(planes)]
@@ -139,13 +154,15 @@
             )
             same = code == lanes_ref[0:1, at]
             scores = jnp.where(same, dots * inverse * lanes_ref[1:2, at], -1.0)
-            if i < returned:
-                back = jnp.maximum(back, scores)
+            back = jnp.maximum(back, scores)
             bests[r] = jnp.maximum(bests[r], jnp.max(scores, axis=0, keepdims=True))
-        if i < returned:
-            back_refs[i][...] = flatten(jnp.max(back, axis=1, keepdims=True), rows)
+        back_refs[i][...] = flatten(jnp.max(back, axis=1, keepdims=True), rows)
+    cross_refs, even_refs = best_refs[:1], best_refs[min(planes - 1, 1):]
     for r in range(planes):
-        best_refs[r][...] = bests[r]
+        if r % 2 == 0:
+            even_refs[r // 2][...] = bests[r]
+        else:
+            cross_refs[0][r // 2:r // 2 + 1] = bests[r]
 
 
 def call(kernel, shapes, *operands):
@@ -175,7 +192,7 @@
         top = 1 << (step.bit_length() - 1)
         rounds.append([(a, a ^ step if a & top else a ^ (step + 1)) for a in range(height)])
     if height > 1:
-        rounds.append([(a, a ^ 1) for a in range(height)])
+        rounds.insert(0, [(a, a ^ 1) for a in range(height)])
     return rounds
 
 
@@ -192,26 +209,28 @@
         [(a * plane + p, b * plane + p) for a, b in pairs for p in range(plane)]
         for pairs in far_rounds(height)
     ]
-    backward = [[(b, a) for a, b in pairs] for pairs in far[:-1]]
+    backward = [[(b, a) for a, b in pairs] for pairs in far[1:]]
     far_codes = [lax.ppermute(codes, "blk", pairs) for pairs in far]
 
-    def near_phase(codes, exponents, clusters):
-        message, side = pl.pallas_call(
-            functools.partial(pack_kernel, groups),
-            out_shape=[
-                jax.ShapeDtypeStruct((rows + SIDE_ROWS, width), jnp.bfloat16),
-                jax.ShapeDtypeStruct((groups + SIDE_ROWS, rows), jnp.bfloat16),
-            ],
-            in_specs=[pl.BlockSpec(memory_space=pl.ANY)] * 3,
-            out_specs=[pl.BlockSpec(memory_space=pltpu.VMEM)] * 2,
-            scratch_shapes=[
-                pltpu.VMEM((rows, width), jnp.bfloat16),
-                pltpu.VMEM((groups, rows), jnp.int32),
-                pltpu.VMEM((1, rows), jnp.int32),
-                pltpu.SemaphoreType.DMA((3,)),
-            ],
-            compiler_params=pltpu.CompilerParams(vmem_limit_bytes=PACK_LIMIT),
-        )(codes, exponents, clusters)
+    message, side = pl.pallas_call(
+        functools.partial(pack_kernel, groups),
+        out_shape=[
+            jax.ShapeDtypeStruct((rows + SIDE_ROWS, width), jnp.bfloat16),
+            jax.ShapeDtypeStruct((groups + SIDE_ROWS, rows), jnp.bfloat16),
+        ],
+        in_specs=[pl.BlockSpec(memory_space=pl.ANY)] * 3,
+        out_specs=[pl.BlockSpec(memory_space=pltpu.VMEM)] * 2,
+        scratch_shapes=[
+            pltpu.VMEM((rows, width), jnp.bfloat16),
+            pltpu.VMEM((groups, rows), jnp.int32),
+            pltpu.VMEM((1, rows), jnp.int32),
+            pltpu.SemaphoreType.DMA((3,)),
+        ],
+        compiler_params=pltpu.CompilerParams(vmem_limit_bytes=PACK_LIMIT),
+    )(codes, exponents.T, clusters[None])
+    far_sides = [lax.ppermute(side, "blk", pairs) for pairs in far[1:]]
+
+    def near_phase(message, side):
         blocks = [message]
         for r in range(1, plane):
             relayed = r > 1 and r & 1
@@ -221,7 +240,7 @@
             )
         if plane > 1:
             side, blocks[1] = lax.optimization_barrier((side, blocks[1]))
-        sides = tuple(lax.ppermute(side, "blk", pairs) for pairs in far)
+        sides = tuple(lax.ppermute(side, "blk", pairs) for pairs in far[:1])
         values, lanes, best = call(
             functools.partial(plane_kernel, plane),
             [
@@ -250,20 +269,40 @@
         lax.axis_index("blk") >= 0,
         near_phase,
         lambda *operands: jax.tree.map(lambda t: jnp.zeros(t.shape, t.dtype), jax.eval_shape(near_phase, *operands)),
-        codes, exponents.T, clusters[None],
+        message, side,
     )
+    for block in zip(far_codes, scales, columns):
+        (best,) = call(
+            functools.partial(swap_kernel, plane),
+            [((1, plane * rows), jnp.float32)],
+            *block, values, lanes, best,
+        )
+    spreads = []
+    for far_side in far_sides:
+        far_side, best = lax.optimization_barrier((far_side, best))
+        spreads.append(
+            call(
+                functools.partial(spread_kernel, groups, width),
+                [((rows, width), jnp.bfloat16), ((rows, 128), jnp.float32)],
+                far_side,
+            )
+        )
+    halves = plane // 2
     outs = call(
-        functools.partial(far_kernel, plane, len(far)),
-        [((1, rows), jnp.float32)] * (plane + len(backward)),
-        *far_codes, *scales, *columns, values, lanes, best,
+        functools.partial(far_kernel, plane, len(backward)),
+        [((1, rows), jnp.float32)] * len(backward)
+        + [((halves, rows), jnp.float32)] * min(halves, 1)
+        + [((1, rows), jnp.float32)] * (plane - halves),
+        *far_codes[1:], *[spread[0] for spread in spreads], *[spread[1] for spread in spreads],
+        values, lanes, best,
     )
     backs, bests = outs[:len(backward)], outs[len(backward):]
 
-    homes = [
-        lax.ppermute(bests[r], "blk", near[r]) for r in [*range(2, plane), *range(1, min(plane, 2))]
-    ]
-    homes.append(bests[0])
-    homes += [lax.ppermute(back, "blk", pairs) for pairs, back in zip(backward, backs)]
+    if halves:
+        crossed = lax.ppermute(bests[0], "blk", near[1])
+        bests = [jnp.maximum(own, crossed[i:i + 1]) for i, own in enumerate(bests[1:])]
+    homes = [lax.ppermute(bests[i], "blk", near[2 * i]) for i in range(1, len(bests))]
+    homes = [lax.ppermute(back, "blk", pairs) for pairs, back in zip(backward, backs)] + homes + [bests[0]]
     result = functools.reduce(jnp.maximum, homes)
     return result.reshape(rows)
 

time: 37.8 us -> 37.5 us (level)
  waiting for transfers between devices: 21.5 us -> 16.9 us
  local copies, waits for them, and re-layouts: 0 us -> 2.51 us
  Pallas kernels: 4.52 us -> 5.85 us
    ppermute x5 -> x4, waiting for transfers between devices: 5.88 us -> 1.11 us  [the longest x1 1.1 us: shards(): far_sides = [lax.ppermute(side, 'blk', pairs) for pairs in far[1:]]]
    unnamed x0 -> x6, local copies, waits for them, and re-layouts: none -> 2.51 us
    ppermute x5 -> x4, starting transfers between devices: 3.93 us -> 2.33 us  [the longest x1 1.49 us: shards(): lax.ppermute(bests[i], 'blk', near[2 * i])]
    pallas_call x4 -> x5, Pallas kernels: 3.14 us -> 4.48 us  [call(): pl.pallas_call(kernel, out_shape=[jax.ShapeDtypeStruct(shape, dtype) for...]
    ppermute x1, starting transfers between devices: 0.42 us -> 1.69 us  [shards(): lax.ppermute(back, 'blk', pairs)]
    ppermute x1, waiting for transfers between devices: 0.16 us -> 1.27 us  [near_phase(): lax.ppermute(blocks[r - 1], 'blk', near[1])]
    ppermute x1, waiting for transfers between devices: 2.86 us -> 2.23 us  [shards(): lax.ppermute(back, 'blk', pairs)]
    ppermute x2, starting transfers between devices: 5.05 us -> 5.5 us  [shards(): far_codes = [lax.ppermute(codes, 'blk', pairs) for pairs in far]]
  transfers between devices with their start and end apart: 11 -> 10, of which waited for: 5 -> 4; matrix products, arithmetic and copies ran while one was open for 0% -> 0% of each run, Pallas kernels for 8% -> 13%
where the time goes in v6:
time: 37.5 us; the launch traced here: 37.2 us
  waiting for transfers between devices  16.9 us (45%)
  starting transfers between devices  11.3 us (30%)
  Pallas kernels  5.85 us (16%)
  local copies, waits for them, and re-layouts  2.51 us (7%)
  other arithmetic  0.57 us (2%)
    ppermute x2, waiting for transfers between devices, near_phase(): lax.ppermute(message, 'blk', near[r])  12.3 us
    ppermute x2, starting transfers between devices, shards(): far_codes = [lax.ppermute(codes, 'blk', pairs) for pairs in far]  5.5 us
    pallas_call x5, Pallas kernels, call(): pl.pallas_call(kernel, out_shape=[jax.ShapeDtypeStruct(shape, dtype) for...  4.48 us
    unnamed x6, local copies, waits for them, and re-layouts  2.51 us
    ppermute x1, waiting for transfers between devices, shards(): lax.ppermute(back, 'blk', pairs)  2.23 us
    ppermute x2, starting transfers between devices, near_phase(): lax.ppermute(message, 'blk', near[r])  1.79 us
    ppermute x1, starting transfers between devices, shards(): lax.ppermute(back, 'blk', pairs)  1.69 us
    ppermute x1, starting transfers between devices, shards(): lax.ppermute(bests[i], 'blk', near[2 * i])  1.49 us
  transfers between devices with their start and end apart: 10, of which 4 were waited for; matrix products, arithmetic and copies ran while one was open for 0% of the time, Pallas kernels for 13%

profile of v6, /device:TPU:0, one launch (start us, length us, event | category | flops | bytes accessed | tf_op | source)
XLA Modules:
  0.0 37.2 jit_solution(10226099731721989783)
XLA Ops:
  0.0 3.0 %collective-permute-start.6 = (bf16[256,1024]{1,0:T(8,128)(2,1)}, bf16[256,1024]{1,0:T(8,128)(2,1)S(1)}, u32[]{:S(2)}, u32[]{:S(2)}) collective-permute-start(bf16[256,1024]{1,0:T(8,128)(2,1)} %codes_hbm.1), channel_id=1, source_target_pairs={{0,4},{1,5},{2,6},{3,7},{4,0},{5,1},{6,2},{7,3},{8,12},{9,13},{10,... | collective-permute-start | bytes 1572872 | tf_op jit(solution)/shard_map/ppermute | solution.py:213
  3.0 2.5 %collective-permute-start.4 = (bf16[256,1024]{1,0:T(8,128)(2,1)}, bf16[256,1024]{1,0:T(8,128)(2,1)S(1)}, u32[]{:S(2)}, u32[]{:S(2)}) collective-permute-start(bf16[256,1024]{1,0:T(8,128)(2,1)} %codes_hbm.1), channel_id=1, source_target_pairs={{0,12},{1,13},{2,14},{3,15},{4,8},{5,9},{6,10},{7,11},{8,0},{9,1},... | collective-permute-start | bytes 1572872 | tf_op jit(solution)/shard_map/ppermute | solution.py:213
  5.5 0.0 copy-start
  5.5 1.1 %copy-done = bf16[256,1024]{1,0:T(8,128)(2,1)S(1)} copy-done((bf16[256,1024]{1,0:T(8,128)(2,1)S(1)}, bf16[256,1024]{1,0:T(8,128)(2,1)}, u32[]{:S(2)}) %copy-start) | copy-done | bytes 524312
  6.6 0.8 %copy-done.1 = s32[256,32]{0,1:T(8,128)S(1)} copy-done((s32[256,32]{0,1:T(8,128)S(1)}, s32[256,32]{0,1:T(8,128)}, u32[]{:S(2)}) %copy-start.1) | copy-done | bytes 32792
  7.3 0.7 %copy-done.2 = s32[256]{0:T(256)S(1)} copy-done((s32[256]{0:T(256)S(1)}, s32[256]{0:T(256)}, u32[]{:S(2)}) %copy-start.2) | copy-done | bytes 1048
  8.0 1.4 %shard_map.37 = (bf16[272,1024]{1,0:T(8,128)(2,1)}, bf16[48,256]{1,0:T(8,128)(2,1)}) custom-call(bf16[256,1024]{1,0:T(8,128)(2,1)S(1)} %copy-done, s32[32,256]{1,0:T(8,128)S(1)} %bitcast.3, s32[1,256]{1,0:T(1,128)S(1)} %bitcast.4), custom_call_target="tpu_custom_call" | custom-call | tf_op jit(solution)/shard_map/pallas_call | solution.py:215
  9.4 0.1 collective-permute-start.5
  9.5 18.5 %conditional.1 = (bf16[1024,1024]{1,0:T(8,128)(2,1)S(1)}, bf16[256,1024]{1,0:T(8,128)(2,1)S(1)}, f32[256,128]{1,0:T(8,128)S(1)}, f32[8,1024]{1,0:T(8,128)S(1)}, f32[1,1024]{1,0:T(1,128)S(1)}) conditional(s32[]{:T(128)} %convert_element_type.3, () %tuple.15, (bf16[272,1024]{1,0:T(8,128)(2,1)}, bf16[48,256]{1,0:T(8,128)(2,1)}) %shard_map.37), branch_computations={%region_0.0_spmd, %region_1.0_spmd} | conditional | flops 2 | bytes 6783178 | solution.py:268
  9.5 1.8 %collective-permute-start.1 = (bf16[272,1024]{1,0:T(8,128)(2,1)}, bf16[272,1024]{1,0:T(8,128)(2,1)S(1)}, u32[]{:S(2)}, u32[]{:S(2)}) collective-permute-start(bf16[272,1024]{1,0:T(8,128)(2,1)} %get-tuple-element.9.refs_0_), channel_id=1, source_target_pairs={{0,2},{1,3},{2,0},{3,1},{4,6},{5,7},{6,4},{7,5},{8,10},{9,11},{10,... | collective-permute-start | bytes 1671176 | tf_op jit(solution)/shard_map/cond/branch_1_fun/ppermute | solution.py:239
  11.3 0.0 collective-permute-start
  11.3 12.3 %collective-permute-done.1.refs_2_ = bf16[272,1024]{1,0:T(8,128)(2,1)S(1)} collective-permute-done((bf16[272,1024]{1,0:T(8,128)(2,1)}, bf16[272,1024]{1,0:T(8,128)(2,1)S(1)}, u32[]{:S(2)}, u32[]{:S(2)}) %collective-permute-start.1) | collective-permute-done | bytes 557088 | tf_op jit(solution)/shard_map/cond/branch_1_fun/ppermute | solution.py:239
  23.5 0.0 collective-permute-start.2
  23.5 0.0 collective-permute-done.refs_1_
  23.6 0.7 %collective-permute-start.3 = (bf16[48,256]{1,0:T(8,128)(2,1)}, bf16[48,256]{1,0:T(8,128)(2,1)S(1)}, u32[]{:S(2)}, u32[]{:S(2)}) collective-permute-start(bf16[48,256]{1,0:T(8,128)(2,1)} %get-tuple-element.13), channel_id=1, source_target_pairs={{0,4},{1,5},{2,6},{3,7},{4,0},{5,1},{6,2},{7,3},{8,12},{9,13},{10,... | collective-permute-start | bytes 73736 | tf_op jit(solution)/shard_map/cond/branch_1_fun/ppermute | solution.py:243
  24.2 1.3 %collective-permute-done.2.refs_3_ = bf16[272,1024]{1,0:T(8,128)(2,1)S(1)} collective-permute-done((bf16[272,1024]{1,0:T(8,128)(2,1)S(1)}, bf16[272,1024]{1,0:T(8,128)(2,1)S(1)}, u32[]{:S(2)}, u32[]{:S(2)}) %collective-permute-start.2) | collective-permute-done | bytes 557088 | tf_op jit(solution)/shard_map/cond/branch_1_fun/ppermute | solution.py:238
  25.5 2.1 %branch_1_fun.2 = (bf16[1024,1024]{1,0:T(8,128)(2,1)S(1)}, f32[8,1024]{1,0:T(8,128)S(1)}, f32[1,1024]{1,0:T(1,128)S(1)}) custom-call(bf16[272,1024]{1,0:T(8,128)(2,1)} %get-tuple-element.9.refs_0_, bf16[272,1024]{1,0:T(8,128)(2,1)S(1)} %collective-permute-done.refs_1_, bf16[272,1024]{1,0:T(8,128)(2,1)S(1)} %collective-permute-done.1.refs_2_, ...), custom_call_target="tpu_custom_call" | custom-call | flops 1 | bytes 1 | tf_op jit(solution)/shard_map/cond/branch_1_fun/pallas_call | solution.py:170
  27.6 0.0 collective-permute-done.3.side_ref
  27.6 0.3 branch_1_fun.3
  27.9 0.0 collective-permute-done.6.code_ref
  28.0 0.8 %shard_map.38.refs_5_ = f32[1,1024]{1,0:T(1,128)S(1)} custom-call(bf16[256,1024]{1,0:T(8,128)(2,1)S(1)} %collective-permute-done.6.code_ref, bf16[256,1024]{1,0:T(8,128)(2,1)S(1)} %get-tuple-element.35.scale_ref, f32[256,128]{1,0:T(8,128)S(1)} %get-tuple-element.36.column_ref, bf16[1024,1024]{1,0:T(8,128)(2,1)S(1)} %get-tuple-element.37.values_ref.refs_3_, ...), custom_call_target="tpu_custom_call" | custom-call | flops 1 | bytes 1 | tf_op jit(solution)/shard_map/pallas_call | solution.py:170
  28.8 1.1 %collective-permute-done.5.side_ref = bf16[48,256]{1,0:T(8,128)(2,1)S(1)} collective-permute-done((bf16[48,256]{1,0:T(8,128)(2,1)}, bf16[48,256]{1,0:T(8,128)(2,1)S(1)}, u32[]{:S(2)}, u32[]{:S(2)}) %collective-permute-start.5) | collective-permute-done | bytes 24608 | tf_op jit(solution)/shard_map/ppermute | solution.py:231
  29.9 0.3 shard_map.39
  30.2 0.0 collective-permute-done.4.refs_0_
  30.2 0.9 %shard_map.40 = (f32[1,256]{1,0:T(1,128)S(1)}, f32[2,256]{1,0:T(2,128)S(1)}, f32[1,256]{1,0:T(1,128)S(1)}, f32[1,256]{1,0:T(1,128)S(1)}) custom-call(bf16[256,1024]{1,0:T(8,128)(2,1)S(1)} %collective-permute-done.4.refs_0_, bf16[256,1024]{1,0:T(8,128)(2,1)S(1)} %get-tuple-element.41.refs_1_, f32[256,128]{1,0:T(8,128)S(1)} %get-tuple-element.42.refs_2_, ...), custom_call_target="tpu_custom_call" | custom-call | flops 1 | bytes 1 | tf_op jit(solution)/shard_map/pallas_call | solution.py:170
  31.1 0.1 collective-permute-start.8
  31.2 1.7 %collective-permute-start.7 = (f32[1,256]{1,0:T(1,128)S(1)}, f32[1,256]{1,0:T(1,128)S(1)}, u32[]{:S(2)}, u32[]{:S(2)}) collective-permute-start(f32[1,256]{1,0:T(1,128)S(1)} %get-tuple-element.44), channel_id=1, source_target_pairs={{12,0},{13,1},{14,2},{15,3},{8,4},{9,5},{10,6},{11,7},{0,8},{1,9},... | collective-permute-start | bytes 3080 | tf_op jit(solution)/shard_map/ppermute | solution.py:305
  32.9 0.0 collective-permute-done.8
  32.9 1.5 %collective-permute-start.9 = (f32[1,256]{1,0:T(1,128)S(1)}, f32[1,256]{1,0:T(1,128)S(1)}, u32[]{:S(2)}, u32[]{:S(2)}) collective-permute-start(f32[1,256]{1,0:T(1,128)S(1)} %slice_maximum_fusion.1), channel_id=1, source_target_pairs={{0,2},{1,3},{2,0},{3,1},{4,6},{5,7},{6,4},{7,5},{8,10},{9,11},{10,... | collective-permute-start | bytes 3080 | tf_op jit(solution)/shard_map/ppermute | solution.py:304
  34.4 2.2 %collective-permute-done.7 = f32[1,256]{1,0:T(1,128)S(1)} collective-permute-done((f32[1,256]{1,0:T(1,128)S(1)}, f32[1,256]{1,0:T(1,128)S(1)}, u32[]{:S(2)}, u32[]{:S(2)}) %collective-permute-start.7) | collective-permute-done | bytes 1056 | tf_op jit(solution)/shard_map/ppermute | solution.py:305
  36.6 0.0 collective-permute-done.9
  36.6 0.6 %fusion = f32[1,256]{1,0:T(1,128)} fusion(f32[1,256]{1,0:T(1,128)S(1)} %get-tuple-element.47, f32[2,256]{1,0:T(2,128)S(1)} %collective-permute-done.8, f32[1,256]{1,0:T(1,128)S(1)} %collective-permute-done.7, f32[1,256]{1,0:T(1,128)S(1)} %collective-permute-done.9), kind=kLoop, calls=%fused_computation.1 | loop fusion | flops 768 | bytes 5120 | tf_op jit(solution)/shard_map/max | solution.py:306
  (3 shorter events, 0.0 us)
Async XLA Ops:
  0.0 27.9 %collective-permute-start.6 = (bf16[256,1024]{1,0:T(8,128)(2,1)}, bf16[256,1024]{1,0:T(8,128)(2,1)S(1)}, u32[]{:S(2)}, u32[]{:S(2)}) collective-permute-start(bf16[256,1024]{1,0:T(8,128)(2,1)} %codes_hbm.1), channel_id=1, source_target_pairs={{0,4},{1,5},{2,6},{3,7},{4,0},{5,1},{6,2},{7,3},{8,12},{9,13},{10,... | collective-permute-start | bytes 1572872 | tf_op jit(solution)/shard_map/ppermute | solution.py:213
  3.0 27.2 %collective-permute-start.4 = (bf16[256,1024]{1,0:T(8,128)(2,1)}, bf16[256,1024]{1,0:T(8,128)(2,1)S(1)}, u32[]{:S(2)}, u32[]{:S(2)}) collective-permute-start(bf16[256,1024]{1,0:T(8,128)(2,1)} %codes_hbm.1), channel_id=1, source_target_pairs={{0,12},{1,13},{2,14},{3,15},{4,8},{5,9},{6,10},{7,11},{8,0},{9,1},... | collective-permute-start | bytes 1572872 | tf_op jit(solution)/shard_map/ppermute | solution.py:213
  5.5 1.1 %copy-start = (bf16[256,1024]{1,0:T(8,128)(2,1)S(1)}, bf16[256,1024]{1,0:T(8,128)(2,1)}, u32[]{:S(2)}) copy-start(bf16[256,1024]{1,0:T(8,128)(2,1)} %codes_hbm.1) | copy-start | bytes 1572868
  6.6 0.8 %copy-start.1 = (s32[256,32]{0,1:T(8,128)S(1)}, s32[256,32]{0,1:T(8,128)}, u32[]{:S(2)}) copy-start(s32[256,32]{0,1:T(8,128)} %param.6) | copy-start | bytes 98308
  7.3 0.7 %copy-start.2 = (s32[256]{0:T(256)S(1)}, s32[256]{0:T(256)}, u32[]{:S(2)}) copy-start(s32[256]{0:T(256)} %param.7) | copy-start | bytes 3076
  9.4 20.5 %collective-permute-start.5 = (bf16[48,256]{1,0:T(8,128)(2,1)}, bf16[48,256]{1,0:T(8,128)(2,1)S(1)}, u32[]{:S(2)}, u32[]{:S(2)}) collective-permute-start(bf16[48,256]{1,0:T(8,128)(2,1)} %get-tuple-element.34), channel_id=1, source_target_pairs={{0,12},{1,13},{2,14},{3,15},{4,8},{5,9},{6,10},{7,11},{8,0},{9,1},... | collective-permute-start | bytes 73736 | tf_op jit(solution)/shard_map/ppermute | solution.py:231
  9.5 14.1 %collective-permute-start.1 = (bf16[272,1024]{1,0:T(8,128)(2,1)}, bf16[272,1024]{1,0:T(8,128)(2,1)S(1)}, u32[]{:S(2)}, u32[]{:S(2)}) collective-permute-start(bf16[272,1024]{1,0:T(8,128)(2,1)} %get-tuple-element.9.refs_0_), channel_id=1, source_target_pairs={{0,2},{1,3},{2,0},{3,1},{4,6},{5,7},{6,4},{7,5},{8,10},{9,11},{10,... | collective-permute-start | bytes 1671176 | tf_op jit(solution)/shard_map/cond/branch_1_fun/ppermute | solution.py:239
  11.3 12.3 %collective-permute-start = (bf16[272,1024]{1,0:T(8,128)(2,1)}, bf16[272,1024]{1,0:T(8,128)(2,1)S(1)}, u32[]{:S(2)}, u32[]{:S(2)}) collective-permute-start(bf16[272,1024]{1,0:T(8,128)(2,1)} %get-tuple-element.9.refs_0_), channel_id=1, source_target_pairs={{0,1},{1,0},{2,3},{3,2},{4,5},{5,4},{6,7},{7,6},{8,9},{9,8},{10,11... | collective-permute-start | bytes 1671176 | tf_op jit(solution)/shard_map/cond/branch_1_fun/ppermute | solution.py:239
  23.5 2.0 %collective-permute-start.2 = (bf16[272,1024]{1,0:T(8,128)(2,1)S(1)}, bf16[272,1024]{1,0:T(8,128)(2,1)S(1)}, u32[]{:S(2)}, u32[]{:S(2)}) collective-permute-start(bf16[272,1024]{1,0:T(8,128)(2,1)S(1)} %collective-permute-done.1.refs_2_), channel_id=1, source_target_pairs={{0,1},{1,0},{2,3},{3,2},{4,5},{5,4},{6,7},{7,6},{8,9},{9,8},{10,11... | collective-permute-start | bytes 1671176 | tf_op jit(solution)/shard_map/cond/branch_1_fun/ppermute | solution.py:238
  23.6 4.1 %collective-permute-start.3 = (bf16[48,256]{1,0:T(8,128)(2,1)}, bf16[48,256]{1,0:T(8,128)(2,1)S(1)}, u32[]{:S(2)}, u32[]{:S(2)}) collective-permute-start(bf16[48,256]{1,0:T(8,128)(2,1)} %get-tuple-element.13), channel_id=1, source_target_pairs={{0,4},{1,5},{2,6},{3,7},{4,0},{5,1},{6,2},{7,3},{8,12},{9,13},{10,... | collective-permute-start | bytes 73736 | tf_op jit(solution)/shard_map/cond/branch_1_fun/ppermute | solution.py:243
  31.1 1.8 %collective-permute-start.8 = (f32[2,256]{1,0:T(2,128)S(1)}, f32[2,256]{1,0:T(2,128)S(1)}, u32[]{:S(2)}, u32[]{:S(2)}) collective-permute-start(f32[2,256]{1,0:T(2,128)S(1)} %get-tuple-element.46), channel_id=1, source_target_pairs={{0,1},{1,0},{2,3},{3,2},{4,5},{5,4},{6,7},{7,6},{8,9},{9,8},{10,11... | collective-permute-start | bytes 6152 | tf_op jit(solution)/shard_map/ppermute | solution.py:302
  31.2 5.4 %collective-permute-start.7 = (f32[1,256]{1,0:T(1,128)S(1)}, f32[1,256]{1,0:T(1,128)S(1)}, u32[]{:S(2)}, u32[]{:S(2)}) collective-permute-start(f32[1,256]{1,0:T(1,128)S(1)} %get-tuple-element.44), channel_id=1, source_target_pairs={{12,0},{13,1},{14,2},{15,3},{8,4},{9,5},{10,6},{11,7},{0,8},{1,9},... | collective-permute-start | bytes 3080 | tf_op jit(solution)/shard_map/ppermute | solution.py:305
  32.9 3.7 %collective-permute-start.9 = (f32[1,256]{1,0:T(1,128)S(1)}, f32[1,256]{1,0:T(1,128)S(1)}, u32[]{:S(2)}, u32[]{:S(2)}) collective-permute-start(f32[1,256]{1,0:T(1,128)S(1)} %slice_maximum_fusion.1), channel_id=1, source_target_pairs={{0,2},{1,3},{2,0},{3,1},{4,6},{5,7},{6,4},{7,5},{8,10},{9,11},{10,... | collective-permute-start | bytes 3080 | tf_op jit(solution)/shard_map/ppermute | solution.py:304

commit v7 on v6

--- a/solution.py
+++ b/solution.py
@@ -135,16 +135,20 @@
 
 
 def far_kernel(planes, fars, *refs):
-    code_refs, scale_refs, column_refs = refs[:fars], refs[fars:2 * fars], refs[2 * fars:3 * fars]
-    values_ref, lanes_ref, before_ref = refs[3 * fars:3 * fars + 3]
-    outs = refs[3 * fars + 3:]
+    code_refs, side_refs = refs[:fars], refs[fars:2 * fars]
+    values_ref, lanes_ref, before_ref = refs[2 * fars:2 * fars + 3]
+    outs = refs[2 * fars + 3:]
+    groups = side_refs[0].shape[0] - SIDE_ROWS if fars else 0
     returned = fars
     back_refs, best_refs = outs[:returned], outs[returned:]
     rows = code_refs[0].shape[0]
     bests = [before_ref[0:1, r * rows:(r + 1) * rows] for r in range(planes)]
     for i in range(fars):
-        values = code_refs[i][...] * scale_refs[i][...]
-        code, inverse = column_refs[i][:, 0:1], column_refs[i][:, 1:2]
+        scale = spread_scale(side_refs[i][0:groups], code_refs[i].shape[1])
+        values = code_refs[i][...] * scale.astype(jnp.bfloat16)
+        parts = side_refs[i][groups:].astype(jnp.float32)
+        code = expand(cluster_code(parts), rows)
+        inverse = expand(parts[2:3] + parts[3:4] + parts[4:5], rows)
         back = jnp.full((rows, rows), -1.0, jnp.float32)
         for r in range(planes):
             at = slice(r * rows, (r + 1) * rows)
@@ -277,24 +281,15 @@
             [((1, plane * rows), jnp.float32)],
             *block, values, lanes, best,
         )
-    spreads = []
-    for far_side in far_sides:
-        far_side, best = lax.optimization_barrier((far_side, best))
-        spreads.append(
-            call(
-                functools.partial(spread_kernel, groups, width),
-                [((rows, width), jnp.bfloat16), ((rows, 128), jnp.float32)],
-                far_side,
-            )
-        )
+    if far_sides:
+        *far_sides, best = lax.optimization_barrier((*far_sides, best))
     halves = plane // 2
     outs = call(
         functools.partial(far_kernel, plane, len(backward)),
         [((1, rows), jnp.float32)] * len(backward)
         + [((halves, rows), jnp.float32)] * min(halves, 1)
         + [((1, rows), jnp.float32)] * (plane - halves),
-        *far_codes[1:], *[spread[0] for spread in spreads], *[spread[1] for spread in spreads],
-        values, lanes, best,
+        *far_codes[1:], *far_sides, values, lanes, best,
     )
     backs, bests = outs[:len(backward)], outs[len(backward):]
 

time: 37.5 us -> 37.3 us (level)
    pallas_call x5 -> x4, Pallas kernels: 4.48 us -> 4.3 us  [call(): pl.pallas_call(kernel, out_shape=[jax.ShapeDtypeStruct(shape, dtype) for...]
  transfers between devices with their start and end apart: 10 -> 10, of which waited for: 4 -> 4; matrix products, arithmetic and copies ran while one was open for 0% -> 0% of each run, Pallas kernels for 13% -> 12%
where the time goes in v7:
time: 37.3 us; the launch traced here: 37 us
  waiting for transfers between devices  16.9 us (45%)
  starting transfers between devices  11.3 us (30%)
  Pallas kernels  5.66 us (15%)
  local copies, waits for them, and re-layouts  2.51 us (7%)
  other arithmetic  0.57 us (2%)
    ppermute x2, waiting for transfers between devices, near_phase(): lax.ppermute(message, 'blk', near[r])  12.3 us
    ppermute x2, starting transfers between devices, shards(): far_codes = [lax.ppermute(codes, 'blk', pairs) for pairs in far]  5.5 us
    pallas_call x4, Pallas kernels, call(): pl.pallas_call(kernel, out_shape=[jax.ShapeDtypeStruct(shape, dtype) for...  4.3 us
    unnamed x6, local copies, waits for them, and re-layouts  2.51 us
    ppermute x1, waiting for transfers between devices, shards(): lax.ppermute(back, 'blk', pairs)  2.24 us
    ppermute x2, starting transfers between devices, near_phase(): lax.ppermute(message, 'blk', near[r])  1.79 us
    ppermute x1, starting transfers between devices, shards(): lax.ppermute(back, 'blk', pairs)  1.67 us
    ppermute x1, starting transfers between devices, shards(): lax.ppermute(bests[i], 'blk', near[2 * i])  1.5 us
  transfers between devices with their start and end apart: 10, of which 4 were waited for; matrix products, arithmetic and copies ran while one was open for 0% of the time, Pallas kernels for 12%

profile of v7, /device:TPU:0, one launch (start us, length us, event | category | flops | bytes accessed | tf_op | source)
XLA Modules:
  0.0 37.0 jit_solution(10407355645333358764)
XLA Ops:
  0.0 3.0 %collective-permute-start.6 = (bf16[256,1024]{1,0:T(8,128)(2,1)}, bf16[256,1024]{1,0:T(8,128)(2,1)S(1)}, u32[]{:S(2)}, u32[]{:S(2)}) collective-permute-start(bf16[256,1024]{1,0:T(8,128)(2,1)} %codes_hbm.1), channel_id=1, source_target_pairs={{0,4},{1,5},{2,6},{3,7},{4,0},{5,1},{6,2},{7,3},{8,12},{9,13},{10,... | collective-permute-start | bytes 1572872 | tf_op jit(solution)/shard_map/ppermute | solution.py:217
  3.0 2.5 %collective-permute-start.4 = (bf16[256,1024]{1,0:T(8,128)(2,1)}, bf16[256,1024]{1,0:T(8,128)(2,1)S(1)}, u32[]{:S(2)}, u32[]{:S(2)}) collective-permute-start(bf16[256,1024]{1,0:T(8,128)(2,1)} %codes_hbm.1), channel_id=1, source_target_pairs={{0,12},{1,13},{2,14},{3,15},{4,8},{5,9},{6,10},{7,11},{8,0},{9,1},... | collective-permute-start | bytes 1572872 | tf_op jit(solution)/shard_map/ppermute | solution.py:217
  5.5 0.0 copy-start
  5.5 1.1 %copy-done = bf16[256,1024]{1,0:T(8,128)(2,1)S(1)} copy-done((bf16[256,1024]{1,0:T(8,128)(2,1)S(1)}, bf16[256,1024]{1,0:T(8,128)(2,1)}, u32[]{:S(2)}) %copy-start) | copy-done | bytes 524312
  6.6 0.0 copy-start.1
  6.6 0.8 %copy-done.1 = s32[256,32]{0,1:T(8,128)S(1)} copy-done((s32[256,32]{0,1:T(8,128)S(1)}, s32[256,32]{0,1:T(8,128)}, u32[]{:S(2)}) %copy-start.1) | copy-done | bytes 32792
  7.3 0.7 %copy-done.2 = s32[256]{0:T(256)S(1)} copy-done((s32[256]{0:T(256)S(1)}, s32[256]{0:T(256)}, u32[]{:S(2)}) %copy-start.2) | copy-done | bytes 1048
  8.0 1.4 %shard_map.37 = (bf16[272,1024]{1,0:T(8,128)(2,1)}, bf16[48,256]{1,0:T(8,128)(2,1)}) custom-call(bf16[256,1024]{1,0:T(8,128)(2,1)S(1)} %copy-done, s32[32,256]{1,0:T(8,128)S(1)} %bitcast.3, s32[1,256]{1,0:T(1,128)S(1)} %bitcast.4), custom_call_target="tpu_custom_call" | custom-call | tf_op jit(solution)/shard_map/pallas_call | solution.py:219
  9.4 0.1 collective-permute-start.5
  9.5 18.5 %conditional.1 = (bf16[1024,1024]{1,0:T(8,128)(2,1)S(1)}, bf16[256,1024]{1,0:T(8,128)(2,1)S(1)}, f32[256,128]{1,0:T(8,128)S(1)}, f32[8,1024]{1,0:T(8,128)S(1)}, f32[1,1024]{1,0:T(1,128)S(1)}) conditional(s32[]{:T(128)} %convert_element_type.3, () %tuple.15, (bf16[272,1024]{1,0:T(8,128)(2,1)}, bf16[48,256]{1,0:T(8,128)(2,1)}) %shard_map.37), branch_computations={%region_0.0_spmd, %region_1.0_spmd} | conditional | flops 2 | bytes 6783178 | solution.py:272
  9.5 1.8 %collective-permute-start.1 = (bf16[272,1024]{1,0:T(8,128)(2,1)}, bf16[272,1024]{1,0:T(8,128)(2,1)S(1)}, u32[]{:S(2)}, u32[]{:S(2)}) collective-permute-start(bf16[272,1024]{1,0:T(8,128)(2,1)} %get-tuple-element.9.refs_0_), channel_id=1, source_target_pairs={{0,2},{1,3},{2,0},{3,1},{4,6},{5,7},{6,4},{7,5},{8,10},{9,11},{10,... | collective-permute-start | bytes 1671176 | tf_op jit(solution)/shard_map/cond/branch_1_fun/ppermute | solution.py:243
  11.3 0.0 collective-permute-start
  11.3 12.3 %collective-permute-done.1.refs_2_ = bf16[272,1024]{1,0:T(8,128)(2,1)S(1)} collective-permute-done((bf16[272,1024]{1,0:T(8,128)(2,1)}, bf16[272,1024]{1,0:T(8,128)(2,1)S(1)}, u32[]{:S(2)}, u32[]{:S(2)}) %collective-permute-start.1) | collective-permute-done | bytes 557088 | tf_op jit(solution)/shard_map/cond/branch_1_fun/ppermute | solution.py:243
  23.5 0.0 collective-permute-start.2
  23.5 0.0 collective-permute-done.refs_1_
  23.5 0.7 %collective-permute-start.3 = (bf16[48,256]{1,0:T(8,128)(2,1)}, bf16[48,256]{1,0:T(8,128)(2,1)S(1)}, u32[]{:S(2)}, u32[]{:S(2)}) collective-permute-start(bf16[48,256]{1,0:T(8,128)(2,1)} %get-tuple-element.13), channel_id=1, source_target_pairs={{0,4},{1,5},{2,6},{3,7},{4,0},{5,1},{6,2},{7,3},{8,12},{9,13},{10,... | collective-permute-start | bytes 73736 | tf_op jit(solution)/shard_map/cond/branch_1_fun/ppermute | solution.py:247
  24.2 1.3 %collective-permute-done.2.refs_3_ = bf16[272,1024]{1,0:T(8,128)(2,1)S(1)} collective-permute-done((bf16[272,1024]{1,0:T(8,128)(2,1)S(1)}, bf16[272,1024]{1,0:T(8,128)(2,1)S(1)}, u32[]{:S(2)}, u32[]{:S(2)}) %collective-permute-start.2) | collective-permute-done | bytes 557088 | tf_op jit(solution)/shard_map/cond/branch_1_fun/ppermute | solution.py:242
  25.5 2.1 %branch_1_fun.2 = (bf16[1024,1024]{1,0:T(8,128)(2,1)S(1)}, f32[8,1024]{1,0:T(8,128)S(1)}, f32[1,1024]{1,0:T(1,128)S(1)}) custom-call(bf16[272,1024]{1,0:T(8,128)(2,1)} %get-tuple-element.9.refs_0_, bf16[272,1024]{1,0:T(8,128)(2,1)S(1)} %collective-permute-done.refs_1_, bf16[272,1024]{1,0:T(8,128)(2,1)S(1)} %collective-permute-done.1.refs_2_, ...), custom_call_target="tpu_custom_call" | custom-call | flops 1 | bytes 1 | tf_op jit(solution)/shard_map/cond/branch_1_fun/pallas_call | solution.py:174
  27.6 0.0 collective-permute-done.3.side_ref
  27.6 0.3 branch_1_fun.3
  27.9 0.0 collective-permute-done.6.code_ref
  28.0 0.8 %shard_map.38.refs_4_ = f32[1,1024]{1,0:T(1,128)S(1)} custom-call(bf16[256,1024]{1,0:T(8,128)(2,1)S(1)} %collective-permute-done.6.code_ref, bf16[256,1024]{1,0:T(8,128)(2,1)S(1)} %get-tuple-element.33.scale_ref, f32[256,128]{1,0:T(8,128)S(1)} %get-tuple-element.34.column_ref, bf16[1024,1024]{1,0:T(8,128)(2,1)S(1)} %get-tuple-element.35.values_ref.refs_2_, ...), custom_call_target="tpu_custom_call" | custom-call | flops 1 | bytes 1 | tf_op jit(solution)/shard_map/pallas_call | solution.py:174
  28.8 1.1 %collective-permute-done.5.refs_1_ = bf16[48,256]{1,0:T(8,128)(2,1)S(1)} collective-permute-done((bf16[48,256]{1,0:T(8,128)(2,1)}, bf16[48,256]{1,0:T(8,128)(2,1)S(1)}, u32[]{:S(2)}, u32[]{:S(2)}) %collective-permute-start.5) | collective-permute-done | bytes 24608 | tf_op jit(solution)/shard_map/ppermute | solution.py:235
  29.9 0.0 collective-permute-done.4.refs_0_
  29.9 1.1 %shard_map.39 = (f32[1,256]{1,0:T(1,128)S(1)}, f32[2,256]{1,0:T(2,128)S(1)}, f32[1,256]{1,0:T(1,128)S(1)}, f32[1,256]{1,0:T(1,128)S(1)}) custom-call(bf16[256,1024]{1,0:T(8,128)(2,1)S(1)} %collective-permute-done.4.refs_0_, bf16[48,256]{1,0:T(8,128)(2,1)S(1)} %collective-permute-done.5.refs_1_, bf16[1024,1024]{1,0:T(8,128)(2,1)S(1)} %get-tuple-element.35.values_ref.refs_2_, ...), custom_call_target="tpu_custom_call" | custom-call | flops 1 | bytes 1 | tf_op jit(solution)/shard_map/pallas_call | solution.py:174
  30.9 0.1 collective-permute-start.8
  31.0 1.7 %collective-permute-start.7 = (f32[1,256]{1,0:T(1,128)S(1)}, f32[1,256]{1,0:T(1,128)S(1)}, u32[]{:S(2)}, u32[]{:S(2)}) collective-permute-start(f32[1,256]{1,0:T(1,128)S(1)} %get-tuple-element.40), channel_id=1, source_target_pairs={{12,0},{13,1},{14,2},{15,3},{8,4},{9,5},{10,6},{11,7},{0,8},{1,9},... | collective-permute-start | bytes 3080 | tf_op jit(solution)/shard_map/ppermute | solution.py:300
  32.7 0.0 collective-permute-done.8
  32.7 1.5 %collective-permute-start.9 = (f32[1,256]{1,0:T(1,128)S(1)}, f32[1,256]{1,0:T(1,128)S(1)}, u32[]{:S(2)}, u32[]{:S(2)}) collective-permute-start(f32[1,256]{1,0:T(1,128)S(1)} %slice_maximum_fusion.1), channel_id=1, source_target_pairs={{0,2},{1,3},{2,0},{3,1},{4,6},{5,7},{6,4},{7,5},{8,10},{9,11},{10,... | collective-permute-start | bytes 3080 | tf_op jit(solution)/shard_map/ppermute | solution.py:299
  34.2 2.2 %collective-permute-done.7 = f32[1,256]{1,0:T(1,128)S(1)} collective-permute-done((f32[1,256]{1,0:T(1,128)S(1)}, f32[1,256]{1,0:T(1,128)S(1)}, u32[]{:S(2)}, u32[]{:S(2)}) %collective-permute-start.7) | collective-permute-done | bytes 1056 | tf_op jit(solution)/shard_map/ppermute | solution.py:300
  36.4 0.0 collective-permute-done.9
  36.4 0.6 %fusion = f32[1,256]{1,0:T(1,128)} fusion(f32[1,256]{1,0:T(1,128)S(1)} %get-tuple-element.43, f32[2,256]{1,0:T(2,128)S(1)} %collective-permute-done.8, f32[1,256]{1,0:T(1,128)S(1)} %collective-permute-done.7, f32[1,256]{1,0:T(1,128)S(1)} %collective-permute-done.9), kind=kLoop, calls=%fused_computation.1 | loop fusion | flops 768 | bytes 5120 | tf_op jit(solution)/shard_map/max | solution.py:301
  (2 shorter events, 0.0 us)
Async XLA Ops:
  0.0 27.9 %collective-permute-start.6 = (bf16[256,1024]{1,0:T(8,128)(2,1)}, bf16[256,1024]{1,0:T(8,128)(2,1)S(1)}, u32[]{:S(2)}, u32[]{:S(2)}) collective-permute-start(bf16[256,1024]{1,0:T(8,128)(2,1)} %codes_hbm.1), channel_id=1, source_target_pairs={{0,4},{1,5},{2,6},{3,7},{4,0},{5,1},{6,2},{7,3},{8,12},{9,13},{10,... | collective-permute-start | bytes 1572872 | tf_op jit(solution)/shard_map/ppermute | solution.py:217
  3.0 26.8 %collective-permute-start.4 = (bf16[256,1024]{1,0:T(8,128)(2,1)}, bf16[256,1024]{1,0:T(8,128)(2,1)S(1)}, u32[]{:S(2)}, u32[]{:S(2)}) collective-permute-start(bf16[256,1024]{1,0:T(8,128)(2,1)} %codes_hbm.1), channel_id=1, source_target_pairs={{0,12},{1,13},{2,14},{3,15},{4,8},{5,9},{6,10},{7,11},{8,0},{9,1},... | collective-permute-start | bytes 1572872 | tf_op jit(solution)/shard_map/ppermute | solution.py:217
  5.5 1.1 %copy-start = (bf16[256,1024]{1,0:T(8,128)(2,1)S(1)}, bf16[256,1024]{1,0:T(8,128)(2,1)}, u32[]{:S(2)}) copy-start(bf16[256,1024]{1,0:T(8,128)(2,1)} %codes_hbm.1) | copy-start | bytes 1572868
  6.6 0.8 %copy-start.1 = (s32[256,32]{0,1:T(8,128)S(1)}, s32[256,32]{0,1:T(8,128)}, u32[]{:S(2)}) copy-start(s32[256,32]{0,1:T(8,128)} %param.6) | copy-start | bytes 98308
  7.3 0.7 %copy-start.2 = (s32[256]{0:T(256)S(1)}, s32[256]{0:T(256)}, u32[]{:S(2)}) copy-start(s32[256]{0:T(256)} %param.7) | copy-start | bytes 3076
  9.4 20.5 %collective-permute-start.5 = (bf16[48,256]{1,0:T(8,128)(2,1)}, bf16[48,256]{1,0:T(8,128)(2,1)S(1)}, u32[]{:S(2)}, u32[]{:S(2)}) collective-permute-start(bf16[48,256]{1,0:T(8,128)(2,1)} %get-tuple-element.32), channel_id=1, source_target_pairs={{0,12},{1,13},{2,14},{3,15},{4,8},{5,9},{6,10},{7,11},{8,0},{9,1},... | collective-permute-start | bytes 73736 | tf_op jit(solution)/shard_map/ppermute | solution.py:235
  9.5 14.1 %collective-permute-start.1 = (bf16[272,1024]{1,0:T(8,128)(2,1)}, bf16[272,1024]{1,0:T(8,128)(2,1)S(1)}, u32[]{:S(2)}, u32[]{:S(2)}) collective-permute-start(bf16[272,1024]{1,0:T(8,128)(2,1)} %get-tuple-element.9.refs_0_), channel_id=1, source_target_pairs={{0,2},{1,3},{2,0},{3,1},{4,6},{5,7},{6,4},{7,5},{8,10},{9,11},{10,... | collective-permute-start | bytes 1671176 | tf_op jit(solution)/shard_map/cond/branch_1_fun/ppermute | solution.py:243
  11.3 12.3 %collective-permute-start = (bf16[272,1024]{1,0:T(8,128)(2,1)}, bf16[272,1024]{1,0:T(8,128)(2,1)S(1)}, u32[]{:S(2)}, u32[]{:S(2)}) collective-permute-start(bf16[272,1024]{1,0:T(8,128)(2,1)} %get-tuple-element.9.refs_0_), channel_id=1, source_target_pairs={{0,1},{1,0},{2,3},{3,2},{4,5},{5,4},{6,7},{7,6},{8,9},{9,8},{10,11... | collective-permute-start | bytes 1671176 | tf_op jit(solution)/shard_map/cond/branch_1_fun/ppermute | solution.py:243
  23.5 2.0 %collective-permute-start.2 = (bf16[272,1024]{1,0:T(8,128)(2,1)S(1)}, bf16[272,1024]{1,0:T(8,128)(2,1)S(1)}, u32[]{:S(2)}, u32[]{:S(2)}) collective-permute-start(bf16[272,1024]{1,0:T(8,128)(2,1)S(1)} %collective-permute-done.1.refs_2_), channel_id=1, source_target_pairs={{0,1},{1,0},{2,3},{3,2},{4,5},{5,4},{6,7},{7,6},{8,9},{9,8},{10,11... | collective-permute-start | bytes 1671176 | tf_op jit(solution)/shard_map/cond/branch_1_fun/ppermute | solution.py:242
  23.5 4.1 %collective-permute-start.3 = (bf16[48,256]{1,0:T(8,128)(2,1)}, bf16[48,256]{1,0:T(8,128)(2,1)S(1)}, u32[]{:S(2)}, u32[]{:S(2)}) collective-permute-start(bf16[48,256]{1,0:T(8,128)(2,1)} %get-tuple-element.13), channel_id=1, source_target_pairs={{0,4},{1,5},{2,6},{3,7},{4,0},{5,1},{6,2},{7,3},{8,12},{9,13},{10,... | collective-permute-start | bytes 73736 | tf_op jit(solution)/shard_map/cond/branch_1_fun/ppermute | solution.py:247
  30.9 1.8 %collective-permute-start.8 = (f32[2,256]{1,0:T(2,128)S(1)}, f32[2,256]{1,0:T(2,128)S(1)}, u32[]{:S(2)}, u32[]{:S(2)}) collective-permute-start(f32[2,256]{1,0:T(2,128)S(1)} %get-tuple-element.42), channel_id=1, source_target_pairs={{0,1},{1,0},{2,3},{3,2},{4,5},{5,4},{6,7},{7,6},{8,9},{9,8},{10,11... | collective-permute-start | bytes 6152 | tf_op jit(solution)/shard_map/ppermute | solution.py:297
  31.0 5.4 %collective-permute-start.7 = (f32[1,256]{1,0:T(1,128)S(1)}, f32[1,256]{1,0:T(1,128)S(1)}, u32[]{:S(2)}, u32[]{:S(2)}) collective-permute-start(f32[1,256]{1,0:T(1,128)S(1)} %get-tuple-element.40), channel_id=1, source_target_pairs={{12,0},{13,1},{14,2},{15,3},{8,4},{9,5},{10,6},{11,7},{0,8},{1,9},... | collective-permute-start | bytes 3080 | tf_op jit(solution)/shard_map/ppermute | solution.py:300
  32.7 3.7 %collective-permute-start.9 = (f32[1,256]{1,0:T(1,128)S(1)}, f32[1,256]{1,0:T(1,128)S(1)}, u32[]{:S(2)}, u32[]{:S(2)}) collective-permute-start(f32[1,256]{1,0:T(1,128)S(1)} %slice_maximum_fusion.1), channel_id=1, source_target_pairs={{0,2},{1,3},{2,0},{3,1},{4,6},{5,7},{6,4},{7,5},{8,10},{9,11},{10,... | collective-permute-start | bytes 3080 | tf_op jit(solution)/shard_map/ppermute | solution.py:299
